TPU v7x, 128 devices: a whole 4x4x4 slice. The times are simulated.
128 devices in a mesh: bx: 16 (over x, y), by: 8 (over z, core).
Axes of the slice: x: 4, y: 4, z: 4, core: 2. Of those that a mesh axis runs over, the one named last changes fastest.
Arguments:
- estimate: float32 [512, 16384], P('bx', 'by'), may hold values from 0.5 to 2
- views: float32 [8, 512, 16384], P(None, 'bx', 'by'), may hold values from 0.25 to 4
- psf: float32 [8, 64, 4096], replicated, as said below
- view_list: int32 [16, 8, 8], P('bx', 'by'), may hold values from 0 to 7, as said below
- view_count: int32 [16, 8], P('bx', 'by'), may hold values from 1 to 5, as said below
Outputs:
- refined: float32 [512, 16384], P('bx', 'by')
Inputs may be any that keep to these rules, and one draw needn't show every extreme that they name: Each row of view_list is an ordering of all 8 views. `view_count`: a block is seen either by 5 views or by at most 2; a block seen by 5 views is never followed along x (the last block by the first) by another such block; some block is seen by 5 views and some by one. `psf`: every entry is positive.
All inputs are finite; a program needn't handle non-finite values.
Results may differ from a plain program's by a relative error of at most 0.0001.
Values sent between devices are 32-bit elements; how exact they have to be, the bound alone decides.
No kernel may reach another device: no remote copies, remote signals or barrier semaphores. Data moves between devices by JAX's collectives and lax.ppermute only.
A program may use at most 256 MiB of HBM per device.

v0:
```python
import jax
import jax.numpy as jnp
from jax import lax
from jax.sharding import PartitionSpec as P

V = 8
K = 64
SZ = 64


def padded(shard, sides, width):
    for axis, dim in sides:
        devices, length = (lax.axis_size(axis), shard.shape[dim])
        up = [(i, (i + 1) % devices) for i in range(devices - 1)]
        down = [(j, i) for i, j in up]
        last = lax.slice_in_dim(shard, length - width, length, axis=dim)
        first = lax.slice_in_dim(shard, 0, width, axis=dim)
        before = lax.ppermute(last, axis, up)
        after = lax.ppermute(first, axis, down)
        shard = jnp.concatenate([before, shard, after], axis=dim)
    return shard


def phase_table(length, entries, offset):
    frequency = jnp.arange(length, dtype=jnp.int32)[:, None]
    position = jnp.arange(entries, dtype=jnp.int32)[None, :] + offset
    turns = jnp.mod(frequency * position, length).astype(jnp.float32)
    return turns * (2.0 * jnp.pi / length)


def forward_table(length, entries, offset):
    angles = phase_table(length, entries, offset)
    return (jnp.cos(angles), -jnp.sin(angles))


def inverse_table(length, entries, offset):
    angles = phase_table(length, entries, offset).T
    return (jnp.cos(angles) / length, jnp.sin(angles) / length)


def apply_axis(matrix, operand, dim_index):
    patterns = ("ab,bjk->ajk", "ab,ibk->iak", "ab,ijb->ija")
    return jnp.einsum(patterns[dim_index], matrix, operand, precision=lax.Precision.HIGHEST)


def transform(real_part, imag_part, tables, dim_index):
    cosine, sine_part = tables
    if imag_part is None:
        return (
            apply_axis(cosine, real_part, dim_index),
            apply_axis(sine_part, real_part, dim_index),
        )
    new_real = apply_axis(cosine, real_part, dim_index) - apply_axis(
        sine_part, imag_part, dim_index
    )
    new_imag = apply_axis(cosine, imag_part, dim_index) + apply_axis(
        sine_part, real_part, dim_index
    )
    return (new_real, new_imag)


def spectrum(volume, tables):
    real_part, imag_part = transform(volume, None, tables[0], 2)
    real_part, imag_part = transform(real_part, imag_part, tables[1], 1)
    return transform(real_part, imag_part, tables[2], 0)


def restore(real_part, imag_part, tables):
    real_part, imag_part = transform(real_part, imag_part, tables[0], 0)
    real_part, imag_part = transform(real_part, imag_part, tables[1], 1)
    cosine, sine_part = tables[2]
    return apply_axis(cosine, real_part, 2) - apply_axis(sine_part, imag_part, 2)


def fold_rims(extended, dim_index, inner_len, half_psf):
    full_len = extended.shape[dim_index]
    own_part = lax.slice_in_dim(extended, 2 * half_psf, 2 * half_psf + inner_len, axis=dim_index)
    low_part = lax.slice_in_dim(extended, 0, half_psf, axis=dim_index)
    high_part = lax.slice_in_dim(extended, full_len - half_psf, full_len, axis=dim_index)
    low_pad = [(0, 0), (0, 0), (0, 0)]
    high_pad = [(0, 0), (0, 0), (0, 0)]
    low_pad[dim_index] = (0, inner_len - half_psf)
    high_pad[dim_index] = (inner_len - half_psf, 0)
    return own_part + low_part + high_part


def per_device(estimate, views, psf, view_list, view_count):
    half_psf = K // 2
    rows_x = estimate.shape[0]
    rows_y = estimate.shape[1] // SZ
    field_block = estimate.reshape(rows_x, rows_y, SZ)
    images = views.reshape(V, rows_x, rows_y, SZ)
    kernels = psf.reshape(V, K, K, K)
    ordering = view_list.reshape(V)
    seen_by = view_count.reshape(())
    span_x = rows_x + K
    span_y = rows_y + K
    span_z = SZ + K
    field_tables = (
        forward_table(span_z, SZ, 0),
        forward_table(span_y, span_y, 0),
        forward_table(span_x, span_x, 0),
    )
    kernel_tables = (
        forward_table(span_z, K, -half_psf),
        forward_table(span_y, K, -half_psf),
        forward_table(span_x, K, -half_psf),
    )
    error_tables = (
        forward_table(span_z, SZ, 0),
        forward_table(span_y, rows_y, half_psf),
        forward_table(span_x, rows_x, half_psf),
    )
    inner_tables = (
        inverse_table(span_x, rows_x, half_psf),
        inverse_table(span_y, rows_y, half_psf),
        inverse_table(span_z, SZ, 0),
    )
    outer_tables = (
        inverse_table(span_x, span_x, 0),
        inverse_table(span_y, span_y, 0),
        inverse_table(span_z, SZ, 0),
    )

    def add_view(totals, spec_field, view_id, view_image):
        kernel = lax.dynamic_index_in_dim(kernels, view_id, 0, keepdims=False)
        otf_real, otf_imag = spectrum(kernel, kernel_tables)
        field_real, field_imag = spec_field
        blurred = restore(
            field_real * otf_real - field_imag * otf_imag,
            field_real * otf_imag + field_imag * otf_real,
            inner_tables,
        )
        rel_error = view_image / blurred - 1.0
        err_real, err_imag = spectrum(rel_error, error_tables)
        return (
            totals[0] + err_real * otf_real + err_imag * otf_imag,
            totals[1] + err_imag * otf_real - err_real * otf_imag,
        )

    rim_field = padded(field_block, (("bx", 0), ("by", 1)), half_psf)
    spec_field = spectrum(rim_field, field_tables)
    zero_spec = jnp.zeros((span_x, span_y, span_z), jnp.float32)

    def own_step(slot, totals):
        view_id = ordering[slot]
        view_image = lax.dynamic_index_in_dim(images, view_id, 0, keepdims=False)
        return add_view(totals, spec_field, view_id, view_image)

    totals = lax.fori_loop(0, seen_by, own_step, (zero_spec, zero_spec))
    back_sums = restore(totals[0], totals[1], outer_tables)
    extended = padded(back_sums, (("bx", 0), ("by", 1)), half_psf)
    correction = fold_rims(fold_rims(extended, 0, rows_x, half_psf), 1, rows_y, half_psf)
    refined = field_block * (1.0 + correction / seen_by.astype(jnp.float32))
    return refined.reshape(rows_x, rows_y * SZ)


def solution(mesh):
    return jax.shard_map(
        per_device,
        mesh=mesh,
        in_specs=(P("bx", "by"), P(None, "bx", "by"), P(), P("bx", "by", None), P("bx", "by")),
        out_specs=P("bx", "by"),
        check_vma=False,
    )
```

profile of v0, /device:TPU:66, one launch (start us, length us, event | category | flops | bytes accessed | tf_op | source)
XLA Modules:
  0.0 906.3 jit_solution(3801811645698931693)
XLA Ops:
  9.5 9.3 %collective-permute-done = f32[32,32,64]{2,1,0:T(8,128)S(1)} collective-permute-done((f32[32,32,64]{2,1,0:T(8,128)S(1)}, f32[32,32,64]{2,1,0:T(8,128)S(1)}, u32[]{:S(2)}, u32[]{:S(2)}) %collective-permute-start) | collective-permute-done | bytes 262176 | tf_op jit(solution)/shard_map/ppermute | solution.py:18
  33.5 14.2 %reshape.32 = f32[8,64,64,64]{3,2,1,0:T(8,128)} reshape(f32[8,64,4096]{2,1,0:T(8,128)} %param.9) | data formatting | bytes 16777216 | tf_op jit(solution)/shard_map/reshape | solution.py:93
  59.2 13.3 %fusion.481 = f32[96,96,128]{2,1,0:T(8,128)S(1)} fusion(f32[96,32,64]{1,2,0:T(8,128)} %copy.151, f32[32,32,64]{1,2,0:T(8,128)} %copy-done.7, f32[32,32,64]{1,2,0:T(8,128)} %copy-done.3, f32[32,32,64]{1,2,0:T(8,128)} %copy-done.5, f32[96,32,64]{1,2,0:T(8,128)S(1)} %copy.150), kind=kOutput, calls=%fused_computation.463 | convolution fusion | flops 908443648 | bytes 7077888 | tf_op jit(solution)/shard_map/ab,ijb->ija/dot_general | solution.py:43
  72.5 9.2 %fusion.479 = f32[96,96,128]{2,1,0:T(8,128)S(1)} fusion(f32[96,32,64]{1,2,0:T(8,128)S(1)} %copy-done.2, f32[32,32,64]{1,2,0:T(8,128)S(1)} %copy-done.8, f32[32,32,64]{1,2,0:T(8,128)S(1)} %copy-done.4, f32[32,32,64]{1,2,0:T(8,128)S(1)} %copy-done.6, f32[96,32,64]{1,2,0:T(8,128)S(1)} %copy.150), kind=kOutput, calls=%fused_computation.461 | convolution fusion | flops 908451840 | bytes 7077888 | tf_op jit(solution)/shard_map/ab,ijb->ija/dot_general | solution.py:43
  95.7 6.9 fusion.402
  102.6 7.1 fusion.404
  114.4 10.1 %fusion.413 = f32[96,96,128]{2,0,1:T(8,128)} fusion(f32[96,96,128]{2,0,1:T(8,128)S(1)} %fusion.402, f32[96,96,128]{2,1,0:T(8,128)S(1)} %subtract_bitcast_fusion.3), kind=kOutput, calls=%fused_computation.392 | convolution fusion | flops 1360226304 | bytes 14155776 | tf_op jit(solution)/shard_map/ab,bjk->ajk/dot_general | solution.py:43
  124.5 10.2 %fusion.410 = f32[96,96,128]{2,0,1:T(8,128)} fusion(f32[96,96,128]{2,0,1:T(8,128)S(1)} %fusion.404, f32[96,96,128]{2,1,0:T(8,128)S(1)} %subtract_bitcast_fusion.3), kind=kOutput, calls=%fused_computation.391 | convolution fusion | flops 1360217088 | bytes 14155776 | tf_op jit(solution)/shard_map/ab,bjk->ajk/dot_general | solution.py:43
  140.1 618.0 %while.18 = (s32[]{:T(128)}, f32[96,96,128]{2,0,1:T(8,128)}, f32[96,96,128]{2,0,1:T(8,128)}, s32[]{:T(128)}, s32[8]{0:T(128)S(1)}, /*index=5*/f32[8,32,32,64]{3,...) while((s32[]{:T(128)}, f32[96,96,128]{2,0,1:T(8,128)}, ...), condition=%wide.region_1.2_spmd.clone.clone.clone, body=%wide.region_0.1_spmd.clone.clone.clone.sunk | while | flops 12106100736 | bytes 230167328 | solution.py:150
  156.5 6.6 fusion.795
  169.0 6.5 fusion.797
  175.5 8.7 fusion.798
  184.2 13.7 %fusion.799 = (f32[96,96,128]{2,0,1:T(8,128)S(1)}, f32[96,96,128]{2,0,1:T(8,128)S(1)}, f32[96,128,96]{1,2,0:T(8,128)}) fusion(f32[96,96,128]{2,0,1:T(8,128)} %get-tuple-element.707, f32[96,96,128]{2,0,1:T(8,128)} %get-tuple-element.706, f32[96,128,96]{1,2,0:T(8,128)S(1)} %fusion.797, f32[96,128,96]{1,2,0:T(8,128)} %fusion.798, ...), kind=kOutput, calls=%fused_computation.22.clone.1 | convolution fusion | flops 914288640 | bytes 36176128 | tf_op jit(solution)/shard_map/while/body/ab,bjk->ajk/dot_general | solution.py:43
  233.3 7.1 convolution_subtract_fusion.4
  240.4 7.1 fusion.813
  247.5 13.8 %fusion.814 = (f32[96,96,128]{2,0,1:T(8,128)}, f32[96,96,128]{2,0,1:T(8,128)}) fusion(f32[96,96,128]{2,0,1:T(8,128)} %get-tuple-element.687, f32[96,128,96]{1,2,0:T(8,128)} %convolution_subtract_fusion.4, f32[96,128,96]{1,2,0:T(8,128)S(1)} %bitcast.352, f32[96,128,96]{1,2,0:T(8,128)S(1)} %fusion.797, f32[96,96,128]{2,0,1:T(8,128)} %get-tuple-element.686, ...), kind=kOutput, calls=%fused_computation.16.clone.1 | convolution fusion | flops 463632384 | bytes 39321728 | tf_op jit(solution)/shard_map/while/body/ab,bjk->ajk/dot_general | solution.py:43
  290.2 6.5 fusion.797
  296.8 8.7 fusion.798
  305.4 13.9 %fusion.799 = (f32[96,96,128]{2,0,1:T(8,128)S(1)}, f32[96,96,128]{2,0,1:T(8,128)S(1)}, f32[96,128,96]{1,2,0:T(8,128)}) fusion(f32[96,96,128]{2,0,1:T(8,128)} %get-tuple-element.707, f32[96,96,128]{2,0,1:T(8,128)} %get-tuple-element.706, f32[96,128,96]{1,2,0:T(8,128)S(1)} %fusion.797, f32[96,128,96]{1,2,0:T(8,128)} %fusion.798, ...), kind=kOutput, calls=%fused_computation.22.clone.1 | convolution fusion | flops 914288640 | bytes 36176128 | tf_op jit(solution)/shard_map/while/body/ab,bjk->ajk/dot_general | solution.py:43
  354.5 7.1 convolution_subtract_fusion.4
  361.6 7.3 fusion.813
  368.9 13.8 %fusion.814 = (f32[96,96,128]{2,0,1:T(8,128)}, f32[96,96,128]{2,0,1:T(8,128)}) fusion(f32[96,96,128]{2,0,1:T(8,128)} %get-tuple-element.687, f32[96,128,96]{1,2,0:T(8,128)} %convolution_subtract_fusion.4, f32[96,128,96]{1,2,0:T(8,128)S(1)} %bitcast.352, f32[96,128,96]{1,2,0:T(8,128)S(1)} %fusion.797, f32[96,96,128]{2,0,1:T(8,128)} %get-tuple-element.686, ...), kind=kOutput, calls=%fused_computation.16.clone.1 | convolution fusion | flops 463632384 | bytes 39321728 | tf_op jit(solution)/shard_map/while/body/ab,bjk->ajk/dot_general | solution.py:43
  411.4 6.7 fusion.797
  418.2 8.7 fusion.798
  426.8 13.6 %fusion.799 = (f32[96,96,128]{2,0,1:T(8,128)S(1)}, f32[96,96,128]{2,0,1:T(8,128)S(1)}, f32[96,128,96]{1,2,0:T(8,128)}) fusion(f32[96,96,128]{2,0,1:T(8,128)} %get-tuple-element.707, f32[96,96,128]{2,0,1:T(8,128)} %get-tuple-element.706, f32[96,128,96]{1,2,0:T(8,128)S(1)} %fusion.797, f32[96,128,96]{1,2,0:T(8,128)} %fusion.798, ...), kind=kOutput, calls=%fused_computation.22.clone.1 | convolution fusion | flops 914288640 | bytes 36176128 | tf_op jit(solution)/shard_map/while/body/ab,bjk->ajk/dot_general | solution.py:43
  475.9 7.1 convolution_subtract_fusion.4
  483.0 7.0 fusion.813
  490.0 13.8 %fusion.814 = (f32[96,96,128]{2,0,1:T(8,128)}, f32[96,96,128]{2,0,1:T(8,128)}) fusion(f32[96,96,128]{2,0,1:T(8,128)} %get-tuple-element.687, f32[96,128,96]{1,2,0:T(8,128)} %convolution_subtract_fusion.4, f32[96,128,96]{1,2,0:T(8,128)S(1)} %bitcast.352, f32[96,128,96]{1,2,0:T(8,128)S(1)} %fusion.797, f32[96,96,128]{2,0,1:T(8,128)} %get-tuple-element.686, ...), kind=kOutput, calls=%fused_computation.16.clone.1 | convolution fusion | flops 463632384 | bytes 39321728 | tf_op jit(solution)/shard_map/while/body/ab,bjk->ajk/dot_general | solution.py:43
  520.3 6.6 fusion.795
  532.8 6.5 fusion.797
  539.3 8.7 fusion.798
  548.0 13.7 %fusion.799 = (f32[96,96,128]{2,0,1:T(8,128)S(1)}, f32[96,96,128]{2,0,1:T(8,128)S(1)}, f32[96,128,96]{1,2,0:T(8,128)}) fusion(f32[96,96,128]{2,0,1:T(8,128)} %get-tuple-element.707, f32[96,96,128]{2,0,1:T(8,128)} %get-tuple-element.706, f32[96,128,96]{1,2,0:T(8,128)S(1)} %fusion.797, f32[96,128,96]{1,2,0:T(8,128)} %fusion.798, ...), kind=kOutput, calls=%fused_computation.22.clone.1 | convolution fusion | flops 914288640 | bytes 36176128 | tf_op jit(solution)/shard_map/while/body/ab,bjk->ajk/dot_general | solution.py:43
  597.1 7.1 convolution_subtract_fusion.4
  604.2 7.1 fusion.813
  611.3 13.8 %fusion.814 = (f32[96,96,128]{2,0,1:T(8,128)}, f32[96,96,128]{2,0,1:T(8,128)}) fusion(f32[96,96,128]{2,0,1:T(8,128)} %get-tuple-element.687, f32[96,128,96]{1,2,0:T(8,128)} %convolution_subtract_fusion.4, f32[96,128,96]{1,2,0:T(8,128)S(1)} %bitcast.352, f32[96,128,96]{1,2,0:T(8,128)S(1)} %fusion.797, f32[96,96,128]{2,0,1:T(8,128)} %get-tuple-element.686, ...), kind=kOutput, calls=%fused_computation.16.clone.1 | convolution fusion | flops 463632384 | bytes 39321728 | tf_op jit(solution)/shard_map/while/body/ab,bjk->ajk/dot_general | solution.py:43
  654.0 6.5 fusion.797
  660.5 8.7 fusion.798
  669.2 13.9 %fusion.799 = (f32[96,96,128]{2,0,1:T(8,128)S(1)}, f32[96,96,128]{2,0,1:T(8,128)S(1)}, f32[96,128,96]{1,2,0:T(8,128)}) fusion(f32[96,96,128]{2,0,1:T(8,128)} %get-tuple-element.707, f32[96,96,128]{2,0,1:T(8,128)} %get-tuple-element.706, f32[96,128,96]{1,2,0:T(8,128)S(1)} %fusion.797, f32[96,128,96]{1,2,0:T(8,128)} %fusion.798, ...), kind=kOutput, calls=%fused_computation.22.clone.1 | convolution fusion | flops 914288640 | bytes 36176128 | tf_op jit(solution)/shard_map/while/body/ab,bjk->ajk/dot_general | solution.py:43
  718.3 7.1 convolution_subtract_fusion.4
  725.4 7.3 fusion.813
  732.7 13.8 %fusion.814 = (f32[96,96,128]{2,0,1:T(8,128)}, f32[96,96,128]{2,0,1:T(8,128)}) fusion(f32[96,96,128]{2,0,1:T(8,128)} %get-tuple-element.687, f32[96,128,96]{1,2,0:T(8,128)} %convolution_subtract_fusion.4, f32[96,128,96]{1,2,0:T(8,128)S(1)} %bitcast.352, f32[96,128,96]{1,2,0:T(8,128)S(1)} %fusion.797, f32[96,96,128]{2,0,1:T(8,128)} %get-tuple-element.686, ...), kind=kOutput, calls=%fused_computation.16.clone.1 | convolution fusion | flops 463632384 | bytes 39321728 | tf_op jit(solution)/shard_map/while/body/ab,bjk->ajk/dot_general | solution.py:43
  758.1 6.5 fusion.445
  773.5 7.3 fusion.398
  780.9 7.1 fusion.400
  792.7 7.1 fusion.394
  799.8 7.6 fusion.396
  829.0 15.8 %collective-permute-done.4 = f32[32,96,64]{1,2,0:T(8,128)S(1)} collective-permute-done((f32[32,96,64]{1,2,0:T(8,128)}, f32[32,96,64]{1,2,0:T(8,128)S(1)}, u32[]{:S(2)}, u32[]{:S(2)}) %collective-permute-start.4) | collective-permute-done | bytes 786464 | tf_op jit(solution)/shard_map/ppermute | solution.py:18
  871.0 17.9 %collective-permute-done.6 = f32[160,32,64]{0,2,1:T(8,128)} collective-permute-done((f32[160,32,64]{0,2,1:T(8,128)}, f32[160,32,64]{0,2,1:T(8,128)}, u32[]{:S(2)}, u32[]{:S(2)}) %collective-permute-start.6) | collective-permute-done | bytes 1310752 | tf_op jit(solution)/shard_map/ppermute | solution.py:18
  (224 shorter events, 431.0 us)
Async XLA Ops:
  1.2 18.0 %copy-start.9 = (f32[32,32,64]{2,1,0:T(8,128)}, f32[32,32,64]{2,1,0:T(8,128)S(1)}, u32[]{:S(2)}) copy-start(f32[32,32,64]{2,1,0:T(8,128)S(1)} %reshape.28) | copy-start | bytes 786436
  1.2 17.7 %collective-permute-start = (f32[32,32,64]{2,1,0:T(8,128)S(1)}, f32[32,32,64]{2,1,0:T(8,128)S(1)}, u32[]{:S(2)}, u32[]{:S(2)}) collective-permute-start(f32[32,32,64]{2,1,0:T(8,128)S(1)} %reshape.28), channel_id=1, source_target_pairs={{0,8},{8,16},{16,24},{24,32},{32,40},{40,48},{48,56},{56,64},{64,7... | collective-permute-start | bytes 786440 | tf_op jit(solution)/shard_map/ppermute | solution.py:18
  4.7 15.4 %collective-permute-start.1 = (f32[32,32,64]{2,1,0:T(8,128)S(1)}, f32[32,32,64]{2,1,0:T(8,128)}, u32[]{:S(2)}, u32[]{:S(2)}) collective-permute-start(f32[32,32,64]{2,1,0:T(8,128)S(1)} %reshape.28), channel_id=1, source_target_pairs={{8,0},{16,8},{24,16},{32,24},{40,32},{48,40},{56,48},{64,56},{72,6... | collective-permute-start | bytes 786440 | tf_op jit(solution)/shard_map/ppermute | solution.py:19
  9.5 13.9 %copy-start.3 = (f32[32,32,64]{1,2,0:T(8,128)}, f32[32,32,64]{1,2,0:T(8,128)S(1)}, u32[]{:S(2)}) copy-start(f32[32,32,64]{1,2,0:T(8,128)S(1)} %copy.146) | copy-start | bytes 786436
  19.2 8.4 copy-start.5
  21.4 6.1 copy-start.7
  27.6 23.2 %collective-permute-start.2 = (f32[96,32,64]{0,2,1:T(8,128)}, f32[96,32,64]{0,2,1:T(8,128)}, u32[]{:S(2)}, u32[]{:S(2)}) collective-permute-start(f32[96,32,64]{0,2,1:T(8,128)} %copy.148), channel_id=1, source_target_pairs={{0,1},{1,2},{2,3},{3,4},{4,5},{5,6},{6,7},{8,9},{9,10},{10,11},{11... | collective-permute-start | bytes 2359304 | tf_op jit(solution)/shard_map/ppermute | solution.py:18
  29.5 18.2 %copy-start.10 = (f32[8,32,2048]{2,1,0:T(8,128)S(1)}, f32[8,32,2048]{2,1,0:T(8,128)}, u32[]{:S(2)}) copy-start(f32[8,32,2048]{2,1,0:T(8,128)} %param.8) | copy-start | bytes 6291460
  29.5 25.1 %collective-permute-start.3 = (f32[96,32,64]{0,2,1:T(8,128)}, f32[96,32,64]{0,2,1:T(8,128)}, u32[]{:S(2)}, u32[]{:S(2)}) collective-permute-start(f32[96,32,64]{0,2,1:T(8,128)} %copy.148), channel_id=1, source_target_pairs={{1,0},{2,1},{3,2},{4,3},{5,4},{6,5},{7,6},{9,8},{10,9},{11,10},{12... | collective-permute-start | bytes 2359304 | tf_op jit(solution)/shard_map/ppermute | solution.py:19
  59.1 13.3 %copy-start.2 = (f32[96,32,64]{1,2,0:T(8,128)S(1)}, f32[96,32,64]{1,2,0:T(8,128)}, u32[]{:S(2)}) copy-start(f32[96,32,64]{1,2,0:T(8,128)} %copy.151) | copy-start | bytes 2359300
  59.1 13.3 %copy-start.4 = (f32[32,32,64]{1,2,0:T(8,128)S(1)}, f32[32,32,64]{1,2,0:T(8,128)}, u32[]{:S(2)}) copy-start(f32[32,32,64]{1,2,0:T(8,128)} %copy-done.3) | copy-start | bytes 786436
  59.1 13.3 %copy-start.6 = (f32[32,32,64]{1,2,0:T(8,128)S(1)}, f32[32,32,64]{1,2,0:T(8,128)}, u32[]{:S(2)}) copy-start(f32[32,32,64]{1,2,0:T(8,128)} %copy-done.5) | copy-start | bytes 786436
  59.1 13.4 %copy-start.8 = (f32[32,32,64]{1,2,0:T(8,128)S(1)}, f32[32,32,64]{1,2,0:T(8,128)}, u32[]{:S(2)}) copy-start(f32[32,32,64]{1,2,0:T(8,128)} %copy-done.7) | copy-start | bytes 786436
  134.7 5.4 copy-start.11
  228.3 19.2 %slice-start = ((s8[4718592]{0:T(1024)(128)(4,1)}), s8[4194304]{0:T(1024)(128)(4,1)S(1)}, s32[]{:S(2)}) async-start(s8[4718592]{0:T(1024)(128)(4,1)} %bitcast.351), calls=%async_computation | async-start | bytes 8388608 | tf_op jit(solution)/shard_map/while
  233.3 14.2 %slice-start.1 = ((s8[4718592]{0:T(1024)(128)(4,1)}), s8[524288]{0:T(1024)(128)(4,1)S(1)}, s32[]{:S(2)}) async-start(s8[4718592]{0:T(1024)(128)(4,1)} %bitcast.351), calls=%async_computation.1 | async-start | bytes 1048576 | tf_op jit(solution)/shard_map/while
  349.5 19.3 %slice-start = ((s8[4718592]{0:T(1024)(128)(4,1)}), s8[4194304]{0:T(1024)(128)(4,1)S(1)}, s32[]{:S(2)}) async-start(s8[4718592]{0:T(1024)(128)(4,1)} %bitcast.351), calls=%async_computation | async-start | bytes 8388608 | tf_op jit(solution)/shard_map/while
  354.5 14.4 %slice-start.1 = ((s8[4718592]{0:T(1024)(128)(4,1)}), s8[524288]{0:T(1024)(128)(4,1)S(1)}, s32[]{:S(2)}) async-start(s8[4718592]{0:T(1024)(128)(4,1)} %bitcast.351), calls=%async_computation.1 | async-start | bytes 1048576 | tf_op jit(solution)/shard_map/while
  470.9 19.1 %slice-start = ((s8[4718592]{0:T(1024)(128)(4,1)}), s8[4194304]{0:T(1024)(128)(4,1)S(1)}, s32[]{:S(2)}) async-start(s8[4718592]{0:T(1024)(128)(4,1)} %bitcast.351), calls=%async_computation | async-start | bytes 8388608 | tf_op jit(solution)/shard_map/while
  475.9 14.2 %slice-start.1 = ((s8[4718592]{0:T(1024)(128)(4,1)}), s8[524288]{0:T(1024)(128)(4,1)S(1)}, s32[]{:S(2)}) async-start(s8[4718592]{0:T(1024)(128)(4,1)} %bitcast.351), calls=%async_computation.1 | async-start | bytes 1048576 | tf_op jit(solution)/shard_map/while
  592.1 19.2 %slice-start = ((s8[4718592]{0:T(1024)(128)(4,1)}), s8[4194304]{0:T(1024)(128)(4,1)S(1)}, s32[]{:S(2)}) async-start(s8[4718592]{0:T(1024)(128)(4,1)} %bitcast.351), calls=%async_computation | async-start | bytes 8388608 | tf_op jit(solution)/shard_map/while
  597.1 14.2 %slice-start.1 = ((s8[4718592]{0:T(1024)(128)(4,1)}), s8[524288]{0:T(1024)(128)(4,1)S(1)}, s32[]{:S(2)}) async-start(s8[4718592]{0:T(1024)(128)(4,1)} %bitcast.351), calls=%async_computation.1 | async-start | bytes 1048576 | tf_op jit(solution)/shard_map/while
  713.3 19.3 %slice-start = ((s8[4718592]{0:T(1024)(128)(4,1)}), s8[4194304]{0:T(1024)(128)(4,1)S(1)}, s32[]{:S(2)}) async-start(s8[4718592]{0:T(1024)(128)(4,1)} %bitcast.351), calls=%async_computation | async-start | bytes 8388608 | tf_op jit(solution)/shard_map/while
  718.3 14.4 %slice-start.1 = ((s8[4718592]{0:T(1024)(128)(4,1)}), s8[524288]{0:T(1024)(128)(4,1)S(1)}, s32[]{:S(2)}) async-start(s8[4718592]{0:T(1024)(128)(4,1)} %bitcast.351), calls=%async_computation.1 | async-start | bytes 1048576 | tf_op jit(solution)/shard_map/while
  758.1 6.5 copy-start
  773.5 14.5 %slice-start.2 = ((s8[4718592]{0:T(1024)(128)(4,1)}), s8[4194304]{0:T(1024)(128)(4,1)S(1)}, s32[]{:S(2)}) async-start(s8[4718592]{0:T(1024)(128)(4,1)} %bitcast.353), calls=%async_computation.2 | async-start | bytes 8388608
  780.9 7.2 slice-start.3
  815.8 2.2 copy-start.1
  819.6 25.2 %collective-permute-start.4 = (f32[32,96,64]{1,2,0:T(8,128)}, f32[32,96,64]{1,2,0:T(8,128)S(1)}, u32[]{:S(2)}, u32[]{:S(2)}) collective-permute-start(f32[32,96,64]{1,2,0:T(8,128)} %copy.162), channel_id=1, source_target_pairs={{0,8},{8,16},{16,24},{24,32},{32,40},{40,48},{48,56},{56,64},{64,7... | collective-permute-start | bytes 2359304 | tf_op jit(solution)/shard_map/ppermute | solution.py:18
  823.0 27.9 %collective-permute-start.5 = (f32[32,96,64]{1,2,0:T(8,128)}, f32[32,96,64]{1,2,0:T(8,128)}, u32[]{:S(2)}, u32[]{:S(2)}) collective-permute-start(f32[32,96,64]{1,2,0:T(8,128)} %copy.163), channel_id=1, source_target_pairs={{8,0},{16,8},{24,16},{32,24},{40,32},{48,40},{56,48},{64,56},{72,6... | collective-permute-start | bytes 2359304 | tf_op jit(solution)/shard_map/ppermute | solution.py:19
  861.2 27.7 %collective-permute-start.6 = (f32[160,32,64]{0,2,1:T(8,128)}, f32[160,32,64]{0,2,1:T(8,128)}, u32[]{:S(2)}, u32[]{:S(2)}) collective-permute-start(f32[160,32,64]{0,2,1:T(8,128)} %copy.166), channel_id=1, source_target_pairs={{0,1},{1,2},{2,3},{3,4},{4,5},{5,6},{6,7},{8,9},{9,10},{10,11},{11... | collective-permute-start | bytes 3932168 | tf_op jit(solution)/shard_map/ppermute | solution.py:18
  866.9 27.4 %collective-permute-start.7 = (f32[160,32,64]{0,2,1:T(8,128)}, f32[160,32,64]{0,2,1:T(8,128)}, u32[]{:S(2)}, u32[]{:S(2)}) collective-permute-start(f32[160,32,64]{0,2,1:T(8,128)} %copy.167), channel_id=1, source_target_pairs={{1,0},{2,1},{3,2},{4,3},{5,4},{6,5},{7,6},{9,8},{10,9},{11,10},{12... | collective-permute-start | bytes 3932168 | tf_op jit(solution)/shard_map/ppermute | solution.py:19
where the time goes:
time: 915 us; the launch traced here: 906 us
  matrix products  722 us (79%)
  local copies, waits for them, and re-layouts  65.3 us (7%)
  waiting for transfers between devices  51.1 us (6%)
  starting transfers between devices  27.3 us (3%)
  loops' own time  25.9 us (3%)
  other arithmetic  13.3 us (1%)
    dot_general x170, matrix products, apply_axis(): jnp.einsum(patterns[dim_index], matrix, operand, precision=lax.Precision....  722 us
    ppermute x4, waiting for transfers between devices, padded(): before = lax.ppermute(last, axis, up)  43 us
    another operation x1, loops' own time, per_device(): totals = lax.fori_loop(0, seen_by, own_step, (zero_spec, zero_spec))  25.9 us
  transfers between devices with their start and end apart: 8, of which 6 were waited for; matrix products, arithmetic and copies ran while one was open for 3% of the time, Pallas kernels for 0%

commit v1 on v0

v1 whole, which is shorter than its diff:
```python
import functools

import jax
import jax.numpy as jnp
import ml_dtypes
import numpy as np
from jax import lax
from jax.experimental import pallas as pl
from jax.experimental.pallas import tpu as pltpu
from jax.sharding import PartitionSpec as P

V = 8
K = 64
SZ = 64
HALF = K // 2
BX = 32
BY = 32
CMAX = 5
PX = 128
PY = 96
PZ = 96
LANES = 128
WX = BX + K
VMEM_LIMIT = 60 * 1024 * 1024

F32 = jnp.float32
BF16 = jnp.bfloat16


def two_parts(table):
    high = table.astype(ml_dtypes.bfloat16)
    low = (table - high.astype(np.float64)).astype(ml_dtypes.bfloat16)
    return high, low


def x_angles(entries, offset):
    position = np.arange(entries) + offset
    turns = np.mod((2 * np.arange(PX // 2)[None, :] + 1) * position[:, None], 2 * PX)
    return turns * (np.pi / PX)


def x_forward(entries, offset):
    angles = x_angles(entries, offset)
    high, low = two_parts(np.concatenate([np.cos(angles), -np.sin(angles)], axis=1))
    return np.concatenate([high, high, low], axis=0)


def x_inverse(entries, offset):
    angles = x_angles(entries, offset)
    table = np.concatenate([np.cos(angles), -np.sin(angles)], axis=1) * (2.0 / PX)
    high, low = two_parts(table)
    return np.concatenate([high, high, low], axis=1)


def angles_full(period, entries, offset):
    turns = np.mod(np.arange(period)[:, None] * (np.arange(entries) + offset)[None, :], period)
    return turns * (2.0 * np.pi / period)


def forward_rows(period, entries, offset):
    angles = angles_full(period, entries, offset)
    high, low = two_parts(np.concatenate([np.cos(angles), -np.sin(angles)], axis=0))
    return np.concatenate([high, high, low], axis=1)


def forward_wide(period, entries, offset):
    angles = angles_full(period, entries, offset)
    high, low = two_parts(np.concatenate([np.cos(angles), -np.sin(angles)], axis=1))
    return np.concatenate([high, high, low], axis=1)


def inverse_rows(period, entries, offset):
    angles = angles_full(period, entries, offset).T
    high, low = two_parts(np.concatenate([np.cos(angles), np.sin(angles)], axis=0) / period)
    return np.concatenate([high, high, low], axis=1)


def split(data):
    high = data.astype(BF16)
    low = (data - high.astype(F32)).astype(BF16)
    return high, low


def stacked(data):
    high, low = split(data)
    return jnp.concatenate([high, low, high], axis=0)


def dot(a, b):
    return lax.dot_general(a, b, (((1,), (0,)), ((), ())), preferred_element_type=F32)


def dot_tn(a, b):
    return lax.dot_general(a, b, (((0,), (0,)), ((), ())), preferred_element_type=F32)


def dot_nt(a, b):
    return lax.dot_general(a, b, (((1,), (1,)), ((), ())), preferred_element_type=F32)


def swap_halves(data):
    return pltpu.roll(data, LANES // 2, 1)


def first_half(shape):
    return lax.broadcasted_iota(jnp.int32, shape, 1) < LANES // 2


def times_i(data):
    swapped = swap_halves(data)
    return jnp.where(first_half(data.shape), -swapped, swapped)


def left_rows(table, pair):
    half = table.shape[0] // 2
    both = dot(table, stacked(jnp.concatenate(pair, axis=1)))
    out = []
    for part in range(2):
        piece = both[:, part * LANES:(part + 1) * LANES]
        out.append(piece[:half] + times_i(piece[half:]))
    return out


def left_wide(table, pair):
    data = jnp.concatenate(pair, axis=1)
    turned = jnp.concatenate([times_i(piece) for piece in pair], axis=1)
    both = dot(table, stacked(jnp.concatenate([data, turned], axis=0)))
    return [both[:, :LANES], both[:, LANES:]]


def loop(count, body, unroll=1):
    def step(index, carry):
        body(index)
        return carry

    lax.fori_loop(0, count, step, 0, unroll=unroll)


def xz_forward(source, wx, wz, target, groups, base):
    def body(j):
        across = dot_tn(stacked(source(j)), wx)
        for pair in range(4):
            first = across[pair * 128:pair * 128 + 64]
            second = across[pair * 128 + 64:pair * 128 + 128]
            low, high = left_rows(wz, (first, second))
            row = pl.multiple_of((base + j * 8 + pair * 2) * PZ, PZ)
            target[pl.ds(row, PZ), :] = low
            target[pl.ds(row + PZ, PZ), :] = high

    loop(groups, body)


def otf_kernel(count_ref, ids_ref, psf_ref, wx_ref, wz_ref, wy_ref, out_ref, mid):
    @pl.when(pl.program_id(0) < count_ref[0])
    def _():
        def source(j):
            return psf_ref[0, :, pl.ds(pl.multiple_of(j * 512, 512), 512)]

        xz_forward(source, wx_ref[...], wz_ref[...], mid, K // 8, 0)

        def body(j):
            for pair in range(2):
                kz = j * 4 + pair * 2
                first = mid[pl.ds(kz, K, stride=PZ), :]
                second = mid[pl.ds(kz + 1, K, stride=PZ), :]
                low, high = left_rows(wy_ref[...], (first, second))
                out_ref[0, kz] = low
                out_ref[0, kz + 1] = high

        loop(PZ // 4, body)


def spread(values):
    swapped = swap_halves(values)
    lane = first_half(values.shape)
    return jnp.where(lane, values, swapped), jnp.where(lane, swapped, values)


def main_kernel(
    count_ref, ids_ref, left_ref, own_ref, right_ref, image_ref, otf_ref,
    wxf_ref, wzf_ref, wyf_ref, wyi_ref, wzi_ref, wxi_ref,
    wxe_ref, wye_ref, wyo_ref, wxo_ref,
    left_out, own_out, right_out,
    field, turned, total, big, mid, lines, error,
):
    slot = pl.program_id(0)

    @pl.when(slot == 0)
    def _():
        for part, ref in enumerate((left_ref, own_ref, right_ref)):
            def source(j, ref=ref):
                return ref[:, pl.ds(pl.multiple_of(j * 512, 512), 512)]

            xz_forward(source, wxf_ref[...], wzf_ref[...], big, BY // 8, part * BY)

        def body(j):
            kz = j * 2
            first = big[pl.ds(kz, PY, stride=PZ), :]
            second = big[pl.ds(kz + 1, PY, stride=PZ), :]
            for at, value in enumerate(left_rows(wyf_ref[...], (first, second))):
                field[kz + at] = value
                turned[kz + at] = times_i(value)
                total[kz + at] = jnp.zeros((PY, LANES), F32)

        loop(PZ // 2, body)

    @pl.when(slot < count_ref[0])
    def _():
        def product(j):
            for pair in range(2):
                kz = j * 4 + pair * 2
                values = []
                for at in range(2):
                    real, imag = spread(otf_ref[0, kz + at])
                    values.append(real * field[kz + at] + imag * turned[kz + at])
                out = left_rows(wyi_ref[...], values)
                for at in range(2):
                    row = pl.multiple_of((kz + at) * BY, BY)
                    mid[pl.ds(row, BY), :] = out[at]

        loop(PZ // 4, product)

        def inverse_z(j):
            for pair in range(4):
                y = j * 8 + pair * 2
                first = mid[pl.ds(y, PZ, stride=BY), :]
                second = mid[pl.ds(y + 1, PZ, stride=BY), :]
                out = left_rows(wzi_ref[...], (first, second))
                for at in range(2):
                    high, low = split(out[at])
                    row = pl.multiple_of((y + at) * SZ, SZ)
                    lines[pl.ds(row, SZ), :] = jnp.concatenate([high, low, high], axis=1)

        loop(BY // 8, inverse_z)

        def relative(j):
            columns = pl.ds(pl.multiple_of(j * 512, 512), 512)
            blurred = dot_nt(wxi_ref[...], lines[columns, :])
            error[:, columns] = image_ref[0, :, columns] / blurred - 1.0

        loop(BY * SZ // 512, relative)

        def source(j):
            return error[:, pl.ds(pl.multiple_of(j * 512, 512), 512)]

        xz_forward(source, wxe_ref[...], wzf_ref[...], mid, BY // 8, 0)

        def gather(j):
            for pair in range(2):
                kz = j * 4 + pair * 2
                first = mid[pl.ds(kz, BY, stride=PZ), :]
                second = mid[pl.ds(kz + 1, BY, stride=PZ), :]
                for at, value in enumerate(left_wide(wye_ref[...], (first, second))):
                    real, imag = spread(otf_ref[0, kz + at])
                    total[kz + at] += real * value - imag * times_i(value)

        loop(PZ // 4, gather)

    @pl.when(slot == CMAX - 1)
    def _():
        def inverse_y(j):
            kz = j * 2
            out = left_rows(wyo_ref[...], (total[kz], total[kz + 1]))
            for at in range(2):
                row = pl.multiple_of((kz + at) * PY, PY)
                big[pl.ds(row, PY), :] = out[at]

        loop(PZ // 2, inverse_y)

        for part, ref in enumerate((left_out, own_out, right_out)):
            def inverse_zx(j, part=part, ref=ref):
                rows = []
                for pair in range(4):
                    y = part * BY + j * 8 + pair * 2
                    first = big[pl.ds(y, PZ, stride=PY), :]
                    second = big[pl.ds(y + 1, PZ, stride=PY), :]
                    rows += left_rows(wzi_ref[...], (first, second))
                high, low = split(jnp.concatenate(rows, axis=0))
                across = jnp.concatenate([high, low, high], axis=1)
                ref[:, pl.ds(pl.multiple_of(j * 512, 512), 512)] = dot_nt(wxo_ref[...], across)

            loop(BY // 8, inverse_zx)


def whole(shape):
    return pl.BlockSpec(shape, lambda *_: (0,) * len(shape))


def last_slot(slot, count):
    return jnp.minimum(slot, count[0] - 1)


def otf_call(count, ids, psf):
    tables = (x_forward(K, -HALF), forward_rows(PZ, K, -HALF), forward_rows(PY, K, -HALF))
    return pl.pallas_call(
        otf_kernel,
        out_shape=jax.ShapeDtypeStruct((CMAX, PZ, PY, LANES), F32),
        grid_spec=pltpu.PrefetchScalarGridSpec(
            num_scalar_prefetch=2,
            grid=(CMAX,),
            in_specs=[
                pl.BlockSpec((1, K, K * K), lambda s, c, i: (i[last_slot(s, c)], 0, 0)),
            ] + [whole(t.shape) for t in tables],
            out_specs=pl.BlockSpec(
                (1, PZ, PY, LANES), lambda s, c, i: (last_slot(s, c), 0, 0, 0)
            ),
            scratch_shapes=[pltpu.VMEM((K * PZ, LANES), F32)],
        ),
        compiler_params=pltpu.CompilerParams(vmem_limit_bytes=VMEM_LIMIT),
        cost_estimate=pl.CostEstimate(flops=20 * 10**9, bytes_accessed=30 * 10**6, transcendentals=0),
        name="otf",
    )(count, ids, psf, *[jnp.asarray(t) for t in tables])


def main_call(count, ids, window, views, otf):
    left, own, right = window
    rows_wide = (WX, BY * SZ)
    tables = (
        x_forward(WX, 0),
        forward_rows(PZ, SZ, 0),
        forward_rows(PY, PY, 0),
        inverse_rows(PY, BY, HALF),
        inverse_rows(PZ, SZ, 0),
        x_inverse(BX, HALF),
        x_forward(BX, HALF),
        forward_wide(PY, BY, HALF),
        inverse_rows(PY, PY, 0),
        x_inverse(WX, 0),
    )
    spectrum = pltpu.VMEM((PZ, PY, LANES), F32)
    return pl.pallas_call(
        main_kernel,
        out_shape=[jax.ShapeDtypeStruct(rows_wide, F32)] * 3,
        grid_spec=pltpu.PrefetchScalarGridSpec(
            num_scalar_prefetch=2,
            grid=(CMAX,),
            in_specs=[whole(rows_wide)] * 3 + [
                pl.BlockSpec((1, BX, BY * SZ), lambda s, c, i: (i[last_slot(s, c)], 0, 0)),
                pl.BlockSpec((1, PZ, PY, LANES), lambda s, c, i: (last_slot(s, c), 0, 0, 0)),
            ] + [whole(t.shape) for t in tables],
            out_specs=[whole(rows_wide)] * 3,
            scratch_shapes=[
                spectrum,
                spectrum,
                spectrum,
                pltpu.VMEM((PY * PZ, LANES), F32),
                pltpu.VMEM((BY * PZ, LANES), F32),
                pltpu.VMEM((BY * SZ, 3 * LANES), BF16),
                pltpu.VMEM((BX, BY * SZ), F32),
            ],
        ),
        compiler_params=pltpu.CompilerParams(vmem_limit_bytes=VMEM_LIMIT),
        cost_estimate=pl.CostEstimate(flops=30 * 10**9, bytes_accessed=40 * 10**6, transcendentals=0),
        name="views",
    )(count, ids, left, own, right, views, otf, *[jnp.asarray(t) for t in tables])


def shifts(axis):
    devices = lax.axis_size(axis)
    up = [(i, i + 1) for i in range(devices - 1)]
    down = [(i + 1, i) for i in range(devices - 1)]
    return up, down


def per_device(estimate, views, psf, view_list, view_count):
    ids = view_list.reshape(V)
    count = view_count.reshape(1)
    up_x, down_x = shifts("bx")
    up_y, down_y = shifts("by")
    before = lax.ppermute(estimate, "bx", up_x)
    after = lax.ppermute(estimate, "bx", down_x)
    own = jnp.concatenate([before, estimate, after], axis=0)
    left = lax.ppermute(own, "by", up_y)
    right = lax.ppermute(own, "by", down_y)
    otf = otf_call(count, ids, psf)
    left_sum, own_sum, right_sum = main_call(count, ids, (left, own, right), views, otf)
    sums = own_sum + lax.ppermute(left_sum, "by", down_y) + lax.ppermute(right_sum, "by", up_y)
    correction = (
        sums[BX:2 * BX]
        + lax.ppermute(sums[:BX], "bx", down_x)
        + lax.ppermute(sums[2 * BX:], "bx", up_x)
    )
    return estimate * (1.0 + correction / count.astype(F32))


def solution(mesh):
    return jax.shard_map(
        per_device,
        mesh=mesh,
        in_specs=(P("bx", "by"), P(None, "bx", "by"), P(), P("bx", "by", None), P("bx", "by")),
        out_specs=P("bx", "by"),
        check_vma=False,
    )
```

time: 915 us -> 300 us (0.33)
  matrix products: 722 us -> 0 us
  starting transfers between devices: 27.3 us -> 183 us
  Pallas kernels: 0 us -> 95.9 us
  local copies, waits for them, and re-layouts: 65.3 us -> 2.23 us
  waiting for transfers between devices: 51.1 us -> 14.5 us
  loops' own time: 25.9 us -> 0 us
  other arithmetic: 13.3 us -> 2.02 us
    dot_general x170 -> x0, matrix products: 722 us -> none  [apply_axis(): jnp.einsum(patterns[dim_index], matrix, operand, precision=lax.Precision....]
    ppermute x8, starting transfers between devices: 27.3 us -> 183 us  [the longest x1 113 us: per_device(): lax.ppermute(right_sum, 'by', up_y)]
    pallas_call x0 -> x2, Pallas kernels: none -> 95.9 us  [the longest x1 78.1 us: main_call(): pl.pallas_call(main_kernel, out_shape=[jax.ShapeDtypeStruct(rows_wide, F3...]
    ppermute x8, waiting for transfers between devices: 51.1 us -> 14.5 us  [the longest x1 6.51 us: per_device(): lax.ppermute(sums[2 * BX:], 'bx', up_x)]
    another operation x1 -> x0, loops' own time: 25.9 us -> none  [per_device(): totals = lax.fori_loop(0, seen_by, own_step, (zero_spec, zero_spec))]
    reshape x5 -> x0, local copies, waits for them, and re-layouts: 20.7 us -> none  [the longest x1 14.2 us: per_device(): kernels = psf.reshape(V, K, K, K)]
    ppermute x8 -> x0, local copies, waits for them, and re-layouts: 19.6 us -> none  [the longest x4 11.3 us: padded(): after = lax.ppermute(first, axis, down)]
    slice x5 -> x1, local copies, waits for them, and re-layouts: 10.2 us -> 0.04 us  [per_device(): sums[:BX]]
  transfers between devices with their start and end apart: 8 -> 8, of which waited for: 6 -> 5; matrix products, arithmetic and copies ran while one was open for 3% -> 0% of each run, Pallas kernels for 0% -> 6%
where the time goes in v1:
time: 300 us; the launch traced here: 299 us
  starting transfers between devices  183 us (61%)
  Pallas kernels  95.9 us (32%)
  waiting for transfers between devices  14.5 us (5%)
    ppermute x1, starting transfers between devices, per_device(): lax.ppermute(right_sum, 'by', up_y)  113 us
    pallas_call x1, Pallas kernels, main_call(): pl.pallas_call(main_kernel, out_shape=[jax.ShapeDtypeStruct(rows_wide, F3...  78.1 us
    ppermute x1, starting transfers between devices, per_device(): lax.ppermute(left_sum, 'by', down_y)  39.1 us
    pallas_call x1, Pallas kernels, otf_call(): pl.pallas_call(otf_kernel, out_shape=jax.ShapeDtypeStruct((CMAX, PZ, PY,...  17.8 us
    ppermute x1, starting transfers between devices, per_device(): lax.ppermute(sums[:BX], 'bx', down_x)  15.9 us
    ppermute x1, waiting for transfers between devices, per_device(): lax.ppermute(sums[2 * BX:], 'bx', up_x)  6.51 us
  transfers between devices with their start and end apart: 8, of which 5 were waited for; matrix products, arithmetic and copies ran while one was open for 0% of the time, Pallas kernels for 6%

profile of v1, /device:TPU:66, one launch (start us, length us, event | category | flops | bytes accessed | tf_op | source)
XLA Modules:
  0.0 298.6 jit_solution(11194096816809939375)
XLA Ops:
  0.0 3.5 %collective-permute-start = (f32[32,2048]{1,0:T(8,128)}, f32[32,2048]{1,0:T(8,128)S(1)}, u32[]{:S(2)}, u32[]{:S(2)}) collective-permute-start(f32[32,2048]{1,0:T(8,128)} %param.18), channel_id=1, source_target_pairs={{0,8},{8,16},{16,24},{24,32},{32,40},{40,48},{48,56},{56,64},{64,7... | collective-permute-start | bytes 786440 | tf_op jit(solution)/shard_map/ppermute | solution.py:370
  3.5 4.5 %collective-permute-start.1 = (f32[32,2048]{1,0:T(8,128)}, f32[32,2048]{1,0:T(8,128)S(1)}, u32[]{:S(2)}, u32[]{:S(2)}) collective-permute-start(f32[32,2048]{1,0:T(8,128)} %param.18), channel_id=1, source_target_pairs={{8,0},{16,8},{24,16},{32,24},{40,32},{48,40},{56,48},{64,56},{72,6... | collective-permute-start | bytes 786440 | tf_op jit(solution)/shard_map/ppermute | solution.py:371
  8.6 3.6 %collective-permute-done = f32[32,2048]{1,0:T(8,128)S(1)} collective-permute-done((f32[32,2048]{1,0:T(8,128)}, f32[32,2048]{1,0:T(8,128)S(1)}, u32[]{:S(2)}, u32[]{:S(2)}) %collective-permute-start) | collective-permute-done | bytes 262176 | tf_op jit(solution)/shard_map/ppermute | solution.py:370
  12.3 1.0 constant_dynamic-update-slice_fusion.1
  13.2 0.3 collective-permute-done.1
  13.6 0.0 copy-start.1
  13.6 1.9 collective-permute-start.2
  15.5 3.6 %collective-permute-start.3 = (f32[96,2048]{1,0:T(8,128)S(1)}, f32[96,2048]{1,0:T(8,128)S(1)}, u32[]{:S(2)}, u32[]{:S(2)}) collective-permute-start(f32[96,2048]{1,0:T(8,128)S(1)} %constant_dynamic-update-slice_fusion.own_ref), channel_id=1, source_target_pairs={{1,0},{2,1},{3,2},{4,3},{5,4},{6,5},{7,6},{9,8},{10,9},{11,10},{12... | collective-permute-start | bytes 2359304 | tf_op jit(solution)/shard_map/ppermute | solution.py:374
  19.1 17.8 %otf.1.otf_ref = f32[5,96,96,128]{3,2,1,0:T(8,128)} custom-call(s32[1]{0:T(128)} %bitcast.3.count_ref, s32[8]{0:T(128)} %bitcast.6, f32[8,64,4096]{2,1,0:T(8,128)} %psf_ref.1, bf16[192,128]{1,0:T(8,128)(2,1)} %constant.26.clone.wx_ref, bf16[192,192]{1,0:T(8,128)(2,1)} %constant.27.clone.wz_ref.wy_ref, bf16[192,192]{1,0:T(8,128)(2,1)} %constant.27.clone.wz_ref.wy_ref), custom_call_target="tpu_custom_call" | custom-call | flops 20000000000 | bytes 30000000 | tf_op jit(solution)/shard_map/otf/pallas_call | solution.py:295
  36.9 0.0 copy-done.1
  36.9 0.0 collective-permute-done.2.left_ref
  36.9 0.0 copy-start.2
  36.9 0.0 collective-permute-done.3.right_ref
  36.9 0.0 copy-start.3
  37.0 0.8 copy-done.2
  37.8 0.3 copy-done.3
  38.1 0.0 copy-start
  38.1 78.1 %views.1 = (f32[96,2048]{1,0:T(8,128)}, f32[96,2048]{1,0:T(8,128)}, f32[96,2048]{1,0:T(8,128)}) custom-call(s32[1]{0:T(128)} %bitcast.4.count_ref, s32[8]{0:T(128)} %bitcast.7, f32[96,2048]{1,0:T(8,128)} %copy-done.2, f32[96,2048]{1,0:T(8,128)} %copy-done.1, f32[96,2048]{1,0:T(8,128)} %copy-done.3, f32[8,32,2048]{2,1,0:T(8,128)} %image_ref.1, ...), custom_call_target="tpu_custom_call" | custom-call | flops 30000001024 | bytes 40000000 | tf_op jit(solution)/shard_map/views/pallas_call | solution.py:331
  116.2 39.1 %collective-permute-start.4 = (f32[96,2048]{1,0:T(8,128)}, f32[96,2048]{1,0:T(8,128)S(1)}, u32[]{:S(2)}, u32[]{:S(2)}) collective-permute-start(f32[96,2048]{1,0:T(8,128)} %get-tuple-element.9), channel_id=1, source_target_pairs={{1,0},{2,1},{3,2},{4,3},{5,4},{6,5},{7,6},{9,8},{10,9},{11,10},{12... | collective-permute-start | bytes 2359304 | tf_op jit(solution)/shard_map/ppermute | solution.py:377
  155.4 112.8 %collective-permute-start.5 = (f32[96,2048]{1,0:T(8,128)}, f32[96,2048]{1,0:T(8,128)S(1)}, u32[]{:S(2)}, u32[]{:S(2)}) collective-permute-start(f32[96,2048]{1,0:T(8,128)} %get-tuple-element.10), channel_id=1, source_target_pairs={{0,1},{1,2},{2,3},{3,4},{4,5},{5,6},{6,7},{8,9},{9,10},{10,11},{11... | collective-permute-start | bytes 2359304 | tf_op jit(solution)/shard_map/ppermute | solution.py:377
  268.2 0.0 collective-permute-done.4
  268.2 2.1 collective-permute-done.5
  270.3 1.3 add_add_fusion
  271.6 15.9 %collective-permute-start.6 = (f32[32,2048]{1,0:T(8,128)S(1)}, f32[32,2048]{1,0:T(8,128)S(1)}, u32[]{:S(2)}, u32[]{:S(2)}) collective-permute-start(f32[32,2048]{1,0:T(8,128)S(1)} %get-tuple-element.11), channel_id=1, source_target_pairs={{8,0},{16,8},{24,16},{32,24},{40,32},{48,40},{56,48},{64,56},{72,6... | collective-permute-start | bytes 786440 | tf_op jit(solution)/shard_map/ppermute | solution.py:380
  287.5 1.9 collective-permute-start.7
  289.4 1.9 collective-permute-done.6
  291.4 6.5 %collective-permute-done.7 = f32[32,2048]{1,0:T(8,128)S(1)} collective-permute-done((f32[32,2048]{1,0:T(8,128)S(1)}, f32[32,2048]{1,0:T(8,128)S(1)}, u32[]{:S(2)}, u32[]{:S(2)}) %collective-permute-start.7) | collective-permute-done | bytes 262176 | tf_op jit(solution)/shard_map/ppermute | solution.py:381
  297.9 0.0 copy-done
  297.9 0.8 fusion.3
  (3 shorter events, 0.1 us)
Async XLA Ops:
  0.0 12.2 %collective-permute-start = (f32[32,2048]{1,0:T(8,128)}, f32[32,2048]{1,0:T(8,128)S(1)}, u32[]{:S(2)}, u32[]{:S(2)}) collective-permute-start(f32[32,2048]{1,0:T(8,128)} %param.18), channel_id=1, source_target_pairs={{0,8},{8,16},{16,24},{24,32},{32,40},{40,48},{48,56},{56,64},{64,7... | collective-permute-start | bytes 786440 | tf_op jit(solution)/shard_map/ppermute | solution.py:370
  3.5 10.1 %collective-permute-start.1 = (f32[32,2048]{1,0:T(8,128)}, f32[32,2048]{1,0:T(8,128)S(1)}, u32[]{:S(2)}, u32[]{:S(2)}) collective-permute-start(f32[32,2048]{1,0:T(8,128)} %param.18), channel_id=1, source_target_pairs={{8,0},{16,8},{24,16},{32,24},{40,32},{48,40},{56,48},{64,56},{72,6... | collective-permute-start | bytes 786440 | tf_op jit(solution)/shard_map/ppermute | solution.py:371
  13.6 23.4 %copy-start.1 = (f32[96,2048]{1,0:T(8,128)}, f32[96,2048]{1,0:T(8,128)S(1)}, u32[]{:S(2)}) copy-start(f32[96,2048]{1,0:T(8,128)S(1)} %constant_dynamic-update-slice_fusion.own_ref) | copy-start | bytes 2359300
  13.6 23.3 %collective-permute-start.2 = (f32[96,2048]{1,0:T(8,128)S(1)}, f32[96,2048]{1,0:T(8,128)S(1)}, u32[]{:S(2)}, u32[]{:S(2)}) collective-permute-start(f32[96,2048]{1,0:T(8,128)S(1)} %constant_dynamic-update-slice_fusion.own_ref), channel_id=1, source_target_pairs={{0,1},{1,2},{2,3},{3,4},{4,5},{5,6},{6,7},{8,9},{9,10},{10,11},{11... | collective-permute-start | bytes 2359304 | tf_op jit(solution)/shard_map/ppermute | solution.py:373
  15.5 21.4 %collective-permute-start.3 = (f32[96,2048]{1,0:T(8,128)S(1)}, f32[96,2048]{1,0:T(8,128)S(1)}, u32[]{:S(2)}, u32[]{:S(2)}) collective-permute-start(f32[96,2048]{1,0:T(8,128)S(1)} %constant_dynamic-update-slice_fusion.own_ref), channel_id=1, source_target_pairs={{1,0},{2,1},{3,2},{4,3},{5,4},{6,5},{7,6},{9,8},{10,9},{11,10},{12... | collective-permute-start | bytes 2359304 | tf_op jit(solution)/shard_map/ppermute | solution.py:374
  36.9 0.9 copy-start.2
  36.9 1.2 copy-start.3
  38.1 259.7 %copy-start = (f32[32,2048]{1,0:T(8,128)S(1)}, f32[32,2048]{1,0:T(8,128)}, u32[]{:S(2)}) copy-start(f32[32,2048]{1,0:T(8,128)} %param.18) | copy-start | bytes 786436
  116.2 152.0 %collective-permute-start.4 = (f32[96,2048]{1,0:T(8,128)}, f32[96,2048]{1,0:T(8,128)S(1)}, u32[]{:S(2)}, u32[]{:S(2)}) collective-permute-start(f32[96,2048]{1,0:T(8,128)} %get-tuple-element.9), channel_id=1, source_target_pairs={{1,0},{2,1},{3,2},{4,3},{5,4},{6,5},{7,6},{9,8},{10,9},{11,10},{12... | collective-permute-start | bytes 2359304 | tf_op jit(solution)/shard_map/ppermute | solution.py:377
  155.4 114.9 %collective-permute-start.5 = (f32[96,2048]{1,0:T(8,128)}, f32[96,2048]{1,0:T(8,128)S(1)}, u32[]{:S(2)}, u32[]{:S(2)}) collective-permute-start(f32[96,2048]{1,0:T(8,128)} %get-tuple-element.10), channel_id=1, source_target_pairs={{0,1},{1,2},{2,3},{3,4},{4,5},{5,6},{6,7},{8,9},{9,10},{10,11},{11... | collective-permute-start | bytes 2359304 | tf_op jit(solution)/shard_map/ppermute | solution.py:377
  271.6 19.8 %collective-permute-start.6 = (f32[32,2048]{1,0:T(8,128)S(1)}, f32[32,2048]{1,0:T(8,128)S(1)}, u32[]{:S(2)}, u32[]{:S(2)}) collective-permute-start(f32[32,2048]{1,0:T(8,128)S(1)} %get-tuple-element.11), channel_id=1, source_target_pairs={{8,0},{16,8},{24,16},{32,24},{40,32},{48,40},{56,48},{64,56},{72,6... | collective-permute-start | bytes 786440 | tf_op jit(solution)/shard_map/ppermute | solution.py:380
  287.5 10.4 %collective-permute-start.7 = (f32[32,2048]{1,0:T(8,128)S(1)}, f32[32,2048]{1,0:T(8,128)S(1)}, u32[]{:S(2)}, u32[]{:S(2)}) collective-permute-start(f32[32,2048]{1,0:T(8,128)S(1)} %get-tuple-element.12), channel_id=1, source_target_pairs={{0,8},{8,16},{16,24},{24,32},{32,40},{40,48},{48,56},{56,64},{64,7... | collective-permute-start | bytes 786440 | tf_op jit(solution)/shard_map/ppermute | solution.py:381

commit v2 on v1

v2 whole, which is shorter than its diff:
```python
import functools

import jax
import jax.numpy as jnp
import ml_dtypes
import numpy as np
from jax import lax
from jax.experimental import pallas as pl
from jax.experimental.pallas import tpu as pltpu
from jax.sharding import PartitionSpec as P

V = 8
K = 64
SZ = 64
HALF = K // 2
BX = 32
BY = 32
CMAX = 5
PX = 128
PY = 96
PZ = 96
KZ = PZ // 2
SLOT = 64
LANES = 128
WX = BX + K
VMEM_LIMIT = 60 * 1024 * 1024

F32 = jnp.float32
BF16 = jnp.bfloat16


def three_parts(table, axis):
    high = table.astype(ml_dtypes.bfloat16)
    low = (table - high.astype(np.float64)).astype(ml_dtypes.bfloat16)
    return np.concatenate([high, high, low], axis=axis)


def turn(frequency, position, period):
    turns = np.mod(frequency[:, None] * position[None, :], 2 * period)
    return turns * (np.pi / period)


def blocks(values, copies):
    rows, columns = values.shape
    out = np.zeros((copies, rows, copies, columns))
    for copy in range(copies):
        out[copy, :, copy, :] = values
    return out.reshape(copies * rows, copies * columns)


def z_angles(offset):
    return turn(2 * np.arange(KZ) + 1, np.arange(SZ) + offset, PZ)


def padded(values):
    return np.pad(values, ((0, 0), (0, SLOT - KZ)))


def z_forward(offset):
    angles = z_angles(offset).T
    parts = [blocks(padded(part), 2) for part in (np.cos(angles), -np.sin(angles))]
    return three_parts(np.concatenate(parts, axis=1), 0)


def z_inverse():
    angles = z_angles(0).T
    parts = [blocks(padded(part).T, 2) for part in (np.cos(angles), -np.sin(angles))]
    return three_parts(np.concatenate(parts, axis=0) * (2.0 / PZ), 0)


def x_forward(entries, offset, room, copies=1):
    angles = turn(2 * np.arange(PX), np.arange(entries) + offset, PX).T
    cosine, sine = [np.pad(f(angles), ((0, room - entries), (0, 0))) for f in (np.cos, np.sin)]
    return three_parts(blocks(np.block([[cosine, -sine], [sine, cosine]]), copies), 0)


def x_inverse(entries, offset):
    angles = turn(2 * np.arange(PX), np.arange(entries) + offset, PX).T
    cosine, sine = np.cos(angles) / PX, np.sin(angles) / PX
    return three_parts(np.block([[cosine, -sine], [sine, cosine]]), 1)


def y_forward(entries, offset):
    angles = turn(2 * np.arange(PY), np.arange(entries) + offset, PY)
    cosine, sine = np.cos(angles), np.sin(angles)
    return three_parts(np.block([[cosine, sine], [-sine, cosine]]), 1)


def y_inverse(entries, offset):
    angles = turn(2 * np.arange(PY), np.arange(entries) + offset, PY).T
    cosine, sine = np.cos(angles) / PY, np.sin(angles) / PY
    return three_parts(np.block([[cosine, -sine], [sine, cosine]]), 1)


def split(data):
    high = data.astype(BF16)
    low = (data - high.astype(F32)).astype(BF16)
    return high, low


def three(data, axis):
    high, low = split(data)
    return jnp.concatenate([high, low, high], axis=axis)


def dot(a, b):
    return lax.dot_general(a, b, (((1,), (0,)), ((), ())), preferred_element_type=F32)


def dot_nt(a, b):
    return lax.dot_general(a, b, (((1,), (1,)), ((), ())), preferred_element_type=F32)


def loop(count, body):
    def step(index, carry):
        body(index)
        return carry

    lax.fori_loop(0, count, step, 0)


def aligned(index, size):
    return pl.ds(pl.multiple_of(index * size, size), size)


def drop_padding(rows):
    return jnp.concatenate([rows[:KZ], rows[SLOT:SLOT + KZ]], axis=0)


def z_then_x(pieces, wz, wx, real_ref, imag_ref, first_pair, copies):
    rows = pieces[0].shape[0]
    along = dot(three(jnp.concatenate(pieces, axis=0), 1), wz)
    groups = []
    for at in range(0, len(pieces), copies):
        parts = []
        for pair in range(at, at + copies):
            piece = along[pair * rows:(pair + 1) * rows]
            parts += [piece[:, :LANES], piece[:, LANES:]]
        if rows * 2 * copies > LANES:
            sides = []
            for part in parts:
                if rows < LANES:
                    part = jnp.concatenate([part, jnp.zeros((LANES - rows, LANES), F32)], axis=0)
                sides.append(drop_padding(part.T))
            groups.append(jnp.concatenate(sides, axis=1))
        else:
            groups.append(drop_padding(jnp.concatenate(parts, axis=0).T))
    across = dot(three(jnp.concatenate(groups, axis=0), 1), wx)
    for at in range(len(groups)):
        piece = across[at * 2 * KZ:(at + 1) * 2 * KZ]
        for copy in range(copies):
            where = aligned(first_pair + at * copies + copy, 2 * KZ)
            real_ref[where, :] = piece[:, (2 * copy) * LANES:(2 * copy + 1) * LANES]
            imag_ref[where, :] = piece[:, (2 * copy + 1) * LANES:(2 * copy + 2) * LANES]


def along_y(table, reals, imags):
    data = jnp.concatenate(
        [jnp.concatenate(reals, axis=1), jnp.concatenate(imags, axis=1)], axis=0
    )
    out = dot(table, three(data, 0))
    half = table.shape[0] // 2
    return [
        (out[:half, at * LANES:(at + 1) * LANES], out[half:, at * LANES:(at + 1) * LANES])
        for at in range(2)
    ]


def strided(ref, start, count, stride):
    return ref[pl.ds(start, count, stride=stride), :]


def y_from_rows(table, real_ref, imag_ref, kz, count):
    reals = [strided(real_ref, kz + at, count, KZ) for at in range(2)]
    imags = [strided(imag_ref, kz + at, count, KZ) for at in range(2)]
    return along_y(table, reals, imags)


def x_from_rows(table, real_ref, imag_ref, ys, stride):
    empty = jnp.zeros((SLOT - KZ, 6 * LANES), BF16)
    rows = []
    for y in ys:
        data = jnp.concatenate(
            [strided(real_ref, y, KZ, stride), strided(imag_ref, y, KZ, stride)], axis=1
        )
        rows += [three(data, 1), empty]
    return dot_nt(table, jnp.concatenate(rows, axis=0))


def otf_kernel(count_ref, ids_ref, psf_ref, wz_ref, wx_ref, wy_ref, out_ref, real, imag):
    @pl.when(pl.program_id(0) < count_ref[0])
    def _():
        def zx(j):
            data = psf_ref[0, :, aligned(j, 4 * LANES)]
            pieces = [data[:, p * LANES:(p + 1) * LANES] for p in range(4)]
            z_then_x(pieces, wz_ref[...], wx_ref[...], real, imag, j * 4, 1)

        loop(K // 8, zx)

        def y(j):
            for pair in range(UY):
                kz = (j * UY + pair) * 2
                for at, out in enumerate(y_from_rows(wy_ref[...], real, imag, kz, K)):
                    out_ref[0, kz + at, 0] = out[0]
                    out_ref[0, kz + at, 1] = out[1]

        loop(KZ // (2 * UY), y)


UY = 4
UP = 4
UG = 4
UF = 2
UT = 2


def main_kernel(
    count_ref, ids_ref, left_ref, own_ref, right_ref, image_ref, otf_ref,
    wz_ref, wzi_ref, wxf_ref, wyf_ref, wyi_ref, wxi_ref, wxe_ref, wye_ref, wyo_ref, wxo_ref,
    left_out, own_out, right_out,
    field, total, big_real, big_imag, real, imag, lines, error,
):
    slot = pl.program_id(0)

    @pl.when(slot == 0)
    def _():
        for part, ref in enumerate((left_ref, own_ref, right_ref)):
            def zx(j, part=part, ref=ref):
                data = ref[:, aligned(j, 4 * LANES)]
                pieces = [data[:, p * LANES:(p + 1) * LANES] for p in range(4)]
                z_then_x(
                    pieces, wz_ref[...], wxf_ref[...], big_real, big_imag, part * (BY // 2) + j * 4, 1
                )

            loop(BY // 8, zx)

        def y(j):
            for pair in range(UF):
                kz = (j * UF + pair) * 2
                for at, out in enumerate(y_from_rows(wyf_ref[...], big_real, big_imag, kz, PY)):
                    for part in range(2):
                        field[kz + at, part] = out[part]
                        total[kz + at, part] = jnp.zeros((PY, LANES), F32)

        loop(KZ // (2 * UF), y)

    @pl.when(slot < count_ref[0])
    def _():
        def product(j):
            for pair in range(UP):
                kz = (j * UP + pair) * 2
                reals, imags = [], []
                for at in range(2):
                    fr, fi = field[kz + at, 0], field[kz + at, 1]
                    pr, pi = otf_ref[0, kz + at, 0], otf_ref[0, kz + at, 1]
                    reals.append(fr * pr - fi * pi)
                    imags.append(fr * pi + fi * pr)
                for at, out in enumerate(along_y(wyi_ref[...], reals, imags)):
                    where = aligned(kz + at, BY)
                    real[where, :] = out[0]
                    imag[where, :] = out[1]

        loop(KZ // (2 * UP), product)

        def inverse_x(j):
            for group in range(2):
                y = j * 8 + group * 4
                out = x_from_rows(wxi_ref[...], real, imag, [y + k for k in range(4)], BY)
                for pair in range(2):
                    piece = out[:, pair * LANES:(pair + 1) * LANES]
                    data = jnp.concatenate([piece[:BX], piece[BX:]], axis=1)
                    lines[aligned(j * 4 + group * 2 + pair, BX), :] = three(data, 1)

        loop(BY // 8, inverse_x)

        def relative(j):
            blurred = dot(lines[aligned(j, 8 * BX), :], wzi_ref[...])
            for pair in range(8):
                columns = aligned(j * 8 + pair, LANES)
                error[:, columns] = image_ref[0, :, columns] / blurred[pair * BX:(pair + 1) * BX] - 1.0

        loop(2, relative)

        def zx(j):
            data = error[:, aligned(j, 4 * LANES)]
            pieces = [data[:, p * LANES:(p + 1) * LANES] for p in range(4)]
            z_then_x(pieces, wz_ref[...], wxe_ref[...], real, imag, j * 4, 2)

        loop(BY // 8, zx)

        def gather(j):
            for pair in range(UG):
                kz = (j * UG + pair) * 2
                for at, (er, ei) in enumerate(y_from_rows(wye_ref[...], real, imag, kz, BY)):
                    pr, pi = otf_ref[0, kz + at, 0], otf_ref[0, kz + at, 1]
                    total[kz + at, 0] += er * pr + ei * pi
                    total[kz + at, 1] += ei * pr - er * pi

        loop(KZ // (2 * UG), gather)

    @pl.when(slot == CMAX - 1)
    def _():
        def inverse_y(j):
            for pair in range(UT):
                kz = (j * UT + pair) * 2
                reals = [total[kz + at, 0] for at in range(2)]
                imags = [total[kz + at, 1] for at in range(2)]
                for at, out in enumerate(along_y(wyo_ref[...], reals, imags)):
                    where = aligned(kz + at, PY)
                    big_real[where, :] = out[0]
                    big_imag[where, :] = out[1]

        loop(KZ // (2 * UT), inverse_y)

        for part, ref in enumerate((left_out, own_out, right_out)):
            def inverse_xz(j, part=part, ref=ref):
                rows = []
                for group in range(2):
                    y = part * BY + j * 8 + group * 4
                    out = x_from_rows(wxo_ref[...], big_real, big_imag, [y + k for k in range(4)], PY)
                    for pair in range(2):
                        piece = out[:, pair * LANES:(pair + 1) * LANES]
                        rows.append(jnp.concatenate([piece[:WX], piece[WX:]], axis=1))
                sums = dot(three(jnp.concatenate(rows, axis=0), 1), wzi_ref[...])
                for pair in range(4):
                    ref[:, aligned(j * 4 + pair, LANES)] = sums[pair * WX:(pair + 1) * WX]

            loop(BY // 8, inverse_xz)


def whole(shape):
    return pl.BlockSpec(shape, lambda *_: (0,) * len(shape))


def last_slot(slot, count):
    return jnp.minimum(slot, count[0] - 1)


SPECTRUM = (KZ, 2, PY, LANES)


def otf_call(count, ids, psf):
    tables = (z_forward(-HALF), x_forward(K, -HALF, K), y_forward(K, -HALF))
    return pl.pallas_call(
        otf_kernel,
        out_shape=jax.ShapeDtypeStruct((CMAX,) + SPECTRUM, F32),
        grid_spec=pltpu.PrefetchScalarGridSpec(
            num_scalar_prefetch=2,
            grid=(CMAX,),
            in_specs=[
                pl.BlockSpec((1, K, K * K), lambda s, c, i: (i[last_slot(s, c)], 0, 0)),
            ] + [whole(t.shape) for t in tables],
            out_specs=pl.BlockSpec(
                (1,) + SPECTRUM, lambda s, c, i: (last_slot(s, c), 0, 0, 0, 0)
            ),
            scratch_shapes=[pltpu.VMEM((K * KZ, LANES), F32)] * 2,
        ),
        compiler_params=pltpu.CompilerParams(vmem_limit_bytes=VMEM_LIMIT),
        cost_estimate=pl.CostEstimate(flops=20 * 10**9, bytes_accessed=30 * 10**6, transcendentals=0),
        name="otf",
    )(count, ids, psf, *[jnp.asarray(t) for t in tables])


def main_call(count, ids, window, views, otf):
    left, own, right = window
    rows_wide = (WX, BY * SZ)
    tables = (
        z_forward(0),
        z_inverse(),
        x_forward(WX, 0, LANES),
        y_forward(PY, 0),
        y_inverse(BY, HALF),
        x_inverse(BX, HALF),
        x_forward(BX, HALF, BX, 2),
        y_forward(BY, HALF),
        y_inverse(PY, 0),
        x_inverse(WX, 0),
    )
    return pl.pallas_call(
        main_kernel,
        out_shape=[jax.ShapeDtypeStruct(rows_wide, F32)] * 3,
        grid_spec=pltpu.PrefetchScalarGridSpec(
            num_scalar_prefetch=2,
            grid=(CMAX,),
            in_specs=[whole(rows_wide)] * 3 + [
                pl.BlockSpec((1, BX, BY * SZ), lambda s, c, i: (i[last_slot(s, c)], 0, 0)),
                pl.BlockSpec((1,) + SPECTRUM, lambda s, c, i: (last_slot(s, c), 0, 0, 0, 0)),
            ] + [whole(t.shape) for t in tables],
            out_specs=[whole(rows_wide)] * 3,
            scratch_shapes=[
                pltpu.VMEM(SPECTRUM, F32),
                pltpu.VMEM(SPECTRUM, F32),
                pltpu.VMEM((PY * KZ, LANES), F32),
                pltpu.VMEM((PY * KZ, LANES), F32),
                pltpu.VMEM((BY * KZ, LANES), F32),
                pltpu.VMEM((BY * KZ, LANES), F32),
                pltpu.VMEM((BX * BY // 2, 6 * LANES), BF16),
                pltpu.VMEM((BX, BY * SZ), F32),
            ],
        ),
        compiler_params=pltpu.CompilerParams(vmem_limit_bytes=VMEM_LIMIT),
        cost_estimate=pl.CostEstimate(flops=30 * 10**9, bytes_accessed=40 * 10**6, transcendentals=0),
        name="views",
    )(count, ids, left, own, right, views, otf, *[jnp.asarray(t) for t in tables])


def shifts(axis):
    devices = lax.axis_size(axis)
    up = [(i, i + 1) for i in range(devices - 1)]
    down = [(i + 1, i) for i in range(devices - 1)]
    return up, down


def per_device(estimate, views, psf, view_list, view_count):
    ids = view_list.reshape(V)
    count = view_count.reshape(1)
    up_x, down_x = shifts("bx")
    up_y, down_y = shifts("by")
    before = lax.ppermute(estimate, "bx", up_x)
    after = lax.ppermute(estimate, "bx", down_x)
    own = jnp.concatenate([before, estimate, after], axis=0)
    left = lax.ppermute(own, "by", up_y)
    right = lax.ppermute(own, "by", down_y)
    otf = otf_call(count, ids, psf)
    left_sum, own_sum, right_sum = main_call(count, ids, (left, own, right), views, otf)
    sums = own_sum + lax.ppermute(left_sum, "by", down_y) + lax.ppermute(right_sum, "by", up_y)
    correction = (
        sums[BX:2 * BX]
        + lax.ppermute(sums[:BX], "bx", down_x)
        + lax.ppermute(sums[2 * BX:], "bx", up_x)
    )
    return estimate * (1.0 + correction / count.astype(F32))


def solution(mesh):
    return jax.shard_map(
        per_device,
        mesh=mesh,
        in_specs=(P("bx", "by"), P(None, "bx", "by"), P(), P("bx", "by", None), P("bx", "by")),
        out_specs=P("bx", "by"),
        check_vma=False,
    )
```

time: 300 us -> 180 us (0.60)
  starting transfers between devices: 183 us -> 27.7 us
  waiting for transfers between devices: 14.5 us -> 73.6 us
  Pallas kernels: 95.9 us -> 72.8 us
    ppermute x1, starting transfers between devices: 113 us -> 2.4 us  [per_device(): lax.ppermute(right_sum, 'by', up_y)]
    ppermute x1, waiting for transfers between devices: 2.05 us -> 52.9 us  [per_device(): lax.ppermute(right_sum, 'by', up_y)]
    ppermute x1, starting transfers between devices: 39.1 us -> 1.91 us  [per_device(): lax.ppermute(left_sum, 'by', down_y)]
    pallas_call x1, Pallas kernels: 78.1 us -> 53 us  [main_call(): pl.pallas_call(main_kernel, out_shape=[jax.ShapeDtypeStruct(rows_wide, F3...]
    ppermute x1, starting transfers between devices: 15.9 us -> 7.92 us  [per_device(): lax.ppermute(sums[:BX], 'bx', down_x)]
    ppermute x1, waiting for transfers between devices: 0.05 us -> 7.39 us  [per_device(): lax.ppermute(left_sum, 'by', down_y)]
  transfers between devices with their start and end apart: 8 -> 8, of which waited for: 5 -> 6; matrix products, arithmetic and copies ran while one was open for 0% -> 1% of each run, Pallas kernels for 6% -> 11%
where the time goes in v2:
time: 180 us; the launch traced here: 179 us
  waiting for transfers between devices  73.6 us (41%)
  Pallas kernels  72.8 us (40%)
  starting transfers between devices  27.7 us (15%)
  local copies, waits for them, and re-layouts  2.23 us (1%)
  other arithmetic  2.02 us (1%)
    pallas_call x1, Pallas kernels, main_call(): pl.pallas_call(main_kernel, out_shape=[jax.ShapeDtypeStruct(rows_wide, F3...  53 us
    ppermute x1, waiting for transfers between devices, per_device(): lax.ppermute(right_sum, 'by', up_y)  52.9 us
    pallas_call x1, Pallas kernels, otf_call(): pl.pallas_call(otf_kernel, out_shape=jax.ShapeDtypeStruct((CMAX,) + SPECT...  19.8 us
    ppermute x1, starting transfers between devices, per_device(): lax.ppermute(sums[:BX], 'bx', down_x)  7.92 us
    ppermute x1, waiting for transfers between devices, per_device(): lax.ppermute(left_sum, 'by', down_y)  7.39 us
    ppermute x1, waiting for transfers between devices, per_device(): lax.ppermute(sums[2 * BX:], 'bx', up_x)  6.23 us
    ppermute x1, starting transfers between devices, per_device(): after = lax.ppermute(estimate, 'bx', down_x)  4.47 us
    ppermute x1, waiting for transfers between devices, per_device(): before = lax.ppermute(estimate, 'bx', up_x)  3.64 us
  transfers between devices with their start and end apart: 8, of which 6 were waited for; matrix products, arithmetic and copies ran while one was open for 1% of the time, Pallas kernels for 11%

profile of v2, /device:TPU:66, one launch (start us, length us, event | category | flops | bytes accessed | tf_op | source)
XLA Modules:
  0.0 179.1 jit_solution(6949250965301450465)
XLA Ops:
  0.0 3.5 %collective-permute-start = (f32[32,2048]{1,0:T(8,128)}, f32[32,2048]{1,0:T(8,128)S(1)}, u32[]{:S(2)}, u32[]{:S(2)}) collective-permute-start(f32[32,2048]{1,0:T(8,128)} %param.18), channel_id=1, source_target_pairs={{0,8},{8,16},{16,24},{24,32},{32,40},{40,48},{48,56},{56,64},{64,7... | collective-permute-start | bytes 786440 | tf_op jit(solution)/shard_map/ppermute | solution.py:419
  3.5 4.5 %collective-permute-start.1 = (f32[32,2048]{1,0:T(8,128)}, f32[32,2048]{1,0:T(8,128)S(1)}, u32[]{:S(2)}, u32[]{:S(2)}) collective-permute-start(f32[32,2048]{1,0:T(8,128)} %param.18), channel_id=1, source_target_pairs={{8,0},{16,8},{24,16},{32,24},{40,32},{48,40},{56,48},{64,56},{72,6... | collective-permute-start | bytes 786440 | tf_op jit(solution)/shard_map/ppermute | solution.py:420
  8.6 3.6 %collective-permute-done = f32[32,2048]{1,0:T(8,128)S(1)} collective-permute-done((f32[32,2048]{1,0:T(8,128)}, f32[32,2048]{1,0:T(8,128)S(1)}, u32[]{:S(2)}, u32[]{:S(2)}) %collective-permute-start) | collective-permute-done | bytes 262176 | tf_op jit(solution)/shard_map/ppermute | solution.py:419
  12.3 1.0 constant_dynamic-update-slice_fusion.1
  13.2 0.3 collective-permute-done.1
  13.6 0.0 copy-start.1
  13.6 1.9 %collective-permute-start.2 = (f32[96,2048]{1,0:T(8,128)S(1)}, f32[96,2048]{1,0:T(8,128)S(1)}, u32[]{:S(2)}, u32[]{:S(2)}) collective-permute-start(f32[96,2048]{1,0:T(8,128)S(1)} %constant_dynamic-update-slice_fusion.own_ref), channel_id=1, source_target_pairs={{0,1},{1,2},{2,3},{3,4},{4,5},{5,6},{6,7},{8,9},{9,10},{10,11},{11... | collective-permute-start | bytes 2359304 | tf_op jit(solution)/shard_map/ppermute | solution.py:422
  15.5 3.6 %collective-permute-start.3 = (f32[96,2048]{1,0:T(8,128)S(1)}, f32[96,2048]{1,0:T(8,128)S(1)}, u32[]{:S(2)}, u32[]{:S(2)}) collective-permute-start(f32[96,2048]{1,0:T(8,128)S(1)} %constant_dynamic-update-slice_fusion.own_ref), channel_id=1, source_target_pairs={{1,0},{2,1},{3,2},{4,3},{5,4},{6,5},{7,6},{9,8},{10,9},{11,10},{12... | collective-permute-start | bytes 2359304 | tf_op jit(solution)/shard_map/ppermute | solution.py:423
  19.1 19.8 %otf.1.otf_ref = f32[5,48,2,96,128]{4,3,2,1,0:T(8,128)} custom-call(s32[1]{0:T(128)} %bitcast.3.count_ref, s32[8]{0:T(128)} %bitcast.6, f32[8,64,4096]{2,1,0:T(8,128)} %psf_ref.1, bf16[384,256]{1,0:T(8,128)(2,1)} %constant.28.clone.wz_ref, bf16[384,256]{1,0:T(8,128)(2,1)} %constant.29.clone.wx_ref, bf16[192,384]{1,0:T(8,128)(2,1)} %constant.30.clone.wy_ref), custom_call_target="tpu_custom_call" | custom-call | flops 20000000000 | bytes 30000000 | tf_op jit(solution)/shard_map/otf/pallas_call | solution.py:344
  38.9 0.0 copy-done.1
  38.9 0.0 collective-permute-done.2.left_ref
  38.9 0.0 copy-start.2
  38.9 0.0 collective-permute-done.3.right_ref
  38.9 0.0 copy-start.3
  38.9 0.8 copy-done.2
  39.8 0.3 copy-done.3
  40.1 0.0 copy-start
  40.1 53.0 %views.1 = (f32[96,2048]{1,0:T(8,128)}, f32[96,2048]{1,0:T(8,128)}, f32[96,2048]{1,0:T(8,128)}) custom-call(s32[1]{0:T(128)} %bitcast.4.count_ref, s32[8]{0:T(128)} %bitcast.7, f32[96,2048]{1,0:T(8,128)} %copy-done.2, f32[96,2048]{1,0:T(8,128)} %copy-done.1, f32[96,2048]{1,0:T(8,128)} %copy-done.3, f32[8,32,2048]{2,1,0:T(8,128)} %image_ref.1, ...), custom_call_target="tpu_custom_call" | custom-call | flops 30000001024 | bytes 40000000 | tf_op jit(solution)/shard_map/views/pallas_call | solution.py:379
  93.1 1.9 %collective-permute-start.4 = (f32[96,2048]{1,0:T(8,128)}, f32[96,2048]{1,0:T(8,128)S(1)}, u32[]{:S(2)}, u32[]{:S(2)}) collective-permute-start(f32[96,2048]{1,0:T(8,128)} %get-tuple-element.9), channel_id=1, source_target_pairs={{1,0},{2,1},{3,2},{4,3},{5,4},{6,5},{7,6},{9,8},{10,9},{11,10},{12... | collective-permute-start | bytes 2359304 | tf_op jit(solution)/shard_map/ppermute | solution.py:426
  95.1 2.4 %collective-permute-start.5 = (f32[96,2048]{1,0:T(8,128)}, f32[96,2048]{1,0:T(8,128)S(1)}, u32[]{:S(2)}, u32[]{:S(2)}) collective-permute-start(f32[96,2048]{1,0:T(8,128)} %get-tuple-element.10), channel_id=1, source_target_pairs={{0,1},{1,2},{2,3},{3,4},{4,5},{5,6},{6,7},{8,9},{9,10},{10,11},{11... | collective-permute-start | bytes 2359304 | tf_op jit(solution)/shard_map/ppermute | solution.py:426
  97.5 7.4 %collective-permute-done.4 = f32[96,2048]{1,0:T(8,128)S(1)} collective-permute-done((f32[96,2048]{1,0:T(8,128)}, f32[96,2048]{1,0:T(8,128)S(1)}, u32[]{:S(2)}, u32[]{:S(2)}) %collective-permute-start.4) | collective-permute-done | bytes 786464 | tf_op jit(solution)/shard_map/ppermute | solution.py:426
  104.9 52.9 %collective-permute-done.5 = f32[96,2048]{1,0:T(8,128)S(1)} collective-permute-done((f32[96,2048]{1,0:T(8,128)}, f32[96,2048]{1,0:T(8,128)S(1)}, u32[]{:S(2)}, u32[]{:S(2)}) %collective-permute-start.5) | collective-permute-done | bytes 786464 | tf_op jit(solution)/shard_map/ppermute | solution.py:426
  157.8 1.3 add_add_fusion
  159.1 7.9 %collective-permute-start.6 = (f32[32,2048]{1,0:T(8,128)S(1)}, f32[32,2048]{1,0:T(8,128)S(1)}, u32[]{:S(2)}, u32[]{:S(2)}) collective-permute-start(f32[32,2048]{1,0:T(8,128)S(1)} %get-tuple-element.11), channel_id=1, source_target_pairs={{8,0},{16,8},{24,16},{32,24},{40,32},{48,40},{56,48},{64,56},{72,6... | collective-permute-start | bytes 786440 | tf_op jit(solution)/shard_map/ppermute | solution.py:429
  167.0 1.9 %collective-permute-start.7 = (f32[32,2048]{1,0:T(8,128)S(1)}, f32[32,2048]{1,0:T(8,128)S(1)}, u32[]{:S(2)}, u32[]{:S(2)}) collective-permute-start(f32[32,2048]{1,0:T(8,128)S(1)} %get-tuple-element.12), channel_id=1, source_target_pairs={{0,8},{8,16},{16,24},{24,32},{32,40},{40,48},{48,56},{56,64},{64,7... | collective-permute-start | bytes 786440 | tf_op jit(solution)/shard_map/ppermute | solution.py:430
  169.0 3.1 %collective-permute-done.6 = f32[32,2048]{1,0:T(8,128)S(1)} collective-permute-done((f32[32,2048]{1,0:T(8,128)S(1)}, f32[32,2048]{1,0:T(8,128)S(1)}, u32[]{:S(2)}, u32[]{:S(2)}) %collective-permute-start.6) | collective-permute-done | bytes 262176 | tf_op jit(solution)/shard_map/ppermute | solution.py:429
  172.1 6.2 %collective-permute-done.7 = f32[32,2048]{1,0:T(8,128)S(1)} collective-permute-done((f32[32,2048]{1,0:T(8,128)S(1)}, f32[32,2048]{1,0:T(8,128)S(1)}, u32[]{:S(2)}, u32[]{:S(2)}) %collective-permute-start.7) | collective-permute-done | bytes 262176 | tf_op jit(solution)/shard_map/ppermute | solution.py:430
  178.3 0.0 copy-done
  178.3 0.8 fusion.3
  (3 shorter events, 0.1 us)
Async XLA Ops:
  0.0 12.2 %collective-permute-start = (f32[32,2048]{1,0:T(8,128)}, f32[32,2048]{1,0:T(8,128)S(1)}, u32[]{:S(2)}, u32[]{:S(2)}) collective-permute-start(f32[32,2048]{1,0:T(8,128)} %param.18), channel_id=1, source_target_pairs={{0,8},{8,16},{16,24},{24,32},{32,40},{40,48},{48,56},{56,64},{64,7... | collective-permute-start | bytes 786440 | tf_op jit(solution)/shard_map/ppermute | solution.py:419
  3.5 10.1 %collective-permute-start.1 = (f32[32,2048]{1,0:T(8,128)}, f32[32,2048]{1,0:T(8,128)S(1)}, u32[]{:S(2)}, u32[]{:S(2)}) collective-permute-start(f32[32,2048]{1,0:T(8,128)} %param.18), channel_id=1, source_target_pairs={{8,0},{16,8},{24,16},{32,24},{40,32},{48,40},{56,48},{64,56},{72,6... | collective-permute-start | bytes 786440 | tf_op jit(solution)/shard_map/ppermute | solution.py:420
  13.6 25.3 %copy-start.1 = (f32[96,2048]{1,0:T(8,128)}, f32[96,2048]{1,0:T(8,128)S(1)}, u32[]{:S(2)}) copy-start(f32[96,2048]{1,0:T(8,128)S(1)} %constant_dynamic-update-slice_fusion.own_ref) | copy-start | bytes 2359300
  13.6 25.3 %collective-permute-start.2 = (f32[96,2048]{1,0:T(8,128)S(1)}, f32[96,2048]{1,0:T(8,128)S(1)}, u32[]{:S(2)}, u32[]{:S(2)}) collective-permute-start(f32[96,2048]{1,0:T(8,128)S(1)} %constant_dynamic-update-slice_fusion.own_ref), channel_id=1, source_target_pairs={{0,1},{1,2},{2,3},{3,4},{4,5},{5,6},{6,7},{8,9},{9,10},{10,11},{11... | collective-permute-start | bytes 2359304 | tf_op jit(solution)/shard_map/ppermute | solution.py:422
  15.5 23.4 %collective-permute-start.3 = (f32[96,2048]{1,0:T(8,128)S(1)}, f32[96,2048]{1,0:T(8,128)S(1)}, u32[]{:S(2)}, u32[]{:S(2)}) collective-permute-start(f32[96,2048]{1,0:T(8,128)S(1)} %constant_dynamic-update-slice_fusion.own_ref), channel_id=1, source_target_pairs={{1,0},{2,1},{3,2},{4,3},{5,4},{6,5},{7,6},{9,8},{10,9},{11,10},{12... | collective-permute-start | bytes 2359304 | tf_op jit(solution)/shard_map/ppermute | solution.py:423
  38.9 0.9 copy-start.2
  38.9 1.2 copy-start.3
  40.1 138.2 %copy-start = (f32[32,2048]{1,0:T(8,128)S(1)}, f32[32,2048]{1,0:T(8,128)}, u32[]{:S(2)}) copy-start(f32[32,2048]{1,0:T(8,128)} %param.18) | copy-start | bytes 786436
  93.1 11.7 %collective-permute-start.4 = (f32[96,2048]{1,0:T(8,128)}, f32[96,2048]{1,0:T(8,128)S(1)}, u32[]{:S(2)}, u32[]{:S(2)}) collective-permute-start(f32[96,2048]{1,0:T(8,128)} %get-tuple-element.9), channel_id=1, source_target_pairs={{1,0},{2,1},{3,2},{4,3},{5,4},{6,5},{7,6},{9,8},{10,9},{11,10},{12... | collective-permute-start | bytes 2359304 | tf_op jit(solution)/shard_map/ppermute | solution.py:426
  95.1 62.7 %collective-permute-start.5 = (f32[96,2048]{1,0:T(8,128)}, f32[96,2048]{1,0:T(8,128)S(1)}, u32[]{:S(2)}, u32[]{:S(2)}) collective-permute-start(f32[96,2048]{1,0:T(8,128)} %get-tuple-element.10), channel_id=1, source_target_pairs={{0,1},{1,2},{2,3},{3,4},{4,5},{5,6},{6,7},{8,9},{9,10},{10,11},{11... | collective-permute-start | bytes 2359304 | tf_op jit(solution)/shard_map/ppermute | solution.py:426
  159.1 13.0 %collective-permute-start.6 = (f32[32,2048]{1,0:T(8,128)S(1)}, f32[32,2048]{1,0:T(8,128)S(1)}, u32[]{:S(2)}, u32[]{:S(2)}) collective-permute-start(f32[32,2048]{1,0:T(8,128)S(1)} %get-tuple-element.11), channel_id=1, source_target_pairs={{8,0},{16,8},{24,16},{32,24},{40,32},{48,40},{56,48},{64,56},{72,6... | collective-permute-start | bytes 786440 | tf_op jit(solution)/shard_map/ppermute | solution.py:429
  167.0 11.3 %collective-permute-start.7 = (f32[32,2048]{1,0:T(8,128)S(1)}, f32[32,2048]{1,0:T(8,128)S(1)}, u32[]{:S(2)}, u32[]{:S(2)}) collective-permute-start(f32[32,2048]{1,0:T(8,128)S(1)} %get-tuple-element.12), channel_id=1, source_target_pairs={{0,8},{8,16},{16,24},{24,32},{32,40},{40,48},{48,56},{56,64},{64,7... | collective-permute-start | bytes 786440 | tf_op jit(solution)/shard_map/ppermute | solution.py:430

commit v3 on v2

--- a/solution.py
+++ b/solution.py
@@ -22,6 +22,9 @@
 KZ = PZ // 2
 SLOT = 64
 LANES = 128
+KPITCH = KZ + 4
+YPITCH = BY + 4
+BIGPITCH = PY + 4
 WX = BX + K
 VMEM_LIMIT = 60 * 1024 * 1024
 
@@ -29,10 +32,16 @@
 BF16 = jnp.bfloat16
 
 
-def three_parts(table, axis):
+def three_parts(table, axis=1):
     high = table.astype(ml_dtypes.bfloat16)
     low = (table - high.astype(np.float64)).astype(ml_dtypes.bfloat16)
     return np.concatenate([high, high, low], axis=axis)
+
+
+def two_rows(table):
+    high = table.astype(ml_dtypes.bfloat16)
+    low = (table - high.astype(np.float64)).astype(ml_dtypes.bfloat16)
+    return np.block([[high, high], [low, np.zeros_like(low)]])
 
 
 def turn(frequency, position, period):
@@ -74,10 +83,10 @@
     return three_parts(blocks(np.block([[cosine, -sine], [sine, cosine]]), copies), 0)
 
 
-def x_inverse(entries, offset):
+def x_inverse(entries, offset, parts):
     angles = turn(2 * np.arange(PX), np.arange(entries) + offset, PX).T
     cosine, sine = np.cos(angles) / PX, np.sin(angles) / PX
-    return three_parts(np.block([[cosine, -sine], [sine, cosine]]), 1)
+    return parts(np.block([[cosine, -sine], [sine, cosine]]))
 
 
 def y_forward(entries, offset):
@@ -86,10 +95,10 @@
     return three_parts(np.block([[cosine, sine], [-sine, cosine]]), 1)
 
 
-def y_inverse(entries, offset):
+def y_inverse(entries, offset, parts):
     angles = turn(2 * np.arange(PY), np.arange(entries) + offset, PY).T
     cosine, sine = np.cos(angles) / PY, np.sin(angles) / PY
-    return three_parts(np.block([[cosine, -sine], [sine, cosine]]), 1)
+    return parts(np.block([[cosine, -sine], [sine, cosine]]))
 
 
 def split(data):
@@ -111,12 +120,13 @@
     return lax.dot_general(a, b, (((1,), (1,)), ((), ())), preferred_element_type=F32)
 
 
-def loop(count, body):
+def loop(count, body, unroll=1):
     def step(index, carry):
-        body(index)
+        for at in range(unroll):
+            body(index * unroll + at)
         return carry
 
-    lax.fori_loop(0, count, step, 0)
+    lax.fori_loop(0, count // unroll, step, 0)
 
 
 def aligned(index, size):
@@ -127,7 +137,7 @@
     return jnp.concatenate([rows[:KZ], rows[SLOT:SLOT + KZ]], axis=0)
 
 
-def z_then_x(pieces, wz, wx, real_ref, imag_ref, first_pair, copies):
+def z_stage(pieces, wz, copies):
     rows = pieces[0].shape[0]
     along = dot(three(jnp.concatenate(pieces, axis=0), 1), wz)
     groups = []
@@ -145,21 +155,61 @@
             groups.append(jnp.concatenate(sides, axis=1))
         else:
             groups.append(drop_padding(jnp.concatenate(parts, axis=0).T))
-    across = dot(three(jnp.concatenate(groups, axis=0), 1), wx)
-    for at in range(len(groups)):
+    return three(jnp.concatenate(groups, axis=0), 1)
+
+
+def x_stage(stash, wx, real_ref, imag_ref, first_pair, copies):
+    across = dot(stash, wx)
+    for at in range(stash.shape[0] // (2 * KZ)):
         piece = across[at * 2 * KZ:(at + 1) * 2 * KZ]
         for copy in range(copies):
-            where = aligned(first_pair + at * copies + copy, 2 * KZ)
-            real_ref[where, :] = piece[:, (2 * copy) * LANES:(2 * copy + 1) * LANES]
-            imag_ref[where, :] = piece[:, (2 * copy + 1) * LANES:(2 * copy + 2) * LANES]
+            for y in range(2):
+                where = pl.ds((2 * (first_pair + at * copies + copy) + y) * KPITCH, KZ)
+                part = piece[y * KZ:(y + 1) * KZ]
+                real_ref[where, :] = part[:, (2 * copy) * LANES:(2 * copy + 1) * LANES]
+                imag_ref[where, :] = part[:, (2 * copy + 1) * LANES:(2 * copy + 2) * LANES]
+
+
+def pipelined(count, first, second, stash):
+    first(0, stash[0])
+    if count == 1:
+        second(0, stash[0])
+
+    def body(j):
+        step = 2 * j
+        first(step + 1, stash[1])
+        second(step, stash[0])
+        first(jnp.minimum(step + 2, count - 1), stash[0])
+        second(step + 1, stash[1])
+
+    loop(count // 2, body)
+
+
+def z_then_x(read, count, wz, wx, real_ref, imag_ref, first_pair, copies, stash):
+    pairs = stash[0].shape[0] // (2 * KZ) * copies
+    count = count // pairs
+
+    def first(step, ref):
+        data = read(aligned(step, pairs * LANES))
+        pieces = [data[:, p * LANES:(p + 1) * LANES] for p in range(pairs)]
+        ref[...] = z_stage(pieces, wz[...], copies)
+
+    def second(step, ref):
+        x_stage(ref[...], wx[...], real_ref, imag_ref, first_pair + step * pairs, copies)
+
+    pipelined(count, first, second, stash)
 
 
 def along_y(table, reals, imags):
     data = jnp.concatenate(
         [jnp.concatenate(reals, axis=1), jnp.concatenate(imags, axis=1)], axis=0
     )
-    out = dot(table, three(data, 0))
-    half = table.shape[0] // 2
+    if table.shape[1] == 2 * data.shape[0]:
+        out = dot(table, jnp.concatenate(split(data), axis=0))
+        out = out[:table.shape[0] // 2] + out[table.shape[0] // 2:]
+    else:
+        out = dot(table, three(data, 0))
+    half = out.shape[0] // 2
     return [
         (out[:half, at * LANES:(at + 1) * LANES], out[half:, at * LANES:(at + 1) * LANES])
         for at in range(2)
@@ -171,31 +221,33 @@
 
 
 def y_from_rows(table, real_ref, imag_ref, kz, count):
-    reals = [strided(real_ref, kz + at, count, KZ) for at in range(2)]
-    imags = [strided(imag_ref, kz + at, count, KZ) for at in range(2)]
+    reals = [strided(real_ref, kz + at, count, KPITCH) for at in range(2)]
+    imags = [strided(imag_ref, kz + at, count, KPITCH) for at in range(2)]
     return along_y(table, reals, imags)
 
 
 def x_from_rows(table, real_ref, imag_ref, ys, stride):
-    empty = jnp.zeros((SLOT - KZ, 6 * LANES), BF16)
+    tall = table.shape[1] == 4 * LANES
+    empty = jnp.zeros((SLOT - KZ, table.shape[1]), BF16)
     rows = []
     for y in ys:
         data = jnp.concatenate(
             [strided(real_ref, y, KZ, stride), strided(imag_ref, y, KZ, stride)], axis=1
         )
-        rows += [three(data, 1), empty]
-    return dot_nt(table, jnp.concatenate(rows, axis=0))
-
-
-def otf_kernel(count_ref, ids_ref, psf_ref, wz_ref, wx_ref, wy_ref, out_ref, real, imag):
-    @pl.when(pl.program_id(0) < count_ref[0])
+        rows += [jnp.concatenate(split(data), axis=1) if tall else three(data, 1), empty]
+    out = dot_nt(table, jnp.concatenate(rows, axis=0))
+    return out[:table.shape[0] // 2] + out[table.shape[0] // 2:] if tall else out
+
+
+def otf_kernel(begin, count_ref, ids_ref, psf_ref, wz_ref, wx_ref, wy_ref, *rest):
+    out_ref, real, imag, stash0, stash1 = rest[-5:]
+
+    @pl.when(pl.program_id(0) + begin < count_ref[0])
     def _():
-        def zx(j):
-            data = psf_ref[0, :, aligned(j, 4 * LANES)]
-            pieces = [data[:, p * LANES:(p + 1) * LANES] for p in range(4)]
-            z_then_x(pieces, wz_ref[...], wx_ref[...], real, imag, j * 4, 1)
-
-        loop(K // 8, zx)
+        def read(columns):
+            return psf_ref[0, :, columns]
+
+        z_then_x(read, K // 2, wz_ref, wx_ref, real, imag, 0, 1, (stash0, stash1))
 
         def y(j):
             for pair in range(UY):
@@ -207,11 +259,16 @@
         loop(KZ // (2 * UY), y)
 
 
-UY = 4
-UP = 4
-UG = 4
-UF = 2
-UT = 2
+ZPO = 16
+ZPF = 8
+ZPE = 8
+UX = 2
+UXZ = 1
+UY = 12
+UP = 12
+UG = 12
+UF = 8
+UT = 12
 
 
 def main_kernel(
@@ -219,20 +276,19 @@
     wz_ref, wzi_ref, wxf_ref, wyf_ref, wyi_ref, wxi_ref, wxe_ref, wye_ref, wyo_ref, wxo_ref,
     left_out, own_out, right_out,
     field, total, big_real, big_imag, real, imag, lines, error,
+    wide0, wide1, thin0, thin1,
 ):
     slot = pl.program_id(0)
 
     @pl.when(slot == 0)
     def _():
         for part, ref in enumerate((left_ref, own_ref, right_ref)):
-            def zx(j, part=part, ref=ref):
-                data = ref[:, aligned(j, 4 * LANES)]
-                pieces = [data[:, p * LANES:(p + 1) * LANES] for p in range(4)]
-                z_then_x(
-                    pieces, wz_ref[...], wxf_ref[...], big_real, big_imag, part * (BY // 2) + j * 4, 1
-                )
-
-            loop(BY // 8, zx)
+            def read(columns, ref=ref):
+                return ref[:, columns]
+
+            z_then_x(
+                read, BY // 2, wz_ref, wxf_ref, big_real, big_imag, part * (BY // 2), 1, (wide0, wide1)
+            )
 
         def y(j):
             for pair in range(UF):
@@ -256,7 +312,7 @@
                     reals.append(fr * pr - fi * pi)
                     imags.append(fr * pi + fi * pr)
                 for at, out in enumerate(along_y(wyi_ref[...], reals, imags)):
-                    where = aligned(kz + at, BY)
+                    where = pl.ds((kz + at) * YPITCH, BY)
                     real[where, :] = out[0]
                     imag[where, :] = out[1]
 
@@ -265,13 +321,13 @@
         def inverse_x(j):
             for group in range(2):
                 y = j * 8 + group * 4
-                out = x_from_rows(wxi_ref[...], real, imag, [y + k for k in range(4)], BY)
+                out = x_from_rows(wxi_ref[...], real, imag, [y + k for k in range(4)], YPITCH)
                 for pair in range(2):
                     piece = out[:, pair * LANES:(pair + 1) * LANES]
                     data = jnp.concatenate([piece[:BX], piece[BX:]], axis=1)
                     lines[aligned(j * 4 + group * 2 + pair, BX), :] = three(data, 1)
 
-        loop(BY // 8, inverse_x)
+        loop(BY // 8, inverse_x, UX)
 
         def relative(j):
             blurred = dot(lines[aligned(j, 8 * BX), :], wzi_ref[...])
@@ -281,12 +337,10 @@
 
         loop(2, relative)
 
-        def zx(j):
-            data = error[:, aligned(j, 4 * LANES)]
-            pieces = [data[:, p * LANES:(p + 1) * LANES] for p in range(4)]
-            z_then_x(pieces, wz_ref[...], wxe_ref[...], real, imag, j * 4, 2)
-
-        loop(BY // 8, zx)
+        def read(columns):
+            return error[:, columns]
+
+        z_then_x(read, BY // 2, wz_ref, wxe_ref, real, imag, 0, 2, (thin0, thin1))
 
         def gather(j):
             for pair in range(UG):
@@ -306,7 +360,7 @@
                 reals = [total[kz + at, 0] for at in range(2)]
                 imags = [total[kz + at, 1] for at in range(2)]
                 for at, out in enumerate(along_y(wyo_ref[...], reals, imags)):
-                    where = aligned(kz + at, PY)
+                    where = pl.ds((kz + at) * BIGPITCH, PY)
                     big_real[where, :] = out[0]
                     big_imag[where, :] = out[1]
 
@@ -317,7 +371,7 @@
                 rows = []
                 for group in range(2):
                     y = part * BY + j * 8 + group * 4
-                    out = x_from_rows(wxo_ref[...], big_real, big_imag, [y + k for k in range(4)], PY)
+                    out = x_from_rows(wxo_ref[...], big_real, big_imag, [y + k for k in range(4)], BIGPITCH)
                     for pair in range(2):
                         piece = out[:, pair * LANES:(pair + 1) * LANES]
                         rows.append(jnp.concatenate([piece[:WX], piece[WX:]], axis=1))
@@ -325,7 +379,7 @@
                 for pair in range(4):
                     ref[:, aligned(j * 4 + pair, LANES)] = sums[pair * WX:(pair + 1) * WX]
 
-            loop(BY // 8, inverse_xz)
+            loop(BY // 8, inverse_xz, UXZ)
 
 
 def whole(shape):
@@ -339,26 +393,41 @@
 SPECTRUM = (KZ, 2, PY, LANES)
 
 
-def otf_call(count, ids, psf):
+def otf_call(count, ids, psf, begin, end, held=None):
     tables = (z_forward(-HALF), x_forward(K, -HALF, K), y_forward(K, -HALF))
+
+    def out_slot(s, c):
+        return jnp.clip(s + begin, begin, jnp.maximum(c[0] - 1, begin))
+
+    inputs = [count, ids, psf] + [jnp.asarray(t) for t in tables]
+    specs = [
+        pl.BlockSpec((1, K, K * K), lambda s, c, i: (i[last_slot(s + begin, c)], 0, 0)),
+    ] + [whole(t.shape) for t in tables]
+    aliases = {}
+    if held is not None:
+        aliases = {len(inputs): 0}
+        inputs.append(held)
+        specs.append(pl.BlockSpec(memory_space=pl.ANY))
     return pl.pallas_call(
-        otf_kernel,
+        functools.partial(otf_kernel, begin),
         out_shape=jax.ShapeDtypeStruct((CMAX,) + SPECTRUM, F32),
         grid_spec=pltpu.PrefetchScalarGridSpec(
             num_scalar_prefetch=2,
-            grid=(CMAX,),
-            in_specs=[
-                pl.BlockSpec((1, K, K * K), lambda s, c, i: (i[last_slot(s, c)], 0, 0)),
-            ] + [whole(t.shape) for t in tables],
+            grid=(end - begin,),
+            in_specs=specs,
             out_specs=pl.BlockSpec(
-                (1,) + SPECTRUM, lambda s, c, i: (last_slot(s, c), 0, 0, 0, 0)
+                (1,) + SPECTRUM, lambda s, c, i: (out_slot(s, c), 0, 0, 0, 0)
             ),
-            scratch_shapes=[pltpu.VMEM((K * KZ, LANES), F32)] * 2,
+            scratch_shapes=[pltpu.VMEM((K * KPITCH, LANES), F32)] * 2
+            + [pltpu.VMEM((ZPO * 2 * KZ, 3 * LANES), BF16)] * 2,
         ),
+        input_output_aliases=aliases,
         compiler_params=pltpu.CompilerParams(vmem_limit_bytes=VMEM_LIMIT),
-        cost_estimate=pl.CostEstimate(flops=20 * 10**9, bytes_accessed=30 * 10**6, transcendentals=0),
+        cost_estimate=pl.CostEstimate(
+            flops=4 * 10**9 * (end - begin), bytes_accessed=6 * 10**6 * (end - begin), transcendentals=0
+        ),
         name="otf",
-    )(count, ids, psf, *[jnp.asarray(t) for t in tables])
+    )(*inputs)
 
 
 def main_call(count, ids, window, views, otf):
@@ -369,12 +438,12 @@
         z_inverse(),
         x_forward(WX, 0, LANES),
         y_forward(PY, 0),
-        y_inverse(BY, HALF),
-        x_inverse(BX, HALF),
+        y_inverse(BY, HALF, two_rows),
+        x_inverse(BX, HALF, two_rows),
         x_forward(BX, HALF, BX, 2),
         y_forward(BY, HALF),
-        y_inverse(PY, 0),
-        x_inverse(WX, 0),
+        y_inverse(PY, 0, three_parts),
+        x_inverse(WX, 0, three_parts),
     )
     return pl.pallas_call(
         main_kernel,
@@ -390,12 +459,16 @@
             scratch_shapes=[
                 pltpu.VMEM(SPECTRUM, F32),
                 pltpu.VMEM(SPECTRUM, F32),
-                pltpu.VMEM((PY * KZ, LANES), F32),
-                pltpu.VMEM((PY * KZ, LANES), F32),
-                pltpu.VMEM((BY * KZ, LANES), F32),
-                pltpu.VMEM((BY * KZ, LANES), F32),
+                pltpu.VMEM((PY * KPITCH, LANES), F32),
+                pltpu.VMEM((PY * KPITCH, LANES), F32),
+                pltpu.VMEM((KZ * YPITCH, LANES), F32),
+                pltpu.VMEM((KZ * YPITCH, LANES), F32),
                 pltpu.VMEM((BX * BY // 2, 6 * LANES), BF16),
                 pltpu.VMEM((BX, BY * SZ), F32),
+                pltpu.VMEM((ZPF * 2 * KZ, 6 * LANES), BF16),
+                pltpu.VMEM((ZPF * 2 * KZ, 6 * LANES), BF16),
+                pltpu.VMEM((ZPE * KZ, 3 * LANES), BF16),
+                pltpu.VMEM((ZPE * KZ, 3 * LANES), BF16),
             ],
         ),
         compiler_params=pltpu.CompilerParams(vmem_limit_bytes=VMEM_LIMIT),
@@ -421,7 +494,8 @@
     own = jnp.concatenate([before, estimate, after], axis=0)
     left = lax.ppermute(own, "by", up_y)
     right = lax.ppermute(own, "by", down_y)
-    otf = otf_call(count, ids, psf)
+    otf = otf_call(count, ids, psf, 0, 2)
+    otf = otf_call(count, ids, psf, 2, CMAX, otf)
     left_sum, own_sum, right_sum = main_call(count, ids, (left, own, right), views, otf)
     sums = own_sum + lax.ppermute(left_sum, "by", down_y) + lax.ppermute(right_sum, "by", up_y)
     correction = (

time: 180 us -> 125 us (0.69)
  waiting for transfers between devices: 73.6 us -> 44.7 us
  Pallas kernels: 72.8 us -> 50.1 us
  starting transfers between devices: 27.7 us -> 25.8 us
    ppermute x1, waiting for transfers between devices: 52.9 us -> 24.9 us  [per_device(): lax.ppermute(right_sum, 'by', up_y)]
    pallas_call x1, Pallas kernels: 53 us -> 34.7 us  [main_call(): pl.pallas_call(main_kernel, out_shape=[jax.ShapeDtypeStruct(rows_wide, F3...]
    pallas_call x1 -> x2, Pallas kernels: 19.8 us -> 15.4 us  [otf_call(): pl.pallas_call(functools.partial(otf_kernel, begin), out_shape=jax.ShapeD...]
    ppermute x1, waiting for transfers between devices: 3.64 us -> 0.01 us  [per_device(): before = lax.ppermute(estimate, 'bx', up_x)]
    ppermute x1, starting transfers between devices: 7.92 us -> 4.32 us  [per_device(): lax.ppermute(sums[:BX], 'bx', down_x)]
    ppermute x1, waiting for transfers between devices: 0.01 us -> 3.29 us  [per_device(): left = lax.ppermute(own, 'by', up_y)]
    ppermute x1, waiting for transfers between devices: 6.23 us -> 4.04 us  [per_device(): lax.ppermute(sums[2 * BX:], 'bx', up_x)]
  transfers between devices with their start and end apart: 8 -> 8, of which waited for: 6 -> 6; matrix products, arithmetic and copies ran while one was open for 1% -> 0% of each run, Pallas kernels for 11% -> 12%
where the time goes in v3:
time: 125 us; the launch traced here: 124 us
  Pallas kernels  50.1 us (40%)
  waiting for transfers between devices  44.7 us (36%)
  starting transfers between devices  25.8 us (21%)
  other arithmetic  2.02 us (2%)
    pallas_call x1, Pallas kernels, main_call(): pl.pallas_call(main_kernel, out_shape=[jax.ShapeDtypeStruct(rows_wide, F3...  34.7 us
    ppermute x1, waiting for transfers between devices, per_device(): lax.ppermute(right_sum, 'by', up_y)  24.9 us
    pallas_call x2, Pallas kernels, otf_call(): pl.pallas_call(functools.partial(otf_kernel, begin), out_shape=jax.ShapeD...  15.4 us
    ppermute x1, waiting for transfers between devices, per_device(): lax.ppermute(left_sum, 'by', down_y)  6 us
    ppermute x1, waiting for transfers between devices, per_device(): lax.ppermute(sums[:BX], 'bx', down_x)  4.74 us
    ppermute x1, starting transfers between devices, per_device(): after = lax.ppermute(estimate, 'bx', down_x)  4.47 us
    ppermute x1, starting transfers between devices, per_device(): lax.ppermute(sums[:BX], 'bx', down_x)  4.32 us
    ppermute x1, waiting for transfers between devices, per_device(): lax.ppermute(sums[2 * BX:], 'bx', up_x)  4.04 us
  transfers between devices with their start and end apart: 8, of which 6 were waited for; matrix products, arithmetic and copies ran while one was open for 0% of the time, Pallas kernels for 12%

profile of v3, /device:TPU:66, one launch (start us, length us, event | category | flops | bytes accessed | tf_op | source)
XLA Modules:
  0.0 124.4 jit_solution(17539642649149750322)
XLA Ops:
  0.0 0.0 copy-start
  0.0 3.6 %collective-permute-start = (f32[32,2048]{1,0:T(8,128)}, f32[32,2048]{1,0:T(8,128)S(1)}, u32[]{:S(2)}, u32[]{:S(2)}) collective-permute-start(f32[32,2048]{1,0:T(8,128)} %param.21), channel_id=1, source_target_pairs={{0,8},{8,16},{16,24},{24,32},{32,40},{40,48},{48,56},{56,64},{64,7... | collective-permute-start | bytes 786440 | tf_op jit(solution)/shard_map/ppermute | solution.py:492
  3.6 4.5 %collective-permute-start.1 = (f32[32,2048]{1,0:T(8,128)}, f32[32,2048]{1,0:T(8,128)S(1)}, u32[]{:S(2)}, u32[]{:S(2)}) collective-permute-start(f32[32,2048]{1,0:T(8,128)} %param.21), channel_id=1, source_target_pairs={{8,0},{16,8},{24,16},{32,24},{40,32},{48,40},{56,48},{64,56},{72,6... | collective-permute-start | bytes 786440 | tf_op jit(solution)/shard_map/ppermute | solution.py:493
  8.7 11.1 %otf.2.rest_0_ = f32[5,48,2,96,128]{4,3,2,1,0:T(8,128)} custom-call(s32[1]{0:T(128)} %bitcast.3.count_ref, s32[8]{0:T(128)} %bitcast.7, f32[8,64,4096]{2,1,0:T(8,128)} %psf_ref.3, bf16[384,256]{1,0:T(8,128)(2,1)} %constant.28.clone.wz_ref, bf16[384,256]{1,0:T(8,128)(2,1)} %constant.29.clone.wx_ref, bf16[192,384]{1,0:T(8,128)(2,1)} %constant.30.clone.wy_ref), custom_call_target="tpu_custom_call" | custom-call | flops 8000000000 | bytes 12000000 | tf_op jit(solution)/shard_map/otf/pallas_call | solution.py:411
  19.9 0.0 collective-permute-done
  19.9 0.0 copy-done
  19.9 0.0 collective-permute-done.1
  20.0 0.0 copy-start.1
  20.0 1.9 %collective-permute-start.2 = (f32[96,2048]{1,0:T(8,128)S(1)}, f32[96,2048]{1,0:T(8,128)S(1)}, u32[]{:S(2)}, u32[]{:S(2)}) collective-permute-start(f32[96,2048]{1,0:T(8,128)S(1)} %constant_dynamic-update-slice_fusion.own_ref), channel_id=1, source_target_pairs={{0,1},{1,2},{2,3},{3,4},{4,5},{5,6},{6,7},{8,9},{9,10},{10,11},{11... | collective-permute-start | bytes 2359304 | tf_op jit(solution)/shard_map/ppermute | solution.py:495
  21.9 3.8 %collective-permute-start.3 = (f32[96,2048]{1,0:T(8,128)S(1)}, f32[96,2048]{1,0:T(8,128)S(1)}, u32[]{:S(2)}, u32[]{:S(2)}) collective-permute-start(f32[96,2048]{1,0:T(8,128)S(1)} %constant_dynamic-update-slice_fusion.own_ref), channel_id=1, source_target_pairs={{1,0},{2,1},{3,2},{4,3},{5,4},{6,5},{7,6},{9,8},{10,9},{11,10},{12... | collective-permute-start | bytes 2359304 | tf_op jit(solution)/shard_map/ppermute | solution.py:496
  25.7 4.3 %otf.3.otf_ref = f32[5,48,2,96,128]{4,3,2,1,0:T(8,128)} custom-call(s32[1]{0:T(128)} %bitcast.4.count_ref, s32[8]{0:T(128)} %bitcast.8, f32[8,64,4096]{2,1,0:T(8,128)} %psf_ref.3, bf16[384,256]{1,0:T(8,128)(2,1)} %constant.28.clone.wz_ref, bf16[384,256]{1,0:T(8,128)(2,1)} %constant.29.clone.wx_ref, ...), custom_call_target="tpu_custom_call", output_to_operand_aliasing={{}: (6, {})} | custom-call | flops 12000000000 | bytes 18000000 | tf_op jit(solution)/shard_map/otf/pallas_call | solution.py:411
  30.0 0.0 copy-done.1
  30.0 3.3 %collective-permute-done.2.left_ref = f32[96,2048]{1,0:T(8,128)S(1)} collective-permute-done((f32[96,2048]{1,0:T(8,128)S(1)}, f32[96,2048]{1,0:T(8,128)S(1)}, u32[]{:S(2)}, u32[]{:S(2)}) %collective-permute-start.2) | collective-permute-done | bytes 786464 | tf_op jit(solution)/shard_map/ppermute | solution.py:495
  33.3 0.0 copy-start.2
  33.3 1.8 %collective-permute-done.3.right_ref = f32[96,2048]{1,0:T(8,128)S(1)} collective-permute-done((f32[96,2048]{1,0:T(8,128)S(1)}, f32[96,2048]{1,0:T(8,128)S(1)}, u32[]{:S(2)}, u32[]{:S(2)}) %collective-permute-start.3) | collective-permute-done | bytes 786464 | tf_op jit(solution)/shard_map/ppermute | solution.py:496
  35.0 0.0 copy-start.3
  35.0 0.0 copy-done.2
  35.0 1.0 copy-done.3
  36.0 34.7 %views.1 = (f32[96,2048]{1,0:T(8,128)}, f32[96,2048]{1,0:T(8,128)}, f32[96,2048]{1,0:T(8,128)}) custom-call(s32[1]{0:T(128)} %bitcast.5.count_ref, s32[8]{0:T(128)} %bitcast.9, f32[96,2048]{1,0:T(8,128)} %copy-done.2, f32[96,2048]{1,0:T(8,128)} %copy-done.1, f32[96,2048]{1,0:T(8,128)} %copy-done.3, f32[8,32,2048]{2,1,0:T(8,128)} %image_ref.1, ...), custom_call_target="tpu_custom_call" | custom-call | flops 30000001024 | bytes 40000000 | tf_op jit(solution)/shard_map/views/pallas_call | solution.py:448
  70.7 1.9 %collective-permute-start.4 = (f32[96,2048]{1,0:T(8,128)}, f32[96,2048]{1,0:T(8,128)S(1)}, u32[]{:S(2)}, u32[]{:S(2)}) collective-permute-start(f32[96,2048]{1,0:T(8,128)} %get-tuple-element.9), channel_id=1, source_target_pairs={{1,0},{2,1},{3,2},{4,3},{5,4},{6,5},{7,6},{9,8},{10,9},{11,10},{12... | collective-permute-start | bytes 2359304 | tf_op jit(solution)/shard_map/ppermute | solution.py:500
  72.6 3.8 %collective-permute-start.5 = (f32[96,2048]{1,0:T(8,128)}, f32[96,2048]{1,0:T(8,128)S(1)}, u32[]{:S(2)}, u32[]{:S(2)}) collective-permute-start(f32[96,2048]{1,0:T(8,128)} %get-tuple-element.10), channel_id=1, source_target_pairs={{0,1},{1,2},{2,3},{3,4},{4,5},{5,6},{6,7},{8,9},{9,10},{10,11},{11... | collective-permute-start | bytes 2359304 | tf_op jit(solution)/shard_map/ppermute | solution.py:500
  76.4 6.0 %collective-permute-done.4 = f32[96,2048]{1,0:T(8,128)S(1)} collective-permute-done((f32[96,2048]{1,0:T(8,128)}, f32[96,2048]{1,0:T(8,128)S(1)}, u32[]{:S(2)}, u32[]{:S(2)}) %collective-permute-start.4) | collective-permute-done | bytes 786464 | tf_op jit(solution)/shard_map/ppermute | solution.py:500
  82.4 24.9 %collective-permute-done.5 = f32[96,2048]{1,0:T(8,128)S(1)} collective-permute-done((f32[96,2048]{1,0:T(8,128)}, f32[96,2048]{1,0:T(8,128)S(1)}, u32[]{:S(2)}, u32[]{:S(2)}) %collective-permute-start.5) | collective-permute-done | bytes 786464 | tf_op jit(solution)/shard_map/ppermute | solution.py:500
  107.3 1.3 %add_add_fusion = f32[96,2048]{1,0:T(8,128)S(1)} fusion(f32[96,2048]{1,0:T(8,128)S(1)} %collective-permute-done.5, f32[96,2048]{1,0:T(8,128)} %get-tuple-element.8, f32[96,2048]{1,0:T(8,128)S(1)} %collective-permute-done.4), kind=kLoop, calls=%fused_computation | loop fusion | flops 393216 | bytes 3145728 | tf_op jit(solution)/shard_map/add | solution.py:500
  108.6 4.3 %collective-permute-start.6 = (f32[32,2048]{1,0:T(8,128)S(1)}, f32[32,2048]{1,0:T(8,128)S(1)}, u32[]{:S(2)}, u32[]{:S(2)}) collective-permute-start(f32[32,2048]{1,0:T(8,128)S(1)} %get-tuple-element.11), channel_id=1, source_target_pairs={{8,0},{16,8},{24,16},{32,24},{40,32},{48,40},{56,48},{64,56},{72,6... | collective-permute-start | bytes 786440 | tf_op jit(solution)/shard_map/ppermute | solution.py:503
  112.9 1.9 %collective-permute-start.7 = (f32[32,2048]{1,0:T(8,128)S(1)}, f32[32,2048]{1,0:T(8,128)S(1)}, u32[]{:S(2)}, u32[]{:S(2)}) collective-permute-start(f32[32,2048]{1,0:T(8,128)S(1)} %get-tuple-element.12), channel_id=1, source_target_pairs={{0,8},{8,16},{16,24},{24,32},{32,40},{40,48},{48,56},{56,64},{64,7... | collective-permute-start | bytes 786440 | tf_op jit(solution)/shard_map/ppermute | solution.py:504
  114.8 4.7 %collective-permute-done.6 = f32[32,2048]{1,0:T(8,128)S(1)} collective-permute-done((f32[32,2048]{1,0:T(8,128)S(1)}, f32[32,2048]{1,0:T(8,128)S(1)}, u32[]{:S(2)}, u32[]{:S(2)}) %collective-permute-start.6) | collective-permute-done | bytes 262176 | tf_op jit(solution)/shard_map/ppermute | solution.py:503
  119.6 4.0 %collective-permute-done.7 = f32[32,2048]{1,0:T(8,128)S(1)} collective-permute-done((f32[32,2048]{1,0:T(8,128)S(1)}, f32[32,2048]{1,0:T(8,128)S(1)}, u32[]{:S(2)}, u32[]{:S(2)}) %collective-permute-start.7) | collective-permute-done | bytes 262176 | tf_op jit(solution)/shard_map/ppermute | solution.py:504
  123.6 0.8 fusion.3
  (4 shorter events, 0.1 us)
Async XLA Ops:
  0.0 19.9 %copy-start = (f32[32,2048]{1,0:T(8,128)S(1)}, f32[32,2048]{1,0:T(8,128)}, u32[]{:S(2)}) copy-start(f32[32,2048]{1,0:T(8,128)} %param.21) | copy-start | bytes 786436
  0.0 19.9 %collective-permute-start = (f32[32,2048]{1,0:T(8,128)}, f32[32,2048]{1,0:T(8,128)S(1)}, u32[]{:S(2)}, u32[]{:S(2)}) collective-permute-start(f32[32,2048]{1,0:T(8,128)} %param.21), channel_id=1, source_target_pairs={{0,8},{8,16},{16,24},{24,32},{32,40},{40,48},{48,56},{56,64},{64,7... | collective-permute-start | bytes 786440 | tf_op jit(solution)/shard_map/ppermute | solution.py:492
  3.6 16.3 %collective-permute-start.1 = (f32[32,2048]{1,0:T(8,128)}, f32[32,2048]{1,0:T(8,128)S(1)}, u32[]{:S(2)}, u32[]{:S(2)}) collective-permute-start(f32[32,2048]{1,0:T(8,128)} %param.21), channel_id=1, source_target_pairs={{8,0},{16,8},{24,16},{32,24},{40,32},{48,40},{56,48},{64,56},{72,6... | collective-permute-start | bytes 786440 | tf_op jit(solution)/shard_map/ppermute | solution.py:493
  20.0 10.0 %copy-start.1 = (f32[96,2048]{1,0:T(8,128)}, f32[96,2048]{1,0:T(8,128)S(1)}, u32[]{:S(2)}) copy-start(f32[96,2048]{1,0:T(8,128)S(1)} %constant_dynamic-update-slice_fusion.own_ref) | copy-start | bytes 2359300
  20.0 13.3 %collective-permute-start.2 = (f32[96,2048]{1,0:T(8,128)S(1)}, f32[96,2048]{1,0:T(8,128)S(1)}, u32[]{:S(2)}, u32[]{:S(2)}) collective-permute-start(f32[96,2048]{1,0:T(8,128)S(1)} %constant_dynamic-update-slice_fusion.own_ref), channel_id=1, source_target_pairs={{0,1},{1,2},{2,3},{3,4},{4,5},{5,6},{6,7},{8,9},{9,10},{10,11},{11... | collective-permute-start | bytes 2359304 | tf_op jit(solution)/shard_map/ppermute | solution.py:495
  21.9 13.1 %collective-permute-start.3 = (f32[96,2048]{1,0:T(8,128)S(1)}, f32[96,2048]{1,0:T(8,128)S(1)}, u32[]{:S(2)}, u32[]{:S(2)}) collective-permute-start(f32[96,2048]{1,0:T(8,128)S(1)} %constant_dynamic-update-slice_fusion.own_ref), channel_id=1, source_target_pairs={{1,0},{2,1},{3,2},{4,3},{5,4},{6,5},{7,6},{9,8},{10,9},{11,10},{12... | collective-permute-start | bytes 2359304 | tf_op jit(solution)/shard_map/ppermute | solution.py:496
  33.3 1.8 %copy-start.2 = (f32[96,2048]{1,0:T(8,128)}, f32[96,2048]{1,0:T(8,128)S(1)}, u32[]{:S(2)}) copy-start(f32[96,2048]{1,0:T(8,128)S(1)} %collective-permute-done.2.left_ref) | copy-start | bytes 2359300
  35.0 1.0 copy-start.3
  70.7 11.7 %collective-permute-start.4 = (f32[96,2048]{1,0:T(8,128)}, f32[96,2048]{1,0:T(8,128)S(1)}, u32[]{:S(2)}, u32[]{:S(2)}) collective-permute-start(f32[96,2048]{1,0:T(8,128)} %get-tuple-element.9), channel_id=1, source_target_pairs={{1,0},{2,1},{3,2},{4,3},{5,4},{6,5},{7,6},{9,8},{10,9},{11,10},{12... | collective-permute-start | bytes 2359304 | tf_op jit(solution)/shard_map/ppermute | solution.py:500
  72.6 34.7 %collective-permute-start.5 = (f32[96,2048]{1,0:T(8,128)}, f32[96,2048]{1,0:T(8,128)S(1)}, u32[]{:S(2)}, u32[]{:S(2)}) collective-permute-start(f32[96,2048]{1,0:T(8,128)} %get-tuple-element.10), channel_id=1, source_target_pairs={{0,1},{1,2},{2,3},{3,4},{4,5},{5,6},{6,7},{8,9},{9,10},{10,11},{11... | collective-permute-start | bytes 2359304 | tf_op jit(solution)/shard_map/ppermute | solution.py:500
  108.6 11.0 %collective-permute-start.6 = (f32[32,2048]{1,0:T(8,128)S(1)}, f32[32,2048]{1,0:T(8,128)S(1)}, u32[]{:S(2)}, u32[]{:S(2)}) collective-permute-start(f32[32,2048]{1,0:T(8,128)S(1)} %get-tuple-element.11), channel_id=1, source_target_pairs={{8,0},{16,8},{24,16},{32,24},{40,32},{48,40},{56,48},{64,56},{72,6... | collective-permute-start | bytes 786440 | tf_op jit(solution)/shard_map/ppermute | solution.py:503
  112.9 10.7 %collective-permute-start.7 = (f32[32,2048]{1,0:T(8,128)S(1)}, f32[32,2048]{1,0:T(8,128)S(1)}, u32[]{:S(2)}, u32[]{:S(2)}) collective-permute-start(f32[32,2048]{1,0:T(8,128)S(1)} %get-tuple-element.12), channel_id=1, source_target_pairs={{0,8},{8,16},{16,24},{24,32},{32,40},{40,48},{48,56},{56,64},{64,7... | collective-permute-start | bytes 786440 | tf_op jit(solution)/shard_map/ppermute | solution.py:504

commit v4 on v3

--- a/solution.py
+++ b/solution.py
@@ -26,7 +26,10 @@
 YPITCH = BY + 4
 BIGPITCH = PY + 4
 WX = BX + K
-VMEM_LIMIT = 60 * 1024 * 1024
+MIB = 1024 * 1024
+OTF_LIMIT = 32 * MIB
+MAIN_LIMIT = 48 * MIB
+TAIL_LIMIT = 16 * MIB
 
 F32 = jnp.float32
 BF16 = jnp.bfloat16
@@ -131,6 +134,10 @@
 
 def aligned(index, size):
     return pl.ds(pl.multiple_of(index * size, size), size)
+
+
+def columns(pair, pairs):
+    return slice(pair * LANES, (pair + pairs) * LANES)
 
 
 def drop_padding(rows):
@@ -172,32 +179,24 @@
 
 def pipelined(count, first, second, stash):
     first(0, stash[0])
-    if count == 1:
-        second(0, stash[0])
-
-    def body(j):
-        step = 2 * j
-        first(step + 1, stash[1])
-        second(step, stash[0])
-        first(jnp.minimum(step + 2, count - 1), stash[0])
-        second(step + 1, stash[1])
-
-    loop(count // 2, body)
-
-
-def z_then_x(read, count, wz, wx, real_ref, imag_ref, first_pair, copies, stash):
+    for step in range(count):
+        if step + 1 < count:
+            first(step + 1, stash[(step + 1) % 2])
+        second(step, stash[step % 2])
+
+
+def z_then_x(read, count, wz, wx, real_ref, imag_ref, copies, stash):
     pairs = stash[0].shape[0] // (2 * KZ) * copies
-    count = count // pairs
 
     def first(step, ref):
-        data = read(aligned(step, pairs * LANES))
+        data = read(step * pairs, pairs)
         pieces = [data[:, p * LANES:(p + 1) * LANES] for p in range(pairs)]
         ref[...] = z_stage(pieces, wz[...], copies)
 
     def second(step, ref):
-        x_stage(ref[...], wx[...], real_ref, imag_ref, first_pair + step * pairs, copies)
-
-    pipelined(count, first, second, stash)
+        x_stage(ref[...], wx[...], real_ref, imag_ref, step * pairs, copies)
+
+    pipelined(count // pairs, first, second, stash)
 
 
 def along_y(table, reals, imags):
@@ -239,31 +238,68 @@
     return out[:table.shape[0] // 2] + out[table.shape[0] // 2:] if tall else out
 
 
-def otf_kernel(begin, count_ref, ids_ref, psf_ref, wz_ref, wx_ref, wy_ref, *rest):
-    out_ref, real, imag, stash0, stash1 = rest[-5:]
-
-    @pl.when(pl.program_id(0) + begin < count_ref[0])
+def otf_kernel(begin, end, count_ref, ids_ref, psf_hbm, wz_ref, wx_ref, wy_ref, *rest):
+    out_hbm, psf, out, real, imag, stash0, stash1, psf_sem, out_sem = rest[-9:]
+    steps = KZ // (2 * UY)
+
+    def fetch(step):
+        buffer = lax.rem(step, 2)
+        return pltpu.make_async_copy(
+            psf_hbm.at[ids_ref[begin + step]], psf.at[buffer], psf_sem.at[buffer]
+        )
+
+    def store(step, j):
+        where = pl.ds(j * 2 * UY, 2 * UY)
+        return pltpu.make_async_copy(
+            out.at[where], out_hbm.at[begin + step, where], out_sem.at[j]
+        )
+
+    slots = jnp.maximum(jnp.minimum(count_ref[0], end) - begin, 0)
+
+    @pl.when(slots > 0)
     def _():
-        def read(columns):
-            return psf_ref[0, :, columns]
-
-        z_then_x(read, K // 2, wz_ref, wx_ref, real, imag, 0, 1, (stash0, stash1))
+        fetch(0).start()
+
+    def body(step, carry):
+        buffer = lax.rem(step, 2)
+        fetch(step).wait()
+
+        @pl.when(step + 1 < slots)
+        def _():
+            fetch(step + 1).start()
+
+        def read(pair, pairs):
+            return psf[buffer, :, columns(pair, pairs)]
+
+        z_then_x(read, K // 2, wz_ref, wx_ref, real, imag, 1, (stash0, stash1))
 
         def y(j):
+            @pl.when(step > 0)
+            def _():
+                store(step - 1, j).wait()
+
             for pair in range(UY):
                 kz = (j * UY + pair) * 2
-                for at, out in enumerate(y_from_rows(wy_ref[...], real, imag, kz, K)):
-                    out_ref[0, kz + at, 0] = out[0]
-                    out_ref[0, kz + at, 1] = out[1]
-
-        loop(KZ // (2 * UY), y)
+                for at, value in enumerate(y_from_rows(wy_ref[...], real, imag, kz, K)):
+                    out[kz + at, 0] = value[0]
+                    out[kz + at, 1] = value[1]
+            store(step, j).start()
+
+        loop(steps, y)
+        return carry
+
+    lax.fori_loop(0, slots, body, 0)
+
+    @pl.when(slots > 0)
+    def _():
+        for j in range(steps):
+            store(slots - 1, j).wait()
 
 
 ZPO = 16
 ZPF = 8
 ZPE = 8
 UX = 2
-UXZ = 1
 UY = 12
 UP = 12
 UG = 12
@@ -271,44 +307,81 @@
 UT = 12
 
 
+def final_sums(wxo, wzi, chunks, stash):
+    def first(step, ref):
+        real_ref, imag_ref, row, _, _ = chunks[step]
+        for group in range(2):
+            ys = [row + group * 4 + k for k in range(4)]
+            out = x_from_rows(wxo[...], real_ref, imag_ref, ys, YPITCH)
+            for pair in range(2):
+                piece = out[:, pair * LANES:(pair + 1) * LANES]
+                data = jnp.concatenate([piece[:WX], piece[WX:]], axis=1)
+                at = (group * 2 + pair) * WX
+                ref[at:at + WX, :] = three(data, 1)
+
+    def second(step, ref):
+        _, _, _, out, pair = chunks[step]
+        sums = dot(ref[...], wzi[...])
+        for at in range(4):
+            out[:, columns(pair + at, 1)] = sums[at * WX:(at + 1) * WX]
+
+    pipelined(len(chunks), first, second, stash)
+
+
 def main_kernel(
-    count_ref, ids_ref, left_ref, own_ref, right_ref, image_ref, otf_ref,
+    count_ref, ids_ref, left_ref, own_ref, right_ref, views_hbm, otf_hbm,
     wz_ref, wzi_ref, wxf_ref, wyf_ref, wyi_ref, wxi_ref, wxe_ref, wye_ref, wyo_ref, wxo_ref,
-    left_out, own_out, right_out,
-    field, total, big_real, big_imag, real, imag, lines, error,
-    wide0, wide1, thin0, thin1,
+    left_out, right_out, real_hbm, imag_hbm,
+    field, total, big_real, big_imag, real, imag, lines, error, otf, image,
+    wide0, wide1, thin0, thin1, last0, last1, otf_sem, image_sem, own_sem,
 ):
-    slot = pl.program_id(0)
-
-    @pl.when(slot == 0)
-    def _():
-        for part, ref in enumerate((left_ref, own_ref, right_ref)):
-            def read(columns, ref=ref):
-                return ref[:, columns]
-
-            z_then_x(
-                read, BY // 2, wz_ref, wxf_ref, big_real, big_imag, part * (BY // 2), 1, (wide0, wide1)
-            )
-
-        def y(j):
-            for pair in range(UF):
-                kz = (j * UF + pair) * 2
-                for at, out in enumerate(y_from_rows(wyf_ref[...], big_real, big_imag, kz, PY)):
-                    for part in range(2):
-                        field[kz + at, part] = out[part]
-                        total[kz + at, part] = jnp.zeros((PY, LANES), F32)
-
-        loop(KZ // (2 * UF), y)
-
-    @pl.when(slot < count_ref[0])
-    def _():
+    count = count_ref[0]
+
+    def fetch(slot):
+        buffer = lax.rem(slot, 2)
+        return (
+            pltpu.make_async_copy(otf_hbm.at[slot], otf.at[buffer], otf_sem.at[buffer]),
+            pltpu.make_async_copy(
+                views_hbm.at[ids_ref[slot]], image.at[buffer], image_sem.at[buffer]
+            ),
+        )
+
+    for copy in fetch(0):
+        copy.start()
+
+    def read_window(pair, pairs):
+        part, pair = divmod(pair, BY // 2)
+        return (left_ref, own_ref, right_ref)[part][:, columns(pair, pairs)]
+
+    z_then_x(read_window, PY // 2, wz_ref, wxf_ref, big_real, big_imag, 1, (wide0, wide1))
+
+    def field_y(j):
+        for pair in range(UF):
+            kz = (j * UF + pair) * 2
+            for at, out in enumerate(y_from_rows(wyf_ref[...], big_real, big_imag, kz, PY)):
+                for part in range(2):
+                    field[kz + at, part] = out[part]
+                    total[kz + at, part] = jnp.zeros((PY, LANES), F32)
+
+    loop(KZ // (2 * UF), field_y)
+
+    def view(slot, carry):
+        buffer = lax.rem(slot, 2)
+        for copy in fetch(slot):
+            copy.wait()
+
+        @pl.when(slot + 1 < count)
+        def _():
+            for copy in fetch(slot + 1):
+                copy.start()
+
         def product(j):
             for pair in range(UP):
                 kz = (j * UP + pair) * 2
                 reals, imags = [], []
                 for at in range(2):
                     fr, fi = field[kz + at, 0], field[kz + at, 1]
-                    pr, pi = otf_ref[0, kz + at, 0], otf_ref[0, kz + at, 1]
+                    pr, pi = otf[buffer, kz + at, 0], otf[buffer, kz + at, 1]
                     reals.append(fr * pr - fi * pi)
                     imags.append(fr * pi + fi * pr)
                 for at, out in enumerate(along_y(wyi_ref[...], reals, imags)):
@@ -329,100 +402,99 @@
 
         loop(BY // 8, inverse_x, UX)
 
-        def relative(j):
-            blurred = dot(lines[aligned(j, 8 * BX), :], wzi_ref[...])
+        for j in range(2):
+            blurred = dot(lines[j * 8 * BX:(j + 1) * 8 * BX, :], wzi_ref[...])
             for pair in range(8):
-                columns = aligned(j * 8 + pair, LANES)
-                error[:, columns] = image_ref[0, :, columns] / blurred[pair * BX:(pair + 1) * BX] - 1.0
-
-        loop(2, relative)
-
-        def read(columns):
-            return error[:, columns]
-
-        z_then_x(read, BY // 2, wz_ref, wxe_ref, real, imag, 0, 2, (thin0, thin1))
+                where = columns(j * 8 + pair, 1)
+                error[:, where] = image[buffer, :, where] / blurred[pair * BX:(pair + 1) * BX] - 1.0
+
+        def read_error(pair, pairs):
+            return error[:, columns(pair, pairs)]
+
+        z_then_x(read_error, BY // 2, wz_ref, wxe_ref, real, imag, 2, (thin0, thin1))
 
         def gather(j):
             for pair in range(UG):
                 kz = (j * UG + pair) * 2
                 for at, (er, ei) in enumerate(y_from_rows(wye_ref[...], real, imag, kz, BY)):
-                    pr, pi = otf_ref[0, kz + at, 0], otf_ref[0, kz + at, 1]
+                    pr, pi = otf[buffer, kz + at, 0], otf[buffer, kz + at, 1]
                     total[kz + at, 0] += er * pr + ei * pi
                     total[kz + at, 1] += ei * pr - er * pi
 
         loop(KZ // (2 * UG), gather)
-
-    @pl.when(slot == CMAX - 1)
-    def _():
-        def inverse_y(j):
-            for pair in range(UT):
-                kz = (j * UT + pair) * 2
-                reals = [total[kz + at, 0] for at in range(2)]
-                imags = [total[kz + at, 1] for at in range(2)]
-                for at, out in enumerate(along_y(wyo_ref[...], reals, imags)):
-                    where = pl.ds((kz + at) * BIGPITCH, PY)
-                    big_real[where, :] = out[0]
-                    big_imag[where, :] = out[1]
-
-        loop(KZ // (2 * UT), inverse_y)
-
-        for part, ref in enumerate((left_out, own_out, right_out)):
-            def inverse_xz(j, part=part, ref=ref):
-                rows = []
-                for group in range(2):
-                    y = part * BY + j * 8 + group * 4
-                    out = x_from_rows(wxo_ref[...], big_real, big_imag, [y + k for k in range(4)], BIGPITCH)
-                    for pair in range(2):
-                        piece = out[:, pair * LANES:(pair + 1) * LANES]
-                        rows.append(jnp.concatenate([piece[:WX], piece[WX:]], axis=1))
-                sums = dot(three(jnp.concatenate(rows, axis=0), 1), wzi_ref[...])
-                for pair in range(4):
-                    ref[:, aligned(j * 4 + pair, LANES)] = sums[pair * WX:(pair + 1) * WX]
-
-            loop(BY // 8, inverse_xz, UXZ)
-
-
-def whole(shape):
-    return pl.BlockSpec(shape, lambda *_: (0,) * len(shape))
-
-
-def last_slot(slot, count):
-    return jnp.minimum(slot, count[0] - 1)
+        return carry
+
+    lax.fori_loop(0, count, view, 0)
+
+    def inverse_y(j):
+        for pair in range(UT):
+            kz = (j * UT + pair) * 2
+            reals = [total[kz + at, 0] for at in range(2)]
+            imags = [total[kz + at, 1] for at in range(2)]
+            for at, out in enumerate(along_y(wyo_ref[...], reals, imags)):
+                row = (kz + at) * YPITCH
+                for value, big, own in zip(out, (big_real, big_imag), (real, imag)):
+                    big[pl.ds(row, BY), :] = value[:BY]
+                    own[pl.ds(row, BY), :] = value[BY:2 * BY]
+                    big[pl.ds(KZ * YPITCH + row, BY), :] = value[2 * BY:]
+
+    loop(KZ // (2 * UT), inverse_y)
+    copies = (
+        pltpu.make_async_copy(real, real_hbm, own_sem.at[0]),
+        pltpu.make_async_copy(imag, imag_hbm, own_sem.at[1]),
+    )
+    for copy in copies:
+        copy.start()
+    chunks = [
+        (big_real, big_imag, side * KZ * YPITCH + y, out, y // 2)
+        for side, out in enumerate((left_out, right_out))
+        for y in range(0, BY, 8)
+    ]
+    final_sums(wxo_ref, wzi_ref, chunks, (last0, last1))
+    for copy in copies:
+        copy.wait()
+
+
+def tail_kernel(real, imag, wzi_ref, wxo_ref, out, last0, last1):
+    chunks = [(real, imag, y, out, y // 2) for y in range(0, BY, 8)]
+    final_sums(wxo_ref, wzi_ref, chunks, (last0, last1))
 
 
 SPECTRUM = (KZ, 2, PY, LANES)
+ROWS = (KZ * YPITCH, LANES)
+WIDE = (WX, BY * SZ)
+LAST = pltpu.VMEM((4 * WX, 6 * LANES), BF16)
+IN_VMEM = pl.BlockSpec(memory_space=pltpu.VMEM)
+IN_SMEM = pl.BlockSpec(memory_space=pltpu.SMEM)
+ANYWHERE = pl.BlockSpec(memory_space=pl.ANY)
 
 
 def otf_call(count, ids, psf, begin, end, held=None):
     tables = (z_forward(-HALF), x_forward(K, -HALF, K), y_forward(K, -HALF))
-
-    def out_slot(s, c):
-        return jnp.clip(s + begin, begin, jnp.maximum(c[0] - 1, begin))
-
     inputs = [count, ids, psf] + [jnp.asarray(t) for t in tables]
-    specs = [
-        pl.BlockSpec((1, K, K * K), lambda s, c, i: (i[last_slot(s + begin, c)], 0, 0)),
-    ] + [whole(t.shape) for t in tables]
+    specs = [IN_SMEM, IN_SMEM, ANYWHERE] + [IN_VMEM] * len(tables)
     aliases = {}
     if held is not None:
         aliases = {len(inputs): 0}
         inputs.append(held)
-        specs.append(pl.BlockSpec(memory_space=pl.ANY))
+        specs.append(ANYWHERE)
     return pl.pallas_call(
-        functools.partial(otf_kernel, begin),
+        functools.partial(otf_kernel, begin, end),
         out_shape=jax.ShapeDtypeStruct((CMAX,) + SPECTRUM, F32),
-        grid_spec=pltpu.PrefetchScalarGridSpec(
-            num_scalar_prefetch=2,
-            grid=(end - begin,),
-            in_specs=specs,
-            out_specs=pl.BlockSpec(
-                (1,) + SPECTRUM, lambda s, c, i: (out_slot(s, c), 0, 0, 0, 0)
-            ),
-            scratch_shapes=[pltpu.VMEM((K * KPITCH, LANES), F32)] * 2
-            + [pltpu.VMEM((ZPO * 2 * KZ, 3 * LANES), BF16)] * 2,
-        ),
+        in_specs=specs,
+        out_specs=ANYWHERE,
+        scratch_shapes=[
+            pltpu.VMEM((2, K, K * K), F32),
+            pltpu.VMEM(SPECTRUM, F32),
+            pltpu.VMEM((K * KPITCH, LANES), F32),
+            pltpu.VMEM((K * KPITCH, LANES), F32),
+            pltpu.VMEM((ZPO * 2 * KZ, 3 * LANES), BF16),
+            pltpu.VMEM((ZPO * 2 * KZ, 3 * LANES), BF16),
+            pltpu.SemaphoreType.DMA((2,)),
+            pltpu.SemaphoreType.DMA((KZ // (2 * UY),)),
+        ],
         input_output_aliases=aliases,
-        compiler_params=pltpu.CompilerParams(vmem_limit_bytes=VMEM_LIMIT),
+        compiler_params=pltpu.CompilerParams(vmem_limit_bytes=OTF_LIMIT),
         cost_estimate=pl.CostEstimate(
             flops=4 * 10**9 * (end - begin), bytes_accessed=6 * 10**6 * (end - begin), transcendentals=0
         ),
@@ -432,7 +504,6 @@
 
 def main_call(count, ids, window, views, otf):
     left, own, right = window
-    rows_wide = (WX, BY * SZ)
     tables = (
         z_forward(0),
         z_inverse(),
@@ -447,34 +518,48 @@
     )
     return pl.pallas_call(
         main_kernel,
-        out_shape=[jax.ShapeDtypeStruct(rows_wide, F32)] * 3,
-        grid_spec=pltpu.PrefetchScalarGridSpec(
-            num_scalar_prefetch=2,
-            grid=(CMAX,),
-            in_specs=[whole(rows_wide)] * 3 + [
-                pl.BlockSpec((1, BX, BY * SZ), lambda s, c, i: (i[last_slot(s, c)], 0, 0)),
-                pl.BlockSpec((1,) + SPECTRUM, lambda s, c, i: (last_slot(s, c), 0, 0, 0, 0)),
-            ] + [whole(t.shape) for t in tables],
-            out_specs=[whole(rows_wide)] * 3,
-            scratch_shapes=[
-                pltpu.VMEM(SPECTRUM, F32),
-                pltpu.VMEM(SPECTRUM, F32),
-                pltpu.VMEM((PY * KPITCH, LANES), F32),
-                pltpu.VMEM((PY * KPITCH, LANES), F32),
-                pltpu.VMEM((KZ * YPITCH, LANES), F32),
-                pltpu.VMEM((KZ * YPITCH, LANES), F32),
-                pltpu.VMEM((BX * BY // 2, 6 * LANES), BF16),
-                pltpu.VMEM((BX, BY * SZ), F32),
-                pltpu.VMEM((ZPF * 2 * KZ, 6 * LANES), BF16),
-                pltpu.VMEM((ZPF * 2 * KZ, 6 * LANES), BF16),
-                pltpu.VMEM((ZPE * KZ, 3 * LANES), BF16),
-                pltpu.VMEM((ZPE * KZ, 3 * LANES), BF16),
-            ],
-        ),
-        compiler_params=pltpu.CompilerParams(vmem_limit_bytes=VMEM_LIMIT),
+        out_shape=[jax.ShapeDtypeStruct(WIDE, F32)] * 2 + [jax.ShapeDtypeStruct(ROWS, F32)] * 2,
+        in_specs=[IN_SMEM] * 2 + [IN_VMEM] * 3 + [ANYWHERE] * 2 + [IN_VMEM] * len(tables),
+        out_specs=[IN_VMEM] * 2 + [ANYWHERE] * 2,
+        scratch_shapes=[
+            pltpu.VMEM(SPECTRUM, F32),
+            pltpu.VMEM(SPECTRUM, F32),
+            pltpu.VMEM((PY * KPITCH, LANES), F32),
+            pltpu.VMEM((PY * KPITCH, LANES), F32),
+            pltpu.VMEM(ROWS, F32),
+            pltpu.VMEM(ROWS, F32),
+            pltpu.VMEM((BX * BY // 2, 6 * LANES), BF16),
+            pltpu.VMEM((BX, BY * SZ), F32),
+            pltpu.VMEM((2,) + SPECTRUM, F32),
+            pltpu.VMEM((2, BX, BY * SZ), F32),
+            pltpu.VMEM((ZPF * 2 * KZ, 6 * LANES), BF16),
+            pltpu.VMEM((ZPF * 2 * KZ, 6 * LANES), BF16),
+            pltpu.VMEM((ZPE * KZ, 3 * LANES), BF16),
+            pltpu.VMEM((ZPE * KZ, 3 * LANES), BF16),
+            LAST,
+            LAST,
+            pltpu.SemaphoreType.DMA((2,)),
+            pltpu.SemaphoreType.DMA((2,)),
+            pltpu.SemaphoreType.DMA((2,)),
+        ],
+        compiler_params=pltpu.CompilerParams(vmem_limit_bytes=MAIN_LIMIT),
         cost_estimate=pl.CostEstimate(flops=30 * 10**9, bytes_accessed=40 * 10**6, transcendentals=0),
         name="views",
     )(count, ids, left, own, right, views, otf, *[jnp.asarray(t) for t in tables])
+
+
+def tail_call(real, imag):
+    tables = (z_inverse(), x_inverse(WX, 0, three_parts))
+    return pl.pallas_call(
+        tail_kernel,
+        out_shape=jax.ShapeDtypeStruct(WIDE, F32),
+        in_specs=[IN_VMEM] * 4,
+        out_specs=IN_VMEM,
+        scratch_shapes=[LAST, LAST],
+        compiler_params=pltpu.CompilerParams(vmem_limit_bytes=TAIL_LIMIT),
+        cost_estimate=pl.CostEstimate(flops=4 * 10**9, bytes_accessed=3 * 10**6, transcendentals=0),
+        name="tail",
+    )(real, imag, *[jnp.asarray(t) for t in tables])
 
 
 def shifts(axis):
@@ -496,8 +581,10 @@
     right = lax.ppermute(own, "by", down_y)
     otf = otf_call(count, ids, psf, 0, 2)
     otf = otf_call(count, ids, psf, 2, CMAX, otf)
-    left_sum, own_sum, right_sum = main_call(count, ids, (left, own, right), views, otf)
-    sums = own_sum + lax.ppermute(left_sum, "by", down_y) + lax.ppermute(right_sum, "by", up_y)
+    left_sum, right_sum, real, imag = main_call(count, ids, (left, own, right), views, otf)
+    from_right = lax.ppermute(left_sum, "by", down_y)
+    from_left = lax.ppermute(right_sum, "by", up_y)
+    sums = tail_call(real, imag) + from_right + from_left
     correction = (
         sums[BX:2 * BX]
         + lax.ppermute(sums[:BX], "bx", down_x)

time: 125 us -> 114 us (0.912)
  waiting for transfers between devices: 44.7 us -> 14.4 us
  Pallas kernels: 50.1 us -> 62.5 us
  local copies, waits for them, and re-layouts: 1.06 us -> 10.2 us
  starting transfers between devices: 25.8 us -> 23.7 us
    ppermute x2, waiting for transfers between devices: 30.9 us -> 6.87 us  [the longest x1 3.82 us: per_device(): from_left = lax.ppermute(right_sum, 'by', up_y)]
    pallas_call x3 -> x4, Pallas kernels: 50.1 us -> 62.5 us  [the longest x1 40.6 us: main_call(): pl.pallas_call(main_kernel, out_shape=[jax.ShapeDtypeStruct(WIDE, F32)] *...]
    unnamed x10 -> x42, local copies, waits for them, and re-layouts: 1.01 us -> 10.2 us
    ppermute x1, waiting for transfers between devices: 3.29 us -> 0.01 us  [per_device(): left = lax.ppermute(own, 'by', up_y)]
    ppermute x1, starting transfers between devices: 4.32 us -> 1.92 us  [per_device(): lax.ppermute(sums[:BX], 'bx', down_x)]
    ppermute x1, starting transfers between devices: 1.92 us -> 3.92 us  [per_device(): lax.ppermute(sums[2 * BX:], 'bx', up_x)]
    ppermute x1, waiting for transfers between devices: 1.75 us -> 0.01 us  [per_device(): right = lax.ppermute(own, 'by', down_y)]
    ppermute x2, starting transfers between devices: 5.71 us -> 4.33 us  [the longest x1 2.39 us: per_device(): from_left = lax.ppermute(right_sum, 'by', up_y)]
  transfers between devices with their start and end apart: 8 -> 8, of which waited for: 6 -> 4; matrix products, arithmetic and copies ran while one was open for 0% -> 0% of each run, Pallas kernels for 12% -> 19%
where the time goes in v4:
time: 114 us; the launch traced here: 113 us
  Pallas kernels  62.5 us (55%)
  starting transfers between devices  23.7 us (21%)
  waiting for transfers between devices  14.4 us (13%)
  local copies, waits for them, and re-layouts  10.2 us (9%)
    pallas_call x1, Pallas kernels, main_call(): pl.pallas_call(main_kernel, out_shape=[jax.ShapeDtypeStruct(WIDE, F32)] *...  40.6 us
    pallas_call x2, Pallas kernels, otf_call(): pl.pallas_call(functools.partial(otf_kernel, begin, end), out_shape=jax.S...  20.2 us
    unnamed x42, local copies, waits for them, and re-layouts  10.2 us
    ppermute x1, starting transfers between devices, per_device(): after = lax.ppermute(estimate, 'bx', down_x)  4.47 us
    ppermute x1, waiting for transfers between devices, per_device(): lax.ppermute(sums[2 * BX:], 'bx', up_x)  4.04 us
    ppermute x1, starting transfers between devices, per_device(): lax.ppermute(sums[2 * BX:], 'bx', up_x)  3.92 us
    ppermute x1, waiting for transfers between devices, per_device(): from_left = lax.ppermute(right_sum, 'by', up_y)  3.82 us
    ppermute x1, starting transfers between devices, per_device(): right = lax.ppermute(own, 'by', down_y)  3.64 us
  transfers between devices with their start and end apart: 8, of which 4 were waited for; matrix products, arithmetic and copies ran while one was open for 0% of the time, Pallas kernels for 19%

profile of v4, /device:TPU:66, one launch (start us, length us, event | category | flops | bytes accessed | tf_op | source)
XLA Modules:
  0.0 112.8 jit_solution(10527434458529504702)
XLA Ops:
  0.0 3.5 %collective-permute-start = (f32[32,2048]{1,0:T(8,128)}, f32[32,2048]{1,0:T(8,128)S(1)}, u32[]{:S(2)}, u32[]{:S(2)}) collective-permute-start(f32[32,2048]{1,0:T(8,128)} %param.23), channel_id=1, source_target_pairs={{0,8},{8,16},{16,24},{24,32},{32,40},{40,48},{48,56},{56,64},{64,7... | collective-permute-start | bytes 786440 | tf_op jit(solution)/shard_map/ppermute | solution.py:577
  3.5 4.5 %collective-permute-start.1 = (f32[32,2048]{1,0:T(8,128)}, f32[32,2048]{1,0:T(8,128)S(1)}, u32[]{:S(2)}, u32[]{:S(2)}) collective-permute-start(f32[32,2048]{1,0:T(8,128)} %param.23), channel_id=1, source_target_pairs={{8,0},{16,8},{24,16},{32,24},{40,32},{48,40},{56,48},{64,56},{72,6... | collective-permute-start | bytes 786440 | tf_op jit(solution)/shard_map/ppermute | solution.py:578
  8.6 0.0 copy-start
  8.6 3.4 %copy-done = f32[8,64,4096]{2,1,0:T(8,128)S(1)} copy-done((f32[8,64,4096]{2,1,0:T(8,128)S(1)}, f32[8,64,4096]{2,1,0:T(8,128)}, u32[]{:S(2)}) %copy-start) | copy-done | bytes 8388632
  12.0 0.9 copy-done.1
  12.9 0.9 copy-done.2
  13.8 0.9 copy-done.3
  14.8 0.7 copy-done.4
  15.4 8.5 %otf.2.rest_0_ = f32[5,48,2,96,128]{4,3,2,1,0:T(8,128)} custom-call(s32[1]{0:T(128)} %bitcast.3.count_ref, s32[8]{0:T(128)S(1)} %bitcast.7, f32[8,64,4096]{2,1,0:T(8,128)S(1)} %copy-done, bf16[384,256]{1,0:T(8,128)(2,1)S(1)} %copy-done.1, bf16[384,256]{1,0:T(8,128)(2,1)S(1)} %copy-done.2, bf16[192,384]{1,0:T(8,128)(2,1)S(1)} %copy-done.3), custom_call_target="tpu_custom_call" | custom-call | flops 8000000000 | bytes 12000000 | tf_op jit(solution)/shard_map/otf/pallas_call | solution.py:481
  23.9 0.0 collective-permute-done
  24.0 0.0 collective-permute-done.1
  24.0 1.9 %collective-permute-start.2 = (f32[96,2048]{1,0:T(8,128)S(1)}, f32[96,2048]{1,0:T(8,128)S(1)}, u32[]{:S(2)}, u32[]{:S(2)}) collective-permute-start(f32[96,2048]{1,0:T(8,128)S(1)} %constant_dynamic-update-slice_fusion.own_ref), channel_id=1, source_target_pairs={{0,1},{1,2},{2,3},{3,4},{4,5},{5,6},{6,7},{8,9},{9,10},{10,11},{11... | collective-permute-start | bytes 2359304 | tf_op jit(solution)/shard_map/ppermute | solution.py:580
  26.0 3.6 %collective-permute-start.3 = (f32[96,2048]{1,0:T(8,128)S(1)}, f32[96,2048]{1,0:T(8,128)S(1)}, u32[]{:S(2)}, u32[]{:S(2)}) collective-permute-start(f32[96,2048]{1,0:T(8,128)S(1)} %constant_dynamic-update-slice_fusion.own_ref), channel_id=1, source_target_pairs={{1,0},{2,1},{3,2},{4,3},{5,4},{6,5},{7,6},{9,8},{10,9},{11,10},{12... | collective-permute-start | bytes 2359304 | tf_op jit(solution)/shard_map/ppermute | solution.py:581
  29.6 0.0 copy-start.5
  29.6 0.0 copy-start.6
  29.7 0.0 copy-start.7
  29.7 0.0 copy-start.8
  29.7 0.0 copy-start.9
  29.7 0.0 copy-start.10
  29.7 0.0 copy-start.11
  29.7 0.0 copy-start.12
  29.7 0.0 copy-start.13
  29.7 0.0 copy-start.14
  29.8 0.0 copy-start.15
  29.8 11.7 %otf.3.otf_hbm = f32[5,48,2,96,128]{4,3,2,1,0:T(8,128)} custom-call(s32[1]{0:T(128)} %bitcast.4.count_ref, s32[8]{0:T(128)S(1)} %bitcast.8, f32[8,64,4096]{2,1,0:T(8,128)S(1)} %copy-done, bf16[384,256]{1,0:T(8,128)(2,1)S(1)} %copy-done.1, bf16[384,256]{1,0:T(8,128)(2,1)S(1)} %copy-done.2, ...), custom_call_target="tpu_custom_call", output_to_operand_aliasing={{}: (6, {})} | custom-call | flops 12000000000 | bytes 18000000 | tf_op jit(solution)/shard_map/otf/pallas_call | solution.py:481
  41.5 0.0 collective-permute-done.2.left_ref
  41.5 0.0 collective-permute-done.3.right_ref
  41.5 0.9 copy-done.19
  42.5 0.0 copy-done.8
  42.5 0.0 copy-done.9
  42.5 0.0 copy-done.10
  42.5 0.0 copy-done.11
  42.5 0.0 copy-done.12
  42.5 0.0 copy-done.13
  42.5 40.6 %views.1 = (f32[96,2048]{1,0:T(8,128)S(1)}, f32[96,2048]{1,0:T(8,128)S(1)}, f32[1728,128]{1,0:T(8,128)}, f32[1728,128]{1,0:T(8,128)}) custom-call(s32[1]{0:T(128)} %bitcast.5.count_ref, s32[8]{0:T(128)S(1)} %bitcast.9, f32[96,2048]{1,0:T(8,128)S(1)} %collective-permute-done.2.left_ref, f32[96,2048]{1,0:T(8,128)S(1)} %constant_dynamic-update-slice_fusion.own_ref, ...), custom_call_target="tpu_custom_call" | custom-call | flops 30000001024 | bytes 40000000 | tf_op jit(solution)/shard_map/views/pallas_call | solution.py:519
  83.1 1.9 %collective-permute-start.4 = (f32[96,2048]{1,0:T(8,128)S(1)}, f32[96,2048]{1,0:T(8,128)S(1)}, u32[]{:S(2)}, u32[]{:S(2)}) collective-permute-start(f32[96,2048]{1,0:T(8,128)S(1)} %get-tuple-element.11), channel_id=1, source_target_pairs={{1,0},{2,1},{3,2},{4,3},{5,4},{6,5},{7,6},{9,8},{10,9},{11,10},{12... | collective-permute-start | bytes 2359304 | tf_op jit(solution)/shard_map/ppermute | solution.py:585
  85.1 2.4 %collective-permute-start.5 = (f32[96,2048]{1,0:T(8,128)S(1)}, f32[96,2048]{1,0:T(8,128)S(1)}, u32[]{:S(2)}, u32[]{:S(2)}) collective-permute-start(f32[96,2048]{1,0:T(8,128)S(1)} %get-tuple-element.12), channel_id=1, source_target_pairs={{0,1},{1,2},{2,3},{3,4},{4,5},{5,6},{6,7},{8,9},{9,10},{10,11},{11... | collective-permute-start | bytes 2359304 | tf_op jit(solution)/shard_map/ppermute | solution.py:586
  87.5 1.2 %copy-done.16 = f32[1728,128]{1,0:T(8,128)S(1)} copy-done((f32[1728,128]{1,0:T(8,128)S(1)}, f32[1728,128]{1,0:T(8,128)}, u32[]{:S(2)}) %copy-start.16) | copy-done | bytes 884760
  88.7 1.2 %copy-done.17 = f32[1728,128]{1,0:T(8,128)S(1)} copy-done((f32[1728,128]{1,0:T(8,128)S(1)}, f32[1728,128]{1,0:T(8,128)}, u32[]{:S(2)}) %copy-start.17) | copy-done | bytes 884760
  89.8 1.7 %tail.1 = f32[96,2048]{1,0:T(8,128)S(1)} custom-call(f32[1728,128]{1,0:T(8,128)S(1)} %copy-done.16, f32[1728,128]{1,0:T(8,128)S(1)} %copy-done.17, bf16[768,128]{1,0:T(8,128)(2,1)S(1)} %copy-done.11, bf16[192,768]{1,0:T(8,128)(2,1)S(1)} %copy-done.8), custom_call_target="tpu_custom_call" | custom-call | flops 4000000000 | bytes 3000000 | tf_op jit(solution)/shard_map/tail/pallas_call | solution.py:553
  91.5 3.0 %collective-permute-done.4 = f32[96,2048]{1,0:T(8,128)S(1)} collective-permute-done((f32[96,2048]{1,0:T(8,128)S(1)}, f32[96,2048]{1,0:T(8,128)S(1)}, u32[]{:S(2)}, u32[]{:S(2)}) %collective-permute-start.4) | collective-permute-done | bytes 786464 | tf_op jit(solution)/shard_map/ppermute | solution.py:585
  94.6 3.8 %collective-permute-done.5 = f32[96,2048]{1,0:T(8,128)S(1)} collective-permute-done((f32[96,2048]{1,0:T(8,128)S(1)}, f32[96,2048]{1,0:T(8,128)S(1)}, u32[]{:S(2)}, u32[]{:S(2)}) %collective-permute-start.5) | collective-permute-done | bytes 786464 | tf_op jit(solution)/shard_map/ppermute | solution.py:586
  98.4 0.2 add_add_fusion
  98.6 1.9 %collective-permute-start.6 = (f32[32,2048]{1,0:T(8,128)S(1)}, f32[32,2048]{1,0:T(8,128)S(1)}, u32[]{:S(2)}, u32[]{:S(2)}) collective-permute-start(f32[32,2048]{1,0:T(8,128)S(1)} %get-tuple-element.13), channel_id=1, source_target_pairs={{8,0},{16,8},{24,16},{32,24},{40,32},{48,40},{56,48},{64,56},{72,6... | collective-permute-start | bytes 786440 | tf_op jit(solution)/shard_map/ppermute | solution.py:590
  100.5 3.9 %collective-permute-start.7 = (f32[32,2048]{1,0:T(8,128)S(1)}, f32[32,2048]{1,0:T(8,128)S(1)}, u32[]{:S(2)}, u32[]{:S(2)}) collective-permute-start(f32[32,2048]{1,0:T(8,128)S(1)} %get-tuple-element.14), channel_id=1, source_target_pairs={{0,8},{8,16},{16,24},{24,32},{32,40},{40,48},{48,56},{56,64},{64,7... | collective-permute-start | bytes 786440 | tf_op jit(solution)/shard_map/ppermute | solution.py:591
  104.5 3.5 %collective-permute-done.6 = f32[32,2048]{1,0:T(8,128)S(1)} collective-permute-done((f32[32,2048]{1,0:T(8,128)S(1)}, f32[32,2048]{1,0:T(8,128)S(1)}, u32[]{:S(2)}, u32[]{:S(2)}) %collective-permute-start.6) | collective-permute-done | bytes 262176 | tf_op jit(solution)/shard_map/ppermute | solution.py:590
  108.0 4.0 %collective-permute-done.7 = f32[32,2048]{1,0:T(8,128)S(1)} collective-permute-done((f32[32,2048]{1,0:T(8,128)S(1)}, f32[32,2048]{1,0:T(8,128)S(1)}, u32[]{:S(2)}, u32[]{:S(2)}) %collective-permute-start.7) | collective-permute-done | bytes 262176 | tf_op jit(solution)/shard_map/ppermute | solution.py:591
  112.0 0.8 fusion.3
  (18 shorter events, 0.1 us)
Async XLA Ops:
  0.0 23.9 %collective-permute-start = (f32[32,2048]{1,0:T(8,128)}, f32[32,2048]{1,0:T(8,128)S(1)}, u32[]{:S(2)}, u32[]{:S(2)}) collective-permute-start(f32[32,2048]{1,0:T(8,128)} %param.23), channel_id=1, source_target_pairs={{0,8},{8,16},{16,24},{24,32},{32,40},{40,48},{48,56},{56,64},{64,7... | collective-permute-start | bytes 786440 | tf_op jit(solution)/shard_map/ppermute | solution.py:577
  3.5 20.5 %collective-permute-start.1 = (f32[32,2048]{1,0:T(8,128)}, f32[32,2048]{1,0:T(8,128)S(1)}, u32[]{:S(2)}, u32[]{:S(2)}) collective-permute-start(f32[32,2048]{1,0:T(8,128)} %param.23), channel_id=1, source_target_pairs={{8,0},{16,8},{24,16},{32,24},{40,32},{48,40},{56,48},{64,56},{72,6... | collective-permute-start | bytes 786440 | tf_op jit(solution)/shard_map/ppermute | solution.py:578
  8.6 3.4 %copy-start = (f32[8,64,4096]{2,1,0:T(8,128)S(1)}, f32[8,64,4096]{2,1,0:T(8,128)}, u32[]{:S(2)}) copy-start(f32[8,64,4096]{2,1,0:T(8,128)} %psf_hbm.3) | copy-start | bytes 25165828
  12.0 0.9 copy-start.1
  12.9 0.9 copy-start.2
  13.8 0.9 copy-start.3
  14.7 0.7 copy-start.4
  15.4 8.6 %copy-start.18 = (f32[32,2048]{1,0:T(8,128)S(1)}, f32[32,2048]{1,0:T(8,128)}, u32[]{:S(2)}) copy-start(f32[32,2048]{1,0:T(8,128)} %param.23) | copy-start | bytes 786436
  24.0 17.4 %collective-permute-start.2 = (f32[96,2048]{1,0:T(8,128)S(1)}, f32[96,2048]{1,0:T(8,128)S(1)}, u32[]{:S(2)}, u32[]{:S(2)}) collective-permute-start(f32[96,2048]{1,0:T(8,128)S(1)} %constant_dynamic-update-slice_fusion.own_ref), channel_id=1, source_target_pairs={{0,1},{1,2},{2,3},{3,4},{4,5},{5,6},{6,7},{8,9},{9,10},{10,11},{11... | collective-permute-start | bytes 2359304 | tf_op jit(solution)/shard_map/ppermute | solution.py:580
  26.0 15.5 %collective-permute-start.3 = (f32[96,2048]{1,0:T(8,128)S(1)}, f32[96,2048]{1,0:T(8,128)S(1)}, u32[]{:S(2)}, u32[]{:S(2)}) collective-permute-start(f32[96,2048]{1,0:T(8,128)S(1)} %constant_dynamic-update-slice_fusion.own_ref), channel_id=1, source_target_pairs={{1,0},{2,1},{3,2},{4,3},{5,4},{6,5},{7,6},{9,8},{10,9},{11,10},{12... | collective-permute-start | bytes 2359304 | tf_op jit(solution)/shard_map/ppermute | solution.py:581
  29.6 12.8 %copy-start.5 = (s32[1,1,8]{2,1,0:T(1,128)S(1)}, s32[1,1,8]{2,1,0:T(1,128)}, u32[]{:S(2)}) copy-start(s32[1,1,8]{2,1,0:T(1,128)} %param.26) | copy-start | bytes 100
  29.6 12.8 %copy-start.6 = (bf16[768,256]{1,0:T(8,128)(2,1)S(1)}, bf16[768,256]{1,0:T(8,128)(2,1)}, u32[]{:S(2)}) copy-start(bf16[768,256]{1,0:T(8,128)(2,1)} %constant.33.clone.wxf_ref) | copy-start | bytes 1179652
  29.7 12.8 %copy-start.7 = (bf16[384,512]{1,0:T(8,128)(2,1)S(1)}, bf16[384,512]{1,0:T(8,128)(2,1)}, u32[]{:S(2)}) copy-start(bf16[384,512]{1,0:T(8,128)(2,1)} %constant.37.clone.wxe_ref) | copy-start | bytes 1179652
  29.7 12.8 %copy-start.8 = (bf16[192,768]{1,0:T(8,128)(2,1)S(1)}, bf16[192,768]{1,0:T(8,128)(2,1)}, u32[]{:S(2)}) copy-start(bf16[192,768]{1,0:T(8,128)(2,1)} %constant.40.clone.wxo_ref) | copy-start | bytes 884740
  29.7 12.8 %copy-start.9 = (bf16[192,576]{1,0:T(8,128)(2,1)S(1)}, bf16[192,576]{1,0:T(8,128)(2,1)}, u32[]{:S(2)}) copy-start(bf16[192,576]{1,0:T(8,128)(2,1)} %constant.34.clone.wyf_ref) | copy-start | bytes 663556
  29.7 12.8 %copy-start.10 = (bf16[192,576]{1,0:T(8,128)(2,1)S(1)}, bf16[192,576]{1,0:T(8,128)(2,1)}, u32[]{:S(2)}) copy-start(bf16[192,576]{1,0:T(8,128)(2,1)} %constant.39.clone.wyo_ref) | copy-start | bytes 663556
  29.7 12.8 %copy-start.11 = (bf16[768,128]{1,0:T(8,128)(2,1)S(1)}, bf16[768,128]{1,0:T(8,128)(2,1)}, u32[]{:S(2)}) copy-start(bf16[768,128]{1,0:T(8,128)(2,1)} %constant.32.clone.wzi_ref) | copy-start | bytes 589828
  29.7 12.8 %copy-start.12 = (bf16[384,256]{1,0:T(8,128)(2,1)S(1)}, bf16[384,256]{1,0:T(8,128)(2,1)}, u32[]{:S(2)}) copy-start(bf16[384,256]{1,0:T(8,128)(2,1)} %constant.31.clone.wz_ref) | copy-start | bytes 589828
  29.7 12.8 %copy-start.13 = (bf16[128,512]{1,0:T(8,128)(2,1)S(1)}, bf16[128,512]{1,0:T(8,128)(2,1)}, u32[]{:S(2)}) copy-start(bf16[128,512]{1,0:T(8,128)(2,1)} %constant.36.clone.wxi_ref) | copy-start | bytes 393220
  29.7 12.8 %copy-start.14 = (bf16[128,384]{1,0:T(8,128)(2,1)S(1)}, bf16[128,384]{1,0:T(8,128)(2,1)}, u32[]{:S(2)}) copy-start(bf16[128,384]{1,0:T(8,128)(2,1)} %constant.35.clone.wyi_ref) | copy-start | bytes 294916
  29.8 12.8 %copy-start.15 = (bf16[192,192]{1,0:T(8,128)(2,1)S(1)}, bf16[192,192]{1,0:T(8,128)(2,1)}, u32[]{:S(2)}) copy-start(bf16[192,192]{1,0:T(8,128)(2,1)} %constant.38.clone.wye_ref) | copy-start | bytes 221188
  41.5 0.9 copy-start.19
  83.1 11.4 %collective-permute-start.4 = (f32[96,2048]{1,0:T(8,128)S(1)}, f32[96,2048]{1,0:T(8,128)S(1)}, u32[]{:S(2)}, u32[]{:S(2)}) collective-permute-start(f32[96,2048]{1,0:T(8,128)S(1)} %get-tuple-element.11), channel_id=1, source_target_pairs={{1,0},{2,1},{3,2},{4,3},{5,4},{6,5},{7,6},{9,8},{10,9},{11,10},{12... | collective-permute-start | bytes 2359304 | tf_op jit(solution)/shard_map/ppermute | solution.py:585
  85.1 13.3 %collective-permute-start.5 = (f32[96,2048]{1,0:T(8,128)S(1)}, f32[96,2048]{1,0:T(8,128)S(1)}, u32[]{:S(2)}, u32[]{:S(2)}) collective-permute-start(f32[96,2048]{1,0:T(8,128)S(1)} %get-tuple-element.12), channel_id=1, source_target_pairs={{0,1},{1,2},{2,3},{3,4},{4,5},{5,6},{6,7},{8,9},{9,10},{10,11},{11... | collective-permute-start | bytes 2359304 | tf_op jit(solution)/shard_map/ppermute | solution.py:586
  87.5 1.2 %copy-start.16 = (f32[1728,128]{1,0:T(8,128)S(1)}, f32[1728,128]{1,0:T(8,128)}, u32[]{:S(2)}) copy-start(f32[1728,128]{1,0:T(8,128)} %get-tuple-element.9.real) | copy-start | bytes 2654212
  88.7 1.2 %copy-start.17 = (f32[1728,128]{1,0:T(8,128)S(1)}, f32[1728,128]{1,0:T(8,128)}, u32[]{:S(2)}) copy-start(f32[1728,128]{1,0:T(8,128)} %get-tuple-element.10.imag) | copy-start | bytes 2654212
  98.6 9.4 %collective-permute-start.6 = (f32[32,2048]{1,0:T(8,128)S(1)}, f32[32,2048]{1,0:T(8,128)S(1)}, u32[]{:S(2)}, u32[]{:S(2)}) collective-permute-start(f32[32,2048]{1,0:T(8,128)S(1)} %get-tuple-element.13), channel_id=1, source_target_pairs={{8,0},{16,8},{24,16},{32,24},{40,32},{48,40},{56,48},{64,56},{72,6... | collective-permute-start | bytes 786440 | tf_op jit(solution)/shard_map/ppermute | solution.py:590
  100.5 11.5 %collective-permute-start.7 = (f32[32,2048]{1,0:T(8,128)S(1)}, f32[32,2048]{1,0:T(8,128)S(1)}, u32[]{:S(2)}, u32[]{:S(2)}) collective-permute-start(f32[32,2048]{1,0:T(8,128)S(1)} %get-tuple-element.14), channel_id=1, source_target_pairs={{0,8},{8,16},{16,24},{24,32},{32,40},{40,48},{48,56},{56,64},{64,7... | collective-permute-start | bytes 786440 | tf_op jit(solution)/shard_map/ppermute | solution.py:591

commit v5 on v4

--- a/solution.py
+++ b/solution.py
@@ -27,9 +27,6 @@
 BIGPITCH = PY + 4
 WX = BX + K
 MIB = 1024 * 1024
-OTF_LIMIT = 32 * MIB
-MAIN_LIMIT = 48 * MIB
-TAIL_LIMIT = 16 * MIB
 
 F32 = jnp.float32
 BF16 = jnp.bfloat16
@@ -238,8 +235,20 @@
     return out[:table.shape[0] // 2] + out[table.shape[0] // 2:] if tall else out
 
 
-def otf_kernel(begin, end, count_ref, ids_ref, psf_hbm, wz_ref, wx_ref, wy_ref, *rest):
-    out_hbm, psf, out, real, imag, stash0, stash1, psf_sem, out_sem = rest[-9:]
+def table_copies(sources, targets, sems):
+    return [
+        pltpu.make_async_copy(source, target, sems.at[at])
+        for at, (source, target) in enumerate(zip(sources, targets))
+    ]
+
+
+def room_for(tables):
+    return [pltpu.VMEM(t.shape, BF16) for t in tables]
+
+
+def otf_kernel(begin, end, count_ref, ids_ref, psf_hbm, wz_hbm, wx_hbm, wy_hbm, *rest):
+    out_hbm, psf, out, real, imag, stash0, stash1, *rest = rest[-13:]
+    wz_ref, wx_ref, wy_ref, psf_sem, out_sem, table_sem = rest
     steps = KZ // (2 * UY)
 
     def fetch(step):
@@ -249,7 +258,7 @@
         )
 
     def store(step, j):
-        where = pl.ds(j * 2 * UY, 2 * UY)
+        where = pl.ds(j * UY, UY)
         return pltpu.make_async_copy(
             out.at[where], out_hbm.at[begin + step, where], out_sem.at[j]
         )
@@ -260,6 +269,12 @@
     def _():
         fetch(0).start()
 
+    tables = table_copies((wz_hbm, wx_hbm, wy_hbm), (wz_ref, wx_ref, wy_ref), table_sem)
+    for copy in tables:
+        copy.start()
+    for copy in tables:
+        copy.wait()
+
     def body(step, carry):
         buffer = lax.rem(step, 2)
         fetch(step).wait()
@@ -276,14 +291,17 @@
         def y(j):
             @pl.when(step > 0)
             def _():
-                store(step - 1, j).wait()
+                store(step - 1, 2 * j).wait()
+                store(step - 1, 2 * j + 1).wait()
 
             for pair in range(UY):
                 kz = (j * UY + pair) * 2
                 for at, value in enumerate(y_from_rows(wy_ref[...], real, imag, kz, K)):
                     out[kz + at, 0] = value[0]
                     out[kz + at, 1] = value[1]
-            store(step, j).start()
+                if pair == UY // 2 - 1:
+                    store(step, 2 * j).start()
+            store(step, 2 * j + 1).start()
 
         loop(steps, y)
         return carry
@@ -292,14 +310,17 @@
 
     @pl.when(slots > 0)
     def _():
-        for j in range(steps):
+        for j in range(2 * steps):
             store(slots - 1, j).wait()
 
 
 ZPO = 16
 ZPF = 8
 ZPE = 8
-UX = 2
+UX = 4
+OTF_LIMITS = (60 * MIB, 60 * MIB)
+MAIN_LIMIT = 48 * MIB
+TAIL_LIMIT = 16 * MIB
 UY = 12
 UP = 12
 UG = 12
@@ -472,7 +493,7 @@
 def otf_call(count, ids, psf, begin, end, held=None):
     tables = (z_forward(-HALF), x_forward(K, -HALF, K), y_forward(K, -HALF))
     inputs = [count, ids, psf] + [jnp.asarray(t) for t in tables]
-    specs = [IN_SMEM, IN_SMEM, ANYWHERE] + [IN_VMEM] * len(tables)
+    specs = [IN_SMEM, IN_SMEM, ANYWHERE] + [ANYWHERE] * len(tables)
     aliases = {}
     if held is not None:
         aliases = {len(inputs): 0}
@@ -490,11 +511,13 @@
             pltpu.VMEM((K * KPITCH, LANES), F32),
             pltpu.VMEM((ZPO * 2 * KZ, 3 * LANES), BF16),
             pltpu.VMEM((ZPO * 2 * KZ, 3 * LANES), BF16),
+        ] + room_for(tables) + [
             pltpu.SemaphoreType.DMA((2,)),
-            pltpu.SemaphoreType.DMA((KZ // (2 * UY),)),
+            pltpu.SemaphoreType.DMA((2 * KZ // (2 * UY),)),
+            pltpu.SemaphoreType.DMA((len(tables),)),
         ],
         input_output_aliases=aliases,
-        compiler_params=pltpu.CompilerParams(vmem_limit_bytes=OTF_LIMIT),
+        compiler_params=pltpu.CompilerParams(vmem_limit_bytes=OTF_LIMITS[0 if held is None else 1]),
         cost_estimate=pl.CostEstimate(
             flops=4 * 10**9 * (end - begin), bytes_accessed=6 * 10**6 * (end - begin), transcendentals=0
         ),

time: 114 us -> 107 us (0.939)
  the two profiles are of different devices: /device:TPU:66 before, /device:TPU:70 now
where the time goes in v5:
time: 107 us; the launch traced here: 106 us
  starting transfers between devices  52.8 us (49%)
  Pallas kernels  28.4 us (27%)
  waiting for transfers between devices  20.7 us (19%)
  local copies, waits for them, and re-layouts  2.51 us (2%)
    ppermute x1, starting transfers between devices, per_device(): lax.ppermute(sums[:BX], 'bx', down_x)  22.9 us
    pallas_call x1, Pallas kernels, main_call(): pl.pallas_call(main_kernel, out_shape=[jax.ShapeDtypeStruct(WIDE, F32)] *...  18.3 us
    ppermute x1, starting transfers between devices, per_device(): from_right = lax.ppermute(left_sum, 'by', down_y)  9.17 us
    pallas_call x2, Pallas kernels, otf_call(): pl.pallas_call(functools.partial(otf_kernel, begin, end), out_shape=jax.S...  8.49 us
    ppermute x1, waiting for transfers between devices, per_device(): lax.ppermute(sums[2 * BX:], 'bx', up_x)  6.51 us
    ppermute x1, waiting for transfers between devices, per_device(): left = lax.ppermute(own, 'by', up_y)  5.32 us
    ppermute x1, starting transfers between devices, per_device(): after = lax.ppermute(estimate, 'bx', down_x)  4.47 us
    ppermute x1, starting transfers between devices, per_device(): from_left = lax.ppermute(right_sum, 'by', up_y)  4.39 us
  transfers between devices with their start and end apart: 8, of which 6 were waited for; matrix products, arithmetic and copies ran while one was open for 0% of the time, Pallas kernels for 10%

profile of v5, /device:TPU:70, one launch (start us, length us, event | category | flops | bytes accessed | tf_op | source)
XLA Modules:
  0.0 106.3 jit_solution(17989069363197385519)
XLA Ops:
  0.0 3.6 %collective-permute-start = (f32[32,2048]{1,0:T(8,128)}, f32[32,2048]{1,0:T(8,128)S(1)}, u32[]{:S(2)}, u32[]{:S(2)}) collective-permute-start(f32[32,2048]{1,0:T(8,128)} %param.23), channel_id=1, source_target_pairs={{0,8},{8,16},{16,24},{24,32},{32,40},{40,48},{48,56},{56,64},{64,7... | collective-permute-start | bytes 786440 | tf_op jit(solution)/shard_map/ppermute | solution.py:600
  3.6 4.5 %collective-permute-start.1 = (f32[32,2048]{1,0:T(8,128)}, f32[32,2048]{1,0:T(8,128)S(1)}, u32[]{:S(2)}, u32[]{:S(2)}) collective-permute-start(f32[32,2048]{1,0:T(8,128)} %param.23), channel_id=1, source_target_pairs={{8,0},{16,8},{24,16},{32,24},{40,32},{48,40},{56,48},{64,56},{72,6... | collective-permute-start | bytes 786440 | tf_op jit(solution)/shard_map/ppermute | solution.py:601
  8.7 6.5 %otf.2.rest_0_ = f32[5,48,2,96,128]{4,3,2,1,0:T(8,128)} custom-call(s32[1]{0:T(128)} %bitcast.3.count_ref, s32[8]{0:T(128)} %bitcast.7, f32[8,64,4096]{2,1,0:T(8,128)} %psf_hbm.3, bf16[384,256]{1,0:T(8,128)(2,1)} %constant.28.clone.wz_hbm, bf16[384,256]{1,0:T(8,128)(2,1)} %constant.29.clone.wx_hbm, bf16[192,384]{1,0:T(8,128)(2,1)} %constant.30.clone.wy_hbm), custom_call_target="tpu_custom_call" | custom-call | flops 8000000000 | bytes 12000000 | tf_op jit(solution)/shard_map/otf/pallas_call | solution.py:502
  15.3 0.0 collective-permute-done
  15.3 0.0 copy-done.13
  15.3 0.0 collective-permute-done.1
  15.4 4.4 %collective-permute-start.2 = (f32[96,2048]{1,0:T(8,128)S(1)}, f32[96,2048]{1,0:T(8,128)S(1)}, u32[]{:S(2)}, u32[]{:S(2)}) collective-permute-start(f32[96,2048]{1,0:T(8,128)S(1)} %constant_dynamic-update-slice_fusion.own_ref), channel_id=1, source_target_pairs={{0,1},{1,2},{2,3},{3,4},{4,5},{5,6},{6,7},{8,9},{9,10},{10,11},{11... | collective-permute-start | bytes 2359304 | tf_op jit(solution)/shard_map/ppermute | solution.py:603
  19.8 1.9 %collective-permute-start.3 = (f32[96,2048]{1,0:T(8,128)S(1)}, f32[96,2048]{1,0:T(8,128)}, u32[]{:S(2)}, u32[]{:S(2)}) collective-permute-start(f32[96,2048]{1,0:T(8,128)S(1)} %constant_dynamic-update-slice_fusion.own_ref), channel_id=1, source_target_pairs={{1,0},{2,1},{3,2},{4,3},{5,4},{6,5},{7,6},{9,8},{10,9},{11,10},{12... | collective-permute-start | bytes 2359304 | tf_op jit(solution)/shard_map/ppermute | solution.py:604
  21.7 0.0 copy-start
  21.7 0.0 copy-start.1
  21.7 0.0 copy-start.2
  21.7 0.0 copy-start.3
  21.7 0.0 copy-start.4
  21.7 0.0 copy-start.5
  21.8 0.0 copy-start.6
  21.8 0.0 copy-start.7
  21.8 0.0 copy-start.8
  21.8 0.0 copy-start.9
  21.8 0.0 copy-start.10
  21.8 2.0 %otf.3.otf_hbm = f32[5,48,2,96,128]{4,3,2,1,0:T(8,128)} custom-call(s32[1]{0:T(128)} %bitcast.4.count_ref, s32[8]{0:T(128)} %bitcast.8, f32[8,64,4096]{2,1,0:T(8,128)} %psf_hbm.3, bf16[384,256]{1,0:T(8,128)(2,1)} %constant.28.clone.wz_hbm, bf16[384,256]{1,0:T(8,128)(2,1)} %constant.29.clone.wx_hbm, ...), custom_call_target="tpu_custom_call", output_to_operand_aliasing={{}: (6, {})} | custom-call | flops 12000000000 | bytes 18000000 | tf_op jit(solution)/shard_map/otf/pallas_call | solution.py:502
  23.8 5.3 %collective-permute-done.2.left_ref = f32[96,2048]{1,0:T(8,128)S(1)} collective-permute-done((f32[96,2048]{1,0:T(8,128)S(1)}, f32[96,2048]{1,0:T(8,128)S(1)}, u32[]{:S(2)}, u32[]{:S(2)}) %collective-permute-start.2) | collective-permute-done | bytes 786464 | tf_op jit(solution)/shard_map/ppermute | solution.py:603
  29.1 2.0 %collective-permute-done.3.right_ref = f32[96,2048]{1,0:T(8,128)} collective-permute-done((f32[96,2048]{1,0:T(8,128)S(1)}, f32[96,2048]{1,0:T(8,128)}, u32[]{:S(2)}, u32[]{:S(2)}) %collective-permute-start.3) | collective-permute-done | bytes 786464 | tf_op jit(solution)/shard_map/ppermute | solution.py:604
  31.2 0.0 copy-done
  31.2 0.0 copy-done.1
  31.2 0.0 copy-done.2
  31.2 0.0 copy-done.4
  31.2 0.0 copy-done.5
  31.2 0.0 copy-done.6
  31.2 0.0 copy-done.7
  31.2 0.0 copy-done.8
  31.2 0.0 copy-done.9
  31.2 0.0 copy-done.10
  31.3 0.0 copy-start.14
  31.3 18.3 %views.1 = (f32[96,2048]{1,0:T(8,128)S(1)}, f32[96,2048]{1,0:T(8,128)S(1)}, f32[1728,128]{1,0:T(8,128)}, f32[1728,128]{1,0:T(8,128)}) custom-call(s32[1]{0:T(128)} %bitcast.5.count_ref, s32[8]{0:T(128)S(1)} %bitcast.9, f32[96,2048]{1,0:T(8,128)S(1)} %collective-permute-done.2.left_ref, f32[96,2048]{1,0:T(8,128)S(1)} %constant_dynamic-update-slice_fusion.own_ref, ...), custom_call_target="tpu_custom_call" | custom-call | flops 30000001024 | bytes 40000000 | tf_op jit(solution)/shard_map/views/pallas_call | solution.py:542
  49.5 9.2 %collective-permute-start.4 = (f32[96,2048]{1,0:T(8,128)S(1)}, f32[96,2048]{1,0:T(8,128)S(1)}, u32[]{:S(2)}, u32[]{:S(2)}) collective-permute-start(f32[96,2048]{1,0:T(8,128)S(1)} %get-tuple-element.11), channel_id=1, source_target_pairs={{1,0},{2,1},{3,2},{4,3},{5,4},{6,5},{7,6},{9,8},{10,9},{11,10},{12... | collective-permute-start | bytes 2359304 | tf_op jit(solution)/shard_map/ppermute | solution.py:608
  58.7 4.4 %collective-permute-start.5 = (f32[96,2048]{1,0:T(8,128)S(1)}, f32[96,2048]{1,0:T(8,128)S(1)}, u32[]{:S(2)}, u32[]{:S(2)}) collective-permute-start(f32[96,2048]{1,0:T(8,128)S(1)} %get-tuple-element.12), channel_id=1, source_target_pairs={{0,1},{1,2},{2,3},{3,4},{4,5},{5,6},{6,7},{8,9},{9,10},{10,11},{11... | collective-permute-start | bytes 2359304 | tf_op jit(solution)/shard_map/ppermute | solution.py:609
  63.1 0.0 copy-start.11
  63.1 1.2 %copy-done.11 = f32[1728,128]{1,0:T(8,128)S(1)} copy-done((f32[1728,128]{1,0:T(8,128)S(1)}, f32[1728,128]{1,0:T(8,128)}, u32[]{:S(2)}) %copy-start.11) | copy-done | bytes 884760
  64.3 1.2 %copy-done.12 = f32[1728,128]{1,0:T(8,128)S(1)} copy-done((f32[1728,128]{1,0:T(8,128)S(1)}, f32[1728,128]{1,0:T(8,128)}, u32[]{:S(2)}) %copy-start.12) | copy-done | bytes 884760
  65.4 1.7 %tail.1 = f32[96,2048]{1,0:T(8,128)S(1)} custom-call(f32[1728,128]{1,0:T(8,128)S(1)} %copy-done.11, f32[1728,128]{1,0:T(8,128)S(1)} %copy-done.12, bf16[768,128]{1,0:T(8,128)(2,1)S(1)} %copy-done.6, bf16[192,768]{1,0:T(8,128)(2,1)S(1)} %copy-done.3), custom_call_target="tpu_custom_call" | custom-call | flops 4000000000 | bytes 3000000 | tf_op jit(solution)/shard_map/tail/pallas_call | solution.py:576
  67.1 1.1 collective-permute-done.4
  68.2 3.8 %collective-permute-done.5 = f32[96,2048]{1,0:T(8,128)S(1)} collective-permute-done((f32[96,2048]{1,0:T(8,128)S(1)}, f32[96,2048]{1,0:T(8,128)S(1)}, u32[]{:S(2)}, u32[]{:S(2)}) %collective-permute-start.5) | collective-permute-done | bytes 786464 | tf_op jit(solution)/shard_map/ppermute | solution.py:609
  72.0 0.2 add_add_fusion
  72.2 22.9 %collective-permute-start.6 = (f32[32,2048]{1,0:T(8,128)S(1)}, f32[32,2048]{1,0:T(8,128)S(1)}, u32[]{:S(2)}, u32[]{:S(2)}) collective-permute-start(f32[32,2048]{1,0:T(8,128)S(1)} %get-tuple-element.13), channel_id=1, source_target_pairs={{8,0},{16,8},{24,16},{32,24},{40,32},{48,40},{56,48},{64,56},{72,6... | collective-permute-start | bytes 786440 | tf_op jit(solution)/shard_map/ppermute | solution.py:613
  95.2 1.9 %collective-permute-start.7 = (f32[32,2048]{1,0:T(8,128)S(1)}, f32[32,2048]{1,0:T(8,128)S(1)}, u32[]{:S(2)}, u32[]{:S(2)}) collective-permute-start(f32[32,2048]{1,0:T(8,128)S(1)} %get-tuple-element.14), channel_id=1, source_target_pairs={{0,8},{8,16},{16,24},{24,32},{32,40},{40,48},{48,56},{56,64},{64,7... | collective-permute-start | bytes 786440 | tf_op jit(solution)/shard_map/ppermute | solution.py:614
  97.1 1.9 %collective-permute-done.6 = f32[32,2048]{1,0:T(8,128)S(1)} collective-permute-done((f32[32,2048]{1,0:T(8,128)S(1)}, f32[32,2048]{1,0:T(8,128)S(1)}, u32[]{:S(2)}, u32[]{:S(2)}) %collective-permute-start.6) | collective-permute-done | bytes 262176 | tf_op jit(solution)/shard_map/ppermute | solution.py:613
  99.0 6.5 %collective-permute-done.7 = f32[32,2048]{1,0:T(8,128)S(1)} collective-permute-done((f32[32,2048]{1,0:T(8,128)S(1)}, f32[32,2048]{1,0:T(8,128)S(1)}, u32[]{:S(2)}, u32[]{:S(2)}) %collective-permute-start.7) | collective-permute-done | bytes 262176 | tf_op jit(solution)/shard_map/ppermute | solution.py:614
  105.5 0.8 fusion.3
  (8 shorter events, 0.1 us)
Async XLA Ops:
  0.0 15.3 %copy-start.13 = (f32[32,2048]{1,0:T(8,128)S(1)}, f32[32,2048]{1,0:T(8,128)}, u32[]{:S(2)}) copy-start(f32[32,2048]{1,0:T(8,128)} %param.23) | copy-start | bytes 786436
  0.0 15.3 %collective-permute-start = (f32[32,2048]{1,0:T(8,128)}, f32[32,2048]{1,0:T(8,128)S(1)}, u32[]{:S(2)}, u32[]{:S(2)}) collective-permute-start(f32[32,2048]{1,0:T(8,128)} %param.23), channel_id=1, source_target_pairs={{0,8},{8,16},{16,24},{24,32},{32,40},{40,48},{48,56},{56,64},{64,7... | collective-permute-start | bytes 786440 | tf_op jit(solution)/shard_map/ppermute | solution.py:600
  3.6 11.7 %collective-permute-start.1 = (f32[32,2048]{1,0:T(8,128)}, f32[32,2048]{1,0:T(8,128)S(1)}, u32[]{:S(2)}, u32[]{:S(2)}) collective-permute-start(f32[32,2048]{1,0:T(8,128)} %param.23), channel_id=1, source_target_pairs={{8,0},{16,8},{24,16},{32,24},{40,32},{48,40},{56,48},{64,56},{72,6... | collective-permute-start | bytes 786440 | tf_op jit(solution)/shard_map/ppermute | solution.py:601
  15.4 13.8 %collective-permute-start.2 = (f32[96,2048]{1,0:T(8,128)S(1)}, f32[96,2048]{1,0:T(8,128)S(1)}, u32[]{:S(2)}, u32[]{:S(2)}) collective-permute-start(f32[96,2048]{1,0:T(8,128)S(1)} %constant_dynamic-update-slice_fusion.own_ref), channel_id=1, source_target_pairs={{0,1},{1,2},{2,3},{3,4},{4,5},{5,6},{6,7},{8,9},{9,10},{10,11},{11... | collective-permute-start | bytes 2359304 | tf_op jit(solution)/shard_map/ppermute | solution.py:603
  19.8 11.4 %collective-permute-start.3 = (f32[96,2048]{1,0:T(8,128)S(1)}, f32[96,2048]{1,0:T(8,128)}, u32[]{:S(2)}, u32[]{:S(2)}) collective-permute-start(f32[96,2048]{1,0:T(8,128)S(1)} %constant_dynamic-update-slice_fusion.own_ref), channel_id=1, source_target_pairs={{1,0},{2,1},{3,2},{4,3},{5,4},{6,5},{7,6},{9,8},{10,9},{11,10},{12... | collective-permute-start | bytes 2359304 | tf_op jit(solution)/shard_map/ppermute | solution.py:604
  21.7 9.5 %copy-start = (s32[1,1,8]{2,1,0:T(1,128)S(1)}, s32[1,1,8]{2,1,0:T(1,128)}, u32[]{:S(2)}) copy-start(s32[1,1,8]{2,1,0:T(1,128)} %param.26) | copy-start | bytes 100
  21.7 9.5 %copy-start.1 = (bf16[768,256]{1,0:T(8,128)(2,1)S(1)}, bf16[768,256]{1,0:T(8,128)(2,1)}, u32[]{:S(2)}) copy-start(bf16[768,256]{1,0:T(8,128)(2,1)} %constant.33.clone.wxf_ref) | copy-start | bytes 1179652
  21.7 9.5 %copy-start.2 = (bf16[384,512]{1,0:T(8,128)(2,1)S(1)}, bf16[384,512]{1,0:T(8,128)(2,1)}, u32[]{:S(2)}) copy-start(bf16[384,512]{1,0:T(8,128)(2,1)} %constant.37.clone.wxe_ref) | copy-start | bytes 1179652
  21.7 9.5 %copy-start.3 = (bf16[192,768]{1,0:T(8,128)(2,1)S(1)}, bf16[192,768]{1,0:T(8,128)(2,1)}, u32[]{:S(2)}) copy-start(bf16[192,768]{1,0:T(8,128)(2,1)} %constant.40.clone.wxo_ref) | copy-start | bytes 884740
  21.7 9.5 %copy-start.4 = (bf16[192,576]{1,0:T(8,128)(2,1)S(1)}, bf16[192,576]{1,0:T(8,128)(2,1)}, u32[]{:S(2)}) copy-start(bf16[192,576]{1,0:T(8,128)(2,1)} %constant.34.clone.wyf_ref) | copy-start | bytes 663556
  21.7 9.4 %copy-start.5 = (bf16[192,576]{1,0:T(8,128)(2,1)S(1)}, bf16[192,576]{1,0:T(8,128)(2,1)}, u32[]{:S(2)}) copy-start(bf16[192,576]{1,0:T(8,128)(2,1)} %constant.39.clone.wyo_ref) | copy-start | bytes 663556
  21.8 9.4 %copy-start.6 = (bf16[768,128]{1,0:T(8,128)(2,1)S(1)}, bf16[768,128]{1,0:T(8,128)(2,1)}, u32[]{:S(2)}) copy-start(bf16[768,128]{1,0:T(8,128)(2,1)} %constant.32.clone.wzi_ref) | copy-start | bytes 589828
  21.8 9.4 %copy-start.7 = (bf16[384,256]{1,0:T(8,128)(2,1)S(1)}, bf16[384,256]{1,0:T(8,128)(2,1)}, u32[]{:S(2)}) copy-start(bf16[384,256]{1,0:T(8,128)(2,1)} %constant.31.clone.wz_ref) | copy-start | bytes 589828
  21.8 9.4 %copy-start.8 = (bf16[128,512]{1,0:T(8,128)(2,1)S(1)}, bf16[128,512]{1,0:T(8,128)(2,1)}, u32[]{:S(2)}) copy-start(bf16[128,512]{1,0:T(8,128)(2,1)} %constant.36.clone.wxi_ref) | copy-start | bytes 393220
  21.8 9.4 %copy-start.9 = (bf16[128,384]{1,0:T(8,128)(2,1)S(1)}, bf16[128,384]{1,0:T(8,128)(2,1)}, u32[]{:S(2)}) copy-start(bf16[128,384]{1,0:T(8,128)(2,1)} %constant.35.clone.wyi_ref) | copy-start | bytes 294916
  21.8 9.4 %copy-start.10 = (bf16[192,192]{1,0:T(8,128)(2,1)S(1)}, bf16[192,192]{1,0:T(8,128)(2,1)}, u32[]{:S(2)}) copy-start(bf16[192,192]{1,0:T(8,128)(2,1)} %constant.38.clone.wye_ref) | copy-start | bytes 221188
  31.3 74.3 %copy-start.14 = (f32[32,2048]{1,0:T(8,128)S(1)}, f32[32,2048]{1,0:T(8,128)}, u32[]{:S(2)}) copy-start(f32[32,2048]{1,0:T(8,128)} %param.23) | copy-start | bytes 786436
  49.5 18.7 %collective-permute-start.4 = (f32[96,2048]{1,0:T(8,128)S(1)}, f32[96,2048]{1,0:T(8,128)S(1)}, u32[]{:S(2)}, u32[]{:S(2)}) collective-permute-start(f32[96,2048]{1,0:T(8,128)S(1)} %get-tuple-element.11), channel_id=1, source_target_pairs={{1,0},{2,1},{3,2},{4,3},{5,4},{6,5},{7,6},{9,8},{10,9},{11,10},{12... | collective-permute-start | bytes 2359304 | tf_op jit(solution)/shard_map/ppermute | solution.py:608
  58.7 13.3 %collective-permute-start.5 = (f32[96,2048]{1,0:T(8,128)S(1)}, f32[96,2048]{1,0:T(8,128)S(1)}, u32[]{:S(2)}, u32[]{:S(2)}) collective-permute-start(f32[96,2048]{1,0:T(8,128)S(1)} %get-tuple-element.12), channel_id=1, source_target_pairs={{0,1},{1,2},{2,3},{3,4},{4,5},{5,6},{6,7},{8,9},{9,10},{10,11},{11... | collective-permute-start | bytes 2359304 | tf_op jit(solution)/shard_map/ppermute | solution.py:609
  63.1 1.2 %copy-start.11 = (f32[1728,128]{1,0:T(8,128)S(1)}, f32[1728,128]{1,0:T(8,128)}, u32[]{:S(2)}) copy-start(f32[1728,128]{1,0:T(8,128)} %get-tuple-element.9.real) | copy-start | bytes 2654212
  64.3 1.2 %copy-start.12 = (f32[1728,128]{1,0:T(8,128)S(1)}, f32[1728,128]{1,0:T(8,128)}, u32[]{:S(2)}) copy-start(f32[1728,128]{1,0:T(8,128)} %get-tuple-element.10.imag) | copy-start | bytes 2654212
  72.2 26.8 %collective-permute-start.6 = (f32[32,2048]{1,0:T(8,128)S(1)}, f32[32,2048]{1,0:T(8,128)S(1)}, u32[]{:S(2)}, u32[]{:S(2)}) collective-permute-start(f32[32,2048]{1,0:T(8,128)S(1)} %get-tuple-element.13), channel_id=1, source_target_pairs={{8,0},{16,8},{24,16},{32,24},{40,32},{48,40},{56,48},{64,56},{72,6... | collective-permute-start | bytes 786440 | tf_op jit(solution)/shard_map/ppermute | solution.py:613
  95.2 10.4 %collective-permute-start.7 = (f32[32,2048]{1,0:T(8,128)S(1)}, f32[32,2048]{1,0:T(8,128)S(1)}, u32[]{:S(2)}, u32[]{:S(2)}) collective-permute-start(f32[32,2048]{1,0:T(8,128)S(1)} %get-tuple-element.14), channel_id=1, source_target_pairs={{0,8},{8,16},{16,24},{24,32},{32,40},{40,48},{48,56},{56,64},{64,7... | collective-permute-start | bytes 786440 | tf_op jit(solution)/shard_map/ppermute | solution.py:614

commit v6 on v5

--- a/solution.py
+++ b/solution.py
@@ -162,13 +162,13 @@
     return three(jnp.concatenate(groups, axis=0), 1)
 
 
-def x_stage(stash, wx, real_ref, imag_ref, first_pair, copies):
+def x_stage(stash, wx, real_ref, imag_ref, first_y, copies):
     across = dot(stash, wx)
     for at in range(stash.shape[0] // (2 * KZ)):
         piece = across[at * 2 * KZ:(at + 1) * 2 * KZ]
         for copy in range(copies):
             for y in range(2):
-                where = pl.ds((2 * (first_pair + at * copies + copy) + y) * KPITCH, KZ)
+                where = pl.ds((first_y + 2 * (at * copies + copy) + y) * KPITCH, KZ)
                 part = piece[y * KZ:(y + 1) * KZ]
                 real_ref[where, :] = part[:, (2 * copy) * LANES:(2 * copy + 1) * LANES]
                 imag_ref[where, :] = part[:, (2 * copy + 1) * LANES:(2 * copy + 2) * LANES]
@@ -182,7 +182,7 @@
         second(step, stash[step % 2])
 
 
-def z_then_x(read, count, wz, wx, real_ref, imag_ref, copies, stash):
+def z_then_x(read, count, wz, wx, real_ref, imag_ref, copies, stash, place=lambda pair: 2 * pair):
     pairs = stash[0].shape[0] // (2 * KZ) * copies
 
     def first(step, ref):
@@ -191,7 +191,7 @@
         ref[...] = z_stage(pieces, wz[...], copies)
 
     def second(step, ref):
-        x_stage(ref[...], wx[...], real_ref, imag_ref, step * pairs, copies)
+        x_stage(ref[...], wx[...], real_ref, imag_ref, place(step * pairs), copies)
 
     pipelined(count // pairs, first, second, stash)
 
@@ -350,9 +350,9 @@
 
 
 def main_kernel(
-    count_ref, ids_ref, left_ref, own_ref, right_ref, views_hbm, otf_hbm,
+    count_ref, ids_ref, odd_ref, own_ref, first_ref, second_ref, views_hbm, otf_hbm,
     wz_ref, wzi_ref, wxf_ref, wyf_ref, wyi_ref, wxi_ref, wxe_ref, wye_ref, wyo_ref, wxo_ref,
-    left_out, right_out, real_hbm, imag_hbm,
+    first_out, second_out, real_hbm, imag_hbm,
     field, total, big_real, big_imag, real, imag, lines, error, otf, image,
     wide0, wide1, thin0, thin1, last0, last1, otf_sem, image_sem, own_sem,
 ):
@@ -370,11 +370,19 @@
     for copy in fetch(0):
         copy.start()
 
+    odd = odd_ref[0]
+
     def read_window(pair, pairs):
         part, pair = divmod(pair, BY // 2)
-        return (left_ref, own_ref, right_ref)[part][:, columns(pair, pairs)]
-
-    z_then_x(read_window, PY // 2, wz_ref, wxf_ref, big_real, big_imag, 1, (wide0, wide1))
+        return (own_ref, first_ref, second_ref)[part][:, columns(pair, pairs)]
+
+    def place_window(pair):
+        part, pair = divmod(pair, BY // 2)
+        return (1, 2 - 2 * odd, 2 * odd)[part] * BY + 2 * pair
+
+    z_then_x(
+        read_window, PY // 2, wz_ref, wxf_ref, big_real, big_imag, 1, (wide0, wide1), place_window
+    )
 
     def field_y(j):
         for pair in range(UF):
@@ -468,7 +476,7 @@
         copy.start()
     chunks = [
         (big_real, big_imag, side * KZ * YPITCH + y, out, y // 2)
-        for side, out in enumerate((left_out, right_out))
+        for side, out in ((1 - odd, first_out), (odd, second_out))
         for y in range(0, BY, 8)
     ]
     final_sums(wxo_ref, wzi_ref, chunks, (last0, last1))
@@ -525,8 +533,8 @@
     )(*inputs)
 
 
-def main_call(count, ids, window, views, otf):
-    left, own, right = window
+def main_call(count, ids, odd, window, views, otf):
+    own, first, second = window
     tables = (
         z_forward(0),
         z_inverse(),
@@ -542,7 +550,7 @@
     return pl.pallas_call(
         main_kernel,
         out_shape=[jax.ShapeDtypeStruct(WIDE, F32)] * 2 + [jax.ShapeDtypeStruct(ROWS, F32)] * 2,
-        in_specs=[IN_SMEM] * 2 + [IN_VMEM] * 3 + [ANYWHERE] * 2 + [IN_VMEM] * len(tables),
+        in_specs=[IN_SMEM] * 3 + [IN_VMEM] * 3 + [ANYWHERE] * 2 + [IN_VMEM] * len(tables),
         out_specs=[IN_VMEM] * 2 + [ANYWHERE] * 2,
         scratch_shapes=[
             pltpu.VMEM(SPECTRUM, F32),
@@ -568,7 +576,7 @@
         compiler_params=pltpu.CompilerParams(vmem_limit_bytes=MAIN_LIMIT),
         cost_estimate=pl.CostEstimate(flops=30 * 10**9, bytes_accessed=40 * 10**6, transcendentals=0),
         name="views",
-    )(count, ids, left, own, right, views, otf, *[jnp.asarray(t) for t in tables])
+    )(count, ids, odd, own, first, second, views, otf, *[jnp.asarray(t) for t in tables])
 
 
 def tail_call(real, imag):
@@ -585,34 +593,35 @@
     )(real, imag, *[jnp.asarray(t) for t in tables])
 
 
-def shifts(axis):
+def swaps(axis):
     devices = lax.axis_size(axis)
-    up = [(i, i + 1) for i in range(devices - 1)]
-    down = [(i + 1, i) for i in range(devices - 1)]
-    return up, down
+    first = [(i, i ^ 1) for i in range(devices) if i ^ 1 < devices]
+    second = [(i, i + 1 if i % 2 else i - 1) for i in range(1, devices)]
+    second = [(i, j) for i, j in second if j < devices]
+    return lax.rem(lax.axis_index(axis), 2), first, second
 
 
 def per_device(estimate, views, psf, view_list, view_count):
     ids = view_list.reshape(V)
     count = view_count.reshape(1)
-    up_x, down_x = shifts("bx")
-    up_y, down_y = shifts("by")
-    before = lax.ppermute(estimate, "bx", up_x)
-    after = lax.ppermute(estimate, "bx", down_x)
+    odd_x, first_x, second_x = swaps("bx")
+    odd_y, first_y, second_y = swaps("by")
+    one = lax.ppermute(estimate, "bx", first_x)
+    other = lax.ppermute(estimate, "bx", second_x)
+    before = jnp.where(odd_x == 1, one, other)
+    after = jnp.where(odd_x == 1, other, one)
     own = jnp.concatenate([before, estimate, after], axis=0)
-    left = lax.ppermute(own, "by", up_y)
-    right = lax.ppermute(own, "by", down_y)
+    window = (own, lax.ppermute(own, "by", first_y), lax.ppermute(own, "by", second_y))
     otf = otf_call(count, ids, psf, 0, 2)
     otf = otf_call(count, ids, psf, 2, CMAX, otf)
-    left_sum, right_sum, real, imag = main_call(count, ids, (left, own, right), views, otf)
-    from_right = lax.ppermute(left_sum, "by", down_y)
-    from_left = lax.ppermute(right_sum, "by", up_y)
-    sums = tail_call(real, imag) + from_right + from_left
-    correction = (
-        sums[BX:2 * BX]
-        + lax.ppermute(sums[:BX], "bx", down_x)
-        + lax.ppermute(sums[2 * BX:], "bx", up_x)
-    )
+    rim, other_rim, real, imag = main_call(count, ids, odd_y.reshape(1), window, views, otf)
+    one = lax.ppermute(rim, "by", first_y)
+    other = lax.ppermute(other_rim, "by", second_y)
+    sums = tail_call(real, imag) + one + other
+    low, high = sums[:BX], sums[2 * BX:]
+    one = lax.ppermute(jnp.where(odd_x == 1, low, high), "bx", first_x)
+    other = lax.ppermute(jnp.where(odd_x == 1, high, low), "bx", second_x)
+    correction = sums[BX:2 * BX] + one + other
     return estimate * (1.0 + correction / count.astype(F32))
 
 

time: 107 us -> 100 us (0.935)
  the two profiles are of different devices: /device:TPU:70 before, /device:TPU:66 now
where the time goes in v6:
time: 100 us; the launch traced here: 98.3 us
  Pallas kernels  63.6 us (64%)
  waiting for transfers between devices  15.8 us (16%)
  starting transfers between devices  14.3 us (14%)
  local copies, waits for them, and re-layouts  2.41 us (2%)
  other arithmetic  1.08 us (1%)
  between operations  1 us (1%)
    pallas_call x1, Pallas kernels, main_call(): pl.pallas_call(main_kernel, out_shape=[jax.ShapeDtypeStruct(WIDE, F32)] *...  39.3 us
    pallas_call x2, Pallas kernels, otf_call(): pl.pallas_call(functools.partial(otf_kernel, begin, end), out_shape=jax.S...  22.7 us
    ppermute x1, waiting for transfers between devices, per_device(): other = lax.ppermute(other_rim, 'by', second_y)  7.17 us
    ppermute x1, waiting for transfers between devices, per_device(): one = lax.ppermute(jnp.where(odd_x == 1, low, high), 'bx', first_x)  4.43 us
    ppermute x1, waiting for transfers between devices, per_device(): other = lax.ppermute(jnp.where(odd_x == 1, high, low), 'bx', second_x)  4.23 us
    ppermute x1, starting transfers between devices, per_device(): other = lax.ppermute(estimate, 'bx', second_x)  4.05 us
    ppermute x1, starting transfers between devices, per_device(): other = lax.ppermute(jnp.where(odd_x == 1, high, low), 'bx', second_x)  3.73 us
    unnamed x30, local copies, waits for them, and re-layouts  2.41 us
  transfers between devices with their start and end apart: 8, of which 3 were waited for; matrix products, arithmetic and copies ran while one was open for 0% of the time, Pallas kernels for 25%

profile of v6, /device:TPU:66, one launch (start us, length us, event | category | flops | bytes accessed | tf_op | source)
XLA Modules:
  0.0 98.3 jit_solution(739074208200638771)
XLA Ops:
  0.0 1.6 %collective-permute-start = (f32[32,2048]{1,0:T(8,128)}, f32[32,2048]{1,0:T(8,128)S(1)}, u32[]{:S(2)}, u32[]{:S(2)}) collective-permute-start(f32[32,2048]{1,0:T(8,128)} %param.23), channel_id=1, source_target_pairs={{0,8},{8,0},{16,24},{24,16},{32,40},{40,32},{48,56},{56,48},{64,72... | collective-permute-start | bytes 786440 | tf_op jit(solution)/shard_map/ppermute | solution.py:609
  1.6 4.1 %collective-permute-start.1 = (f32[32,2048]{1,0:T(8,128)}, f32[32,2048]{1,0:T(8,128)S(1)}, u32[]{:S(2)}, u32[]{:S(2)}) collective-permute-start(f32[32,2048]{1,0:T(8,128)} %param.23), channel_id=1, source_target_pairs={{8,16},{16,8},{24,32},{32,24},{40,48},{48,40},{56,64},{64,56},{72,... | collective-permute-start | bytes 786440 | tf_op jit(solution)/shard_map/ppermute | solution.py:610
  6.3 9.7 %otf.2.rest_0_ = f32[5,48,2,96,128]{4,3,2,1,0:T(8,128)} custom-call(s32[1]{0:T(128)} %bitcast.4.count_ref, s32[8]{0:T(128)} %bitcast.8, f32[8,64,4096]{2,1,0:T(8,128)} %psf_hbm.3, bf16[384,256]{1,0:T(8,128)(2,1)} %constant.45.clone.wz_hbm, bf16[384,256]{1,0:T(8,128)(2,1)} %constant.46.clone.wx_hbm, bf16[192,384]{1,0:T(8,128)(2,1)} %constant.47.clone.wy_hbm), custom_call_target="tpu_custom_call" | custom-call | flops 8000000000 | bytes 12000000 | tf_op jit(solution)/shard_map/otf/pallas_call | solution.py:510
  16.0 0.0 collective-permute-done
  16.0 0.0 collective-permute-done.1
  16.1 0.0 copy-done.13
  16.1 0.1 pad_maximum_fusion.own_ref
  16.2 0.1 collective-permute-start.2
  16.3 2.1 %collective-permute-start.3 = (f32[96,2048]{1,0:T(8,128)S(1)}, f32[96,2048]{1,0:T(8,128)}, u32[]{:S(2)}, u32[]{:S(2)}) collective-permute-start(f32[96,2048]{1,0:T(8,128)S(1)} %pad_maximum_fusion.own_ref), channel_id=1, source_target_pairs={{1,2},{2,1},{3,4},{4,3},{5,6},{6,5},{9,10},{10,9},{11,12},{12,11},... | collective-permute-start | bytes 2359304 | tf_op jit(solution)/shard_map/ppermute | solution.py:614
  18.4 0.0 copy-start
  18.4 0.0 copy-start.1
  18.4 0.0 copy-start.2
  18.4 0.0 copy-start.3
  18.4 0.0 copy-start.4
  18.4 0.0 copy-start.5
  18.5 0.0 copy-start.6
  18.5 0.0 copy-start.7
  18.5 0.0 copy-start.8
  18.5 0.0 copy-start.9
  18.5 0.0 copy-start.10
  18.5 12.9 %otf.3.otf_hbm = f32[5,48,2,96,128]{4,3,2,1,0:T(8,128)} custom-call(s32[1]{0:T(128)} %bitcast.5.count_ref, s32[8]{0:T(128)} %bitcast.9, f32[8,64,4096]{2,1,0:T(8,128)} %psf_hbm.3, bf16[384,256]{1,0:T(8,128)(2,1)} %constant.45.clone.wz_hbm, bf16[384,256]{1,0:T(8,128)(2,1)} %constant.46.clone.wx_hbm, ...), custom_call_target="tpu_custom_call", output_to_operand_aliasing={{}: (6, {})} | custom-call | flops 12000000000 | bytes 18000000 | tf_op jit(solution)/shard_map/otf/pallas_call | solution.py:510
  31.5 0.0 collective-permute-done.2.first_ref
  31.5 0.0 collective-permute-done.3.second_ref
  31.5 0.0 copy-done
  31.5 0.0 copy-done.1
  31.5 0.0 copy-done.2
  31.5 0.0 copy-done.3
  31.5 0.0 copy-done.4
  31.5 0.0 copy-done.5
  31.5 0.0 copy-done.6
  31.6 0.0 copy-done.7
  31.6 0.0 copy-done.8
  31.6 0.0 copy-done.9
  31.6 0.0 copy-start.14
  31.6 39.3 %views.1 = (f32[96,2048]{1,0:T(8,128)S(1)}, f32[96,2048]{1,0:T(8,128)S(1)}, f32[1728,128]{1,0:T(8,128)}, f32[1728,128]{1,0:T(8,128)}) custom-call(s32[1]{0:T(128)} %bitcast.6.count_ref, s32[8]{0:T(128)S(1)} %bitcast.10, s32[1]{0:T(128)} %bitcast.2.odd_ref, f32[96,2048]{1,0:T(8,128)S(1)} %pad_maximum_fusion.own_ref, ...), custom_call_target="tpu_custom_call" | custom-call | flops 30000001024 | bytes 40000000 | tf_op jit(solution)/shard_map/views/pallas_call | solution.py:550
  70.9 0.1 collective-permute-start.4
  71.0 2.1 %collective-permute-start.5 = (f32[96,2048]{1,0:T(8,128)S(1)}, f32[96,2048]{1,0:T(8,128)S(1)}, u32[]{:S(2)}, u32[]{:S(2)}) collective-permute-start(f32[96,2048]{1,0:T(8,128)S(1)} %get-tuple-element.12), channel_id=1, source_target_pairs={{1,2},{2,1},{3,4},{4,3},{5,6},{6,5},{9,10},{10,9},{11,12},{12,11},... | collective-permute-start | bytes 2359304 | tf_op jit(solution)/shard_map/ppermute | solution.py:619
  73.1 1.2 %copy-done.11 = f32[1728,128]{1,0:T(8,128)S(1)} copy-done((f32[1728,128]{1,0:T(8,128)S(1)}, f32[1728,128]{1,0:T(8,128)}, u32[]{:S(2)}) %copy-start.11) | copy-done | bytes 884760
  74.2 1.2 %copy-done.12 = f32[1728,128]{1,0:T(8,128)S(1)} copy-done((f32[1728,128]{1,0:T(8,128)S(1)}, f32[1728,128]{1,0:T(8,128)}, u32[]{:S(2)}) %copy-start.12) | copy-done | bytes 884760
  75.4 1.7 %tail.1 = f32[96,2048]{1,0:T(8,128)S(1)} custom-call(f32[1728,128]{1,0:T(8,128)S(1)} %copy-done.11, f32[1728,128]{1,0:T(8,128)S(1)} %copy-done.12, bf16[768,128]{1,0:T(8,128)(2,1)S(1)} %copy-done.6, bf16[192,768]{1,0:T(8,128)(2,1)S(1)} %copy-done.3), custom_call_target="tpu_custom_call" | custom-call | flops 4000000000 | bytes 3000000 | tf_op jit(solution)/shard_map/tail/pallas_call | solution.py:584
  77.1 0.0 collective-permute-done.4
  77.1 7.2 %collective-permute-done.5 = f32[96,2048]{1,0:T(8,128)S(1)} collective-permute-done((f32[96,2048]{1,0:T(8,128)S(1)}, f32[96,2048]{1,0:T(8,128)S(1)}, u32[]{:S(2)}, u32[]{:S(2)}) %collective-permute-start.5) | collective-permute-done | bytes 786464 | tf_op jit(solution)/shard_map/ppermute | solution.py:619
  84.3 0.2 add_add_fusion
  84.5 0.6 collective-permute-start.6
  85.1 3.7 %collective-permute-start.7 = (f32[32,2048]{1,0:T(8,128)S(1)}, f32[32,2048]{1,0:T(8,128)S(1)}, u32[]{:S(2)}, u32[]{:S(2)}) collective-permute-start(f32[32,2048]{1,0:T(8,128)S(1)} %get-tuple-element.14), channel_id=1, source_target_pairs={{8,16},{16,8},{24,32},{32,24},{40,48},{48,40},{56,64},{64,56},{72,... | collective-permute-start | bytes 786440 | tf_op jit(solution)/shard_map/ppermute | solution.py:623
  88.8 4.4 %collective-permute-done.6 = f32[32,2048]{1,0:T(8,128)S(1)} collective-permute-done((f32[32,2048]{1,0:T(8,128)S(1)}, f32[32,2048]{1,0:T(8,128)S(1)}, u32[]{:S(2)}, u32[]{:S(2)}) %collective-permute-start.6) | collective-permute-done | bytes 262176 | tf_op jit(solution)/shard_map/ppermute | solution.py:622
  93.3 4.2 %collective-permute-done.7 = f32[32,2048]{1,0:T(8,128)S(1)} collective-permute-done((f32[32,2048]{1,0:T(8,128)S(1)}, f32[32,2048]{1,0:T(8,128)S(1)}, u32[]{:S(2)}, u32[]{:S(2)}) %collective-permute-start.7) | collective-permute-done | bytes 262176 | tf_op jit(solution)/shard_map/ppermute | solution.py:623
  97.5 0.8 fusion.3
  (7 shorter events, 0.1 us)
Async XLA Ops:
  0.0 16.1 %copy-start.13 = (f32[32,2048]{1,0:T(8,128)S(1)}, f32[32,2048]{1,0:T(8,128)}, u32[]{:S(2)}) copy-start(f32[32,2048]{1,0:T(8,128)} %param.23) | copy-start | bytes 786436
  0.0 16.0 %collective-permute-start = (f32[32,2048]{1,0:T(8,128)}, f32[32,2048]{1,0:T(8,128)S(1)}, u32[]{:S(2)}, u32[]{:S(2)}) collective-permute-start(f32[32,2048]{1,0:T(8,128)} %param.23), channel_id=1, source_target_pairs={{0,8},{8,0},{16,24},{24,16},{32,40},{40,32},{48,56},{56,48},{64,72... | collective-permute-start | bytes 786440 | tf_op jit(solution)/shard_map/ppermute | solution.py:609
  1.6 14.5 %collective-permute-start.1 = (f32[32,2048]{1,0:T(8,128)}, f32[32,2048]{1,0:T(8,128)S(1)}, u32[]{:S(2)}, u32[]{:S(2)}) collective-permute-start(f32[32,2048]{1,0:T(8,128)} %param.23), channel_id=1, source_target_pairs={{8,16},{16,8},{24,32},{32,24},{40,48},{48,40},{56,64},{64,56},{72,... | collective-permute-start | bytes 786440 | tf_op jit(solution)/shard_map/ppermute | solution.py:610
  16.2 15.3 %collective-permute-start.2 = (f32[96,2048]{1,0:T(8,128)S(1)}, f32[96,2048]{1,0:T(8,128)S(1)}, u32[]{:S(2)}, u32[]{:S(2)}) collective-permute-start(f32[96,2048]{1,0:T(8,128)S(1)} %pad_maximum_fusion.own_ref), channel_id=1, source_target_pairs={{0,1},{1,0},{2,3},{3,2},{4,5},{5,4},{6,7},{7,6},{8,9},{9,8},{10,11... | collective-permute-start | bytes 2359304 | tf_op jit(solution)/shard_map/ppermute | solution.py:614
  16.3 15.2 %collective-permute-start.3 = (f32[96,2048]{1,0:T(8,128)S(1)}, f32[96,2048]{1,0:T(8,128)}, u32[]{:S(2)}, u32[]{:S(2)}) collective-permute-start(f32[96,2048]{1,0:T(8,128)S(1)} %pad_maximum_fusion.own_ref), channel_id=1, source_target_pairs={{1,2},{2,1},{3,4},{4,3},{5,6},{6,5},{9,10},{10,9},{11,12},{12,11},... | collective-permute-start | bytes 2359304 | tf_op jit(solution)/shard_map/ppermute | solution.py:614
  18.4 13.1 %copy-start = (s32[1,1,8]{2,1,0:T(1,128)S(1)}, s32[1,1,8]{2,1,0:T(1,128)}, u32[]{:S(2)}) copy-start(s32[1,1,8]{2,1,0:T(1,128)} %param.26) | copy-start | bytes 100
  18.4 13.1 %copy-start.1 = (bf16[768,256]{1,0:T(8,128)(2,1)S(1)}, bf16[768,256]{1,0:T(8,128)(2,1)}, u32[]{:S(2)}) copy-start(bf16[768,256]{1,0:T(8,128)(2,1)} %constant.50.clone.wxf_ref) | copy-start | bytes 1179652
  18.4 13.1 %copy-start.2 = (bf16[384,512]{1,0:T(8,128)(2,1)S(1)}, bf16[384,512]{1,0:T(8,128)(2,1)}, u32[]{:S(2)}) copy-start(bf16[384,512]{1,0:T(8,128)(2,1)} %constant.54.clone.wxe_ref) | copy-start | bytes 1179652
  18.4 13.1 %copy-start.3 = (bf16[192,768]{1,0:T(8,128)(2,1)S(1)}, bf16[192,768]{1,0:T(8,128)(2,1)}, u32[]{:S(2)}) copy-start(bf16[192,768]{1,0:T(8,128)(2,1)} %constant.57.clone.wxo_ref) | copy-start | bytes 884740
  18.4 13.1 %copy-start.4 = (bf16[192,576]{1,0:T(8,128)(2,1)S(1)}, bf16[192,576]{1,0:T(8,128)(2,1)}, u32[]{:S(2)}) copy-start(bf16[192,576]{1,0:T(8,128)(2,1)} %constant.51.clone.wyf_ref) | copy-start | bytes 663556
  18.4 13.1 %copy-start.5 = (bf16[192,576]{1,0:T(8,128)(2,1)S(1)}, bf16[192,576]{1,0:T(8,128)(2,1)}, u32[]{:S(2)}) copy-start(bf16[192,576]{1,0:T(8,128)(2,1)} %constant.56.clone.wyo_ref) | copy-start | bytes 663556
  18.5 13.1 %copy-start.6 = (bf16[768,128]{1,0:T(8,128)(2,1)S(1)}, bf16[768,128]{1,0:T(8,128)(2,1)}, u32[]{:S(2)}) copy-start(bf16[768,128]{1,0:T(8,128)(2,1)} %constant.49.clone.wzi_ref) | copy-start | bytes 589828
  18.5 13.1 %copy-start.7 = (bf16[384,256]{1,0:T(8,128)(2,1)S(1)}, bf16[384,256]{1,0:T(8,128)(2,1)}, u32[]{:S(2)}) copy-start(bf16[384,256]{1,0:T(8,128)(2,1)} %constant.48.clone.wz_ref) | copy-start | bytes 589828
  18.5 13.1 %copy-start.8 = (bf16[128,512]{1,0:T(8,128)(2,1)S(1)}, bf16[128,512]{1,0:T(8,128)(2,1)}, u32[]{:S(2)}) copy-start(bf16[128,512]{1,0:T(8,128)(2,1)} %constant.53.clone.wxi_ref) | copy-start | bytes 393220
  18.5 13.1 %copy-start.9 = (bf16[128,384]{1,0:T(8,128)(2,1)S(1)}, bf16[128,384]{1,0:T(8,128)(2,1)}, u32[]{:S(2)}) copy-start(bf16[128,384]{1,0:T(8,128)(2,1)} %constant.52.clone.wyi_ref) | copy-start | bytes 294916
  18.5 13.1 %copy-start.10 = (bf16[192,192]{1,0:T(8,128)(2,1)S(1)}, bf16[192,192]{1,0:T(8,128)(2,1)}, u32[]{:S(2)}) copy-start(bf16[192,192]{1,0:T(8,128)(2,1)} %constant.55.clone.wye_ref) | copy-start | bytes 221188
  31.6 65.9 %copy-start.14 = (f32[32,2048]{1,0:T(8,128)S(1)}, f32[32,2048]{1,0:T(8,128)}, u32[]{:S(2)}) copy-start(f32[32,2048]{1,0:T(8,128)} %param.23) | copy-start | bytes 786436
  70.9 6.2 %collective-permute-start.4 = (f32[96,2048]{1,0:T(8,128)S(1)}, f32[96,2048]{1,0:T(8,128)S(1)}, u32[]{:S(2)}, u32[]{:S(2)}) collective-permute-start(f32[96,2048]{1,0:T(8,128)S(1)} %get-tuple-element.11), channel_id=1, source_target_pairs={{0,1},{1,0},{2,3},{3,2},{4,5},{5,4},{6,7},{7,6},{8,9},{9,8},{10,11... | collective-permute-start | bytes 2359304 | tf_op jit(solution)/shard_map/ppermute | solution.py:618
  71.0 13.3 %collective-permute-start.5 = (f32[96,2048]{1,0:T(8,128)S(1)}, f32[96,2048]{1,0:T(8,128)S(1)}, u32[]{:S(2)}, u32[]{:S(2)}) collective-permute-start(f32[96,2048]{1,0:T(8,128)S(1)} %get-tuple-element.12), channel_id=1, source_target_pairs={{1,2},{2,1},{3,4},{4,3},{5,6},{6,5},{9,10},{10,9},{11,12},{12,11},... | collective-permute-start | bytes 2359304 | tf_op jit(solution)/shard_map/ppermute | solution.py:619
  73.1 1.2 %copy-start.11 = (f32[1728,128]{1,0:T(8,128)S(1)}, f32[1728,128]{1,0:T(8,128)}, u32[]{:S(2)}) copy-start(f32[1728,128]{1,0:T(8,128)} %get-tuple-element.9.real) | copy-start | bytes 2654212
  74.2 1.2 %copy-start.12 = (f32[1728,128]{1,0:T(8,128)S(1)}, f32[1728,128]{1,0:T(8,128)}, u32[]{:S(2)}) copy-start(f32[1728,128]{1,0:T(8,128)} %get-tuple-element.10.imag) | copy-start | bytes 2654212
  84.5 8.8 %collective-permute-start.6 = (f32[32,2048]{1,0:T(8,128)S(1)}, f32[32,2048]{1,0:T(8,128)S(1)}, u32[]{:S(2)}, u32[]{:S(2)}) collective-permute-start(f32[32,2048]{1,0:T(8,128)S(1)} %get-tuple-element.13), channel_id=1, source_target_pairs={{0,8},{8,0},{16,24},{24,16},{32,40},{40,32},{48,56},{56,48},{64,72... | collective-permute-start | bytes 786440 | tf_op jit(solution)/shard_map/ppermute | solution.py:622
  85.1 12.4 %collective-permute-start.7 = (f32[32,2048]{1,0:T(8,128)S(1)}, f32[32,2048]{1,0:T(8,128)S(1)}, u32[]{:S(2)}, u32[]{:S(2)}) collective-permute-start(f32[32,2048]{1,0:T(8,128)S(1)} %get-tuple-element.14), channel_id=1, source_target_pairs={{8,16},{16,8},{24,32},{32,24},{40,48},{48,40},{56,64},{64,56},{72,... | collective-permute-start | bytes 786440 | tf_op jit(solution)/shard_map/ppermute | solution.py:623

commit v7 on v6

--- a/solution.py
+++ b/solution.py
@@ -344,7 +344,13 @@
         _, _, _, out, pair = chunks[step]
         sums = dot(ref[...], wzi[...])
         for at in range(4):
-            out[:, columns(pair + at, 1)] = sums[at * WX:(at + 1) * WX]
+            lanes, part = columns(pair + at, 1), sums[at * WX:(at + 1) * WX]
+            if len(out) == 1:
+                out[0][:, lanes] = part
+            else:
+                out[0][:BX, lanes] = part[:BX]
+                out[0][BX:, lanes] = part[2 * BX:]
+                out[1][:, lanes] = part[BX:2 * BX]
 
     pipelined(len(chunks), first, second, stash)
 
@@ -352,7 +358,7 @@
 def main_kernel(
     count_ref, ids_ref, odd_ref, own_ref, first_ref, second_ref, views_hbm, otf_hbm,
     wz_ref, wzi_ref, wxf_ref, wyf_ref, wyi_ref, wxi_ref, wxe_ref, wye_ref, wyo_ref, wxo_ref,
-    first_out, second_out, real_hbm, imag_hbm,
+    first_out, outer_out, inner_out, real_hbm, imag_hbm,
     field, total, big_real, big_imag, real, imag, lines, error, otf, image,
     wide0, wide1, thin0, thin1, last0, last1, otf_sem, image_sem, own_sem,
 ):
@@ -476,7 +482,7 @@
         copy.start()
     chunks = [
         (big_real, big_imag, side * KZ * YPITCH + y, out, y // 2)
-        for side, out in ((1 - odd, first_out), (odd, second_out))
+        for side, out in ((odd, (outer_out, inner_out)), (1 - odd, (first_out,)))
         for y in range(0, BY, 8)
     ]
     final_sums(wxo_ref, wzi_ref, chunks, (last0, last1))
@@ -485,7 +491,7 @@
 
 
 def tail_kernel(real, imag, wzi_ref, wxo_ref, out, last0, last1):
-    chunks = [(real, imag, y, out, y // 2) for y in range(0, BY, 8)]
+    chunks = [(real, imag, y, (out,), y // 2) for y in range(0, BY, 8)]
     final_sums(wxo_ref, wzi_ref, chunks, (last0, last1))
 
 
@@ -549,9 +555,12 @@
     )
     return pl.pallas_call(
         main_kernel,
-        out_shape=[jax.ShapeDtypeStruct(WIDE, F32)] * 2 + [jax.ShapeDtypeStruct(ROWS, F32)] * 2,
+        out_shape=[
+            jax.ShapeDtypeStruct(shape, F32)
+            for shape in (WIDE, (2 * BX, BY * SZ), (BX, BY * SZ), ROWS, ROWS)
+        ],
         in_specs=[IN_SMEM] * 3 + [IN_VMEM] * 3 + [ANYWHERE] * 2 + [IN_VMEM] * len(tables),
-        out_specs=[IN_VMEM] * 2 + [ANYWHERE] * 2,
+        out_specs=[IN_VMEM] * 3 + [ANYWHERE] * 2,
         scratch_shapes=[
             pltpu.VMEM(SPECTRUM, F32),
             pltpu.VMEM(SPECTRUM, F32),
@@ -614,14 +623,18 @@
     window = (own, lax.ppermute(own, "by", first_y), lax.ppermute(own, "by", second_y))
     otf = otf_call(count, ids, psf, 0, 2)
     otf = otf_call(count, ids, psf, 2, CMAX, otf)
-    rim, other_rim, real, imag = main_call(count, ids, odd_y.reshape(1), window, views, otf)
+    rim, outer, inner, real, imag = main_call(
+        count, ids, odd_y.reshape(1), window, views, otf
+    )
+    other_outer = lax.ppermute(outer, "by", second_y)
     one = lax.ppermute(rim, "by", first_y)
-    other = lax.ppermute(other_rim, "by", second_y)
-    sums = tail_call(real, imag) + one + other
-    low, high = sums[:BX], sums[2 * BX:]
+    other_inner = lax.ppermute(inner, "by", second_y)
+    sums = tail_call(real, imag) + one
+    low = sums[:BX] + other_outer[:BX]
+    high = sums[2 * BX:] + other_outer[BX:]
+    other = lax.ppermute(jnp.where(odd_x == 1, high, low), "bx", second_x)
     one = lax.ppermute(jnp.where(odd_x == 1, low, high), "bx", first_x)
-    other = lax.ppermute(jnp.where(odd_x == 1, high, low), "bx", second_x)
-    correction = sums[BX:2 * BX] + one + other
+    correction = sums[BX:2 * BX] + other_inner + one + other
     return estimate * (1.0 + correction / count.astype(F32))
 
 

time: 100 us -> 97.6 us (0.976)
  waiting for transfers between devices: 15.8 us -> 11.1 us
  starting transfers between devices: 14.3 us -> 16.9 us
    ppermute x1 -> x2, waiting for transfers between devices: 7.17 us -> 0.76 us  [the longest x1 0.76 us: per_device(): other_outer = lax.ppermute(outer, 'by', second_y)]
    ppermute x1 -> x2, starting transfers between devices: 2.08 us -> 5.56 us  [the longest x1 3.64 us: per_device(): other_inner = lax.ppermute(inner, 'by', second_y)]
    ppermute x1, starting transfers between devices: 3.73 us -> 1.91 us  [per_device(): other = lax.ppermute(jnp.where(odd_x == 1, high, low), 'bx', second_x)]
    ppermute x1, waiting for transfers between devices: 4.43 us -> 5.6 us  [per_device(): one = lax.ppermute(jnp.where(odd_x == 1, low, high), 'bx', first_x)]
  transfers between devices with their start and end apart: 8 -> 9, of which waited for: 3 -> 3; matrix products, arithmetic and copies ran while one was open for 0% -> 0% of each run, Pallas kernels for 25% -> 25%
where the time goes in v7:
time: 97.6 us; the launch traced here: 96.1 us
  Pallas kernels  63.6 us (65%)
  starting transfers between devices  16.9 us (17%)
  waiting for transfers between devices  11.1 us (11%)
  local copies, waits for them, and re-layouts  2.41 us (2%)
  other arithmetic  1.08 us (1%)
  between operations  1.01 us (1%)
    pallas_call x1, Pallas kernels, main_call(): pl.pallas_call(main_kernel, out_shape=[jax.ShapeDtypeStruct(shape, F32) f...  39.3 us
    pallas_call x2, Pallas kernels, otf_call(): pl.pallas_call(functools.partial(otf_kernel, begin, end), out_shape=jax.S...  22.7 us
    ppermute x1, waiting for transfers between devices, per_device(): one = lax.ppermute(jnp.where(odd_x == 1, low, high), 'bx', first_x)  5.6 us
    ppermute x1, waiting for transfers between devices, per_device(): other = lax.ppermute(jnp.where(odd_x == 1, high, low), 'bx', second_x)  4.71 us
    ppermute x1, starting transfers between devices, per_device(): other = lax.ppermute(estimate, 'bx', second_x)  4.05 us
    ppermute x1, starting transfers between devices, per_device(): other_inner = lax.ppermute(inner, 'by', second_y)  3.64 us
    unnamed x30, local copies, waits for them, and re-layouts  2.41 us
    ppermute x1, starting transfers between devices, per_device(): lax.ppermute(own, 'by', second_y)  2.11 us
  transfers between devices with their start and end apart: 9, of which 3 were waited for; matrix products, arithmetic and copies ran while one was open for 0% of the time, Pallas kernels for 25%

profile of v7, /device:TPU:66, one launch (start us, length us, event | category | flops | bytes accessed | tf_op | source)
XLA Modules:
  0.0 96.1 jit_solution(15421307357228853526)
XLA Ops:
  0.0 1.6 %collective-permute-start = (f32[32,2048]{1,0:T(8,128)}, f32[32,2048]{1,0:T(8,128)S(1)}, u32[]{:S(2)}, u32[]{:S(2)}) collective-permute-start(f32[32,2048]{1,0:T(8,128)} %param.23), channel_id=1, source_target_pairs={{0,8},{8,0},{16,24},{24,16},{32,40},{40,32},{48,56},{56,48},{64,72... | collective-permute-start | bytes 786440 | tf_op jit(solution)/shard_map/ppermute | solution.py:618
  1.6 4.1 %collective-permute-start.1 = (f32[32,2048]{1,0:T(8,128)}, f32[32,2048]{1,0:T(8,128)S(1)}, u32[]{:S(2)}, u32[]{:S(2)}) collective-permute-start(f32[32,2048]{1,0:T(8,128)} %param.23), channel_id=1, source_target_pairs={{8,16},{16,8},{24,32},{32,24},{40,48},{48,40},{56,64},{64,56},{72,... | collective-permute-start | bytes 786440 | tf_op jit(solution)/shard_map/ppermute | solution.py:619
  6.3 9.7 %otf.2.rest_0_ = f32[5,48,2,96,128]{4,3,2,1,0:T(8,128)} custom-call(s32[1]{0:T(128)} %bitcast.4.count_ref, s32[8]{0:T(128)} %bitcast.8, f32[8,64,4096]{2,1,0:T(8,128)} %psf_hbm.3, bf16[384,256]{1,0:T(8,128)(2,1)} %constant.45.clone.wz_hbm, bf16[384,256]{1,0:T(8,128)(2,1)} %constant.46.clone.wx_hbm, bf16[192,384]{1,0:T(8,128)(2,1)} %constant.47.clone.wy_hbm), custom_call_target="tpu_custom_call" | custom-call | flops 8000000000 | bytes 12000000 | tf_op jit(solution)/shard_map/otf/pallas_call | solution.py:516
  16.0 0.0 collective-permute-done
  16.0 0.0 collective-permute-done.1
  16.1 0.0 copy-done.13
  16.1 0.1 pad_maximum_fusion.own_ref
  16.2 0.1 collective-permute-start.2
  16.3 2.1 %collective-permute-start.3 = (f32[96,2048]{1,0:T(8,128)S(1)}, f32[96,2048]{1,0:T(8,128)}, u32[]{:S(2)}, u32[]{:S(2)}) collective-permute-start(f32[96,2048]{1,0:T(8,128)S(1)} %pad_maximum_fusion.own_ref), channel_id=1, source_target_pairs={{1,2},{2,1},{3,4},{4,3},{5,6},{6,5},{9,10},{10,9},{11,12},{12,11},... | collective-permute-start | bytes 2359304 | tf_op jit(solution)/shard_map/ppermute | solution.py:623
  18.4 0.0 copy-start
  18.4 0.0 copy-start.1
  18.4 0.0 copy-start.2
  18.4 0.0 copy-start.3
  18.4 0.0 copy-start.4
  18.4 0.0 copy-start.5
  18.4 0.0 copy-start.6
  18.5 0.0 copy-start.7
  18.5 0.0 copy-start.8
  18.5 0.0 copy-start.9
  18.5 0.0 copy-start.10
  18.5 12.9 %otf.3.otf_hbm = f32[5,48,2,96,128]{4,3,2,1,0:T(8,128)} custom-call(s32[1]{0:T(128)} %bitcast.5.count_ref, s32[8]{0:T(128)} %bitcast.9, f32[8,64,4096]{2,1,0:T(8,128)} %psf_hbm.3, bf16[384,256]{1,0:T(8,128)(2,1)} %constant.45.clone.wz_hbm, bf16[384,256]{1,0:T(8,128)(2,1)} %constant.46.clone.wx_hbm, ...), custom_call_target="tpu_custom_call", output_to_operand_aliasing={{}: (6, {})} | custom-call | flops 12000000000 | bytes 18000000 | tf_op jit(solution)/shard_map/otf/pallas_call | solution.py:516
  31.5 0.0 collective-permute-done.2.first_ref
  31.5 0.0 collective-permute-done.3.second_ref
  31.5 0.0 copy-done
  31.5 0.0 copy-done.1
  31.5 0.0 copy-done.2
  31.5 0.0 copy-done.3
  31.5 0.0 copy-done.4
  31.5 0.0 copy-done.5
  31.5 0.0 copy-done.6
  31.6 0.0 copy-start.14
  31.6 39.3 %views.1 = (f32[96,2048]{1,0:T(8,128)S(1)}, f32[64,2048]{1,0:T(8,128)S(1)}, f32[32,2048]{1,0:T(8,128)S(1)}, f32[1728,128]{1,0:T(8,128)}, f32[1728,128]{1,0:T(8,128)}) custom-call(s32[1]{0:T(128)} %bitcast.6.count_ref, s32[8]{0:T(128)S(1)} %bitcast.10, s32[1]{0:T(128)} %bitcast.2.odd_ref, f32[96,2048]{1,0:T(8,128)S(1)} %pad_maximum_fusion.own_ref, ...), custom_call_target="tpu_custom_call" | custom-call | flops 30000001024 | bytes 40000000 | tf_op jit(solution)/shard_map/views/pallas_call | solution.py:556
  70.9 0.1 collective-permute-start.4
  71.0 1.9 %collective-permute-start.6 = (f32[64,2048]{1,0:T(8,128)S(1)}, f32[64,2048]{1,0:T(8,128)S(1)}, u32[]{:S(2)}, u32[]{:S(2)}) collective-permute-start(f32[64,2048]{1,0:T(8,128)S(1)} %get-tuple-element.14), channel_id=1, source_target_pairs={{1,2},{2,1},{3,4},{4,3},{5,6},{6,5},{9,10},{10,9},{11,12},{12,11},... | collective-permute-start | bytes 1572872 | tf_op jit(solution)/shard_map/ppermute | solution.py:629
  72.9 3.6 %collective-permute-start.5 = (f32[32,2048]{1,0:T(8,128)S(1)}, f32[32,2048]{1,0:T(8,128)S(1)}, u32[]{:S(2)}, u32[]{:S(2)}) collective-permute-start(f32[32,2048]{1,0:T(8,128)S(1)} %get-tuple-element.13), channel_id=1, source_target_pairs={{1,2},{2,1},{3,4},{4,3},{5,6},{6,5},{9,10},{10,9},{11,12},{12,11},... | collective-permute-start | bytes 786440 | tf_op jit(solution)/shard_map/ppermute | solution.py:631
  76.6 1.2 %copy-done.11 = f32[1728,128]{1,0:T(8,128)S(1)} copy-done((f32[1728,128]{1,0:T(8,128)S(1)}, f32[1728,128]{1,0:T(8,128)}, u32[]{:S(2)}) %copy-start.11) | copy-done | bytes 884760
  77.7 1.2 %copy-done.12 = f32[1728,128]{1,0:T(8,128)S(1)} copy-done((f32[1728,128]{1,0:T(8,128)S(1)}, f32[1728,128]{1,0:T(8,128)}, u32[]{:S(2)}) %copy-start.12) | copy-done | bytes 884760
  78.9 1.7 %tail.1 = f32[96,2048]{1,0:T(8,128)S(1)} custom-call(f32[1728,128]{1,0:T(8,128)S(1)} %copy-done.11, f32[1728,128]{1,0:T(8,128)S(1)} %copy-done.12, bf16[768,128]{1,0:T(8,128)(2,1)S(1)} %copy-done.6, bf16[192,768]{1,0:T(8,128)(2,1)S(1)} %copy-done.3), custom_call_target="tpu_custom_call" | custom-call | flops 4000000000 | bytes 3000000 | tf_op jit(solution)/shard_map/tail/pallas_call | solution.py:593
  80.6 0.0 collective-permute-done.4
  80.6 0.1 add.24
  80.7 0.8 collective-permute-done.6
  81.5 0.1 broadcast_select_fusion.1
  81.5 1.5 %collective-permute-start.7 = (f32[32,2048]{1,0:T(8,128)S(1)}, f32[32,2048]{1,0:T(8,128)S(1)}, u32[]{:S(2)}, u32[]{:S(2)}) collective-permute-start(f32[32,2048]{1,0:T(8,128)S(1)} %get-tuple-element.15), channel_id=1, source_target_pairs={{0,8},{8,0},{16,24},{24,16},{32,40},{40,32},{48,56},{56,48},{64,72... | collective-permute-start | bytes 786440 | tf_op jit(solution)/shard_map/ppermute | solution.py:636
  83.1 1.9 %collective-permute-start.8 = (f32[32,2048]{1,0:T(8,128)S(1)}, f32[32,2048]{1,0:T(8,128)S(1)}, u32[]{:S(2)}, u32[]{:S(2)}) collective-permute-start(f32[32,2048]{1,0:T(8,128)S(1)} %get-tuple-element.16), channel_id=1, source_target_pairs={{8,16},{16,8},{24,32},{32,24},{40,48},{48,40},{56,64},{64,56},{72,... | collective-permute-start | bytes 786440 | tf_op jit(solution)/shard_map/ppermute | solution.py:635
  85.0 0.0 collective-permute-done.5
  85.0 5.6 %collective-permute-done.7 = f32[32,2048]{1,0:T(8,128)S(1)} collective-permute-done((f32[32,2048]{1,0:T(8,128)S(1)}, f32[32,2048]{1,0:T(8,128)S(1)}, u32[]{:S(2)}, u32[]{:S(2)}) %collective-permute-start.7) | collective-permute-done | bytes 262176 | tf_op jit(solution)/shard_map/ppermute | solution.py:636
  90.6 4.7 %collective-permute-done.8 = f32[32,2048]{1,0:T(8,128)S(1)} collective-permute-done((f32[32,2048]{1,0:T(8,128)S(1)}, f32[32,2048]{1,0:T(8,128)S(1)}, u32[]{:S(2)}, u32[]{:S(2)}) %collective-permute-start.8) | collective-permute-done | bytes 262176 | tf_op jit(solution)/shard_map/ppermute | solution.py:635
  95.3 0.8 fusion.4
  (9 shorter events, 0.1 us)
Async XLA Ops:
  0.0 16.1 %copy-start.13 = (f32[32,2048]{1,0:T(8,128)S(1)}, f32[32,2048]{1,0:T(8,128)}, u32[]{:S(2)}) copy-start(f32[32,2048]{1,0:T(8,128)} %param.23) | copy-start | bytes 786436
  0.0 16.0 %collective-permute-start = (f32[32,2048]{1,0:T(8,128)}, f32[32,2048]{1,0:T(8,128)S(1)}, u32[]{:S(2)}, u32[]{:S(2)}) collective-permute-start(f32[32,2048]{1,0:T(8,128)} %param.23), channel_id=1, source_target_pairs={{0,8},{8,0},{16,24},{24,16},{32,40},{40,32},{48,56},{56,48},{64,72... | collective-permute-start | bytes 786440 | tf_op jit(solution)/shard_map/ppermute | solution.py:618
  1.6 14.5 %collective-permute-start.1 = (f32[32,2048]{1,0:T(8,128)}, f32[32,2048]{1,0:T(8,128)S(1)}, u32[]{:S(2)}, u32[]{:S(2)}) collective-permute-start(f32[32,2048]{1,0:T(8,128)} %param.23), channel_id=1, source_target_pairs={{8,16},{16,8},{24,32},{32,24},{40,48},{48,40},{56,64},{64,56},{72,... | collective-permute-start | bytes 786440 | tf_op jit(solution)/shard_map/ppermute | solution.py:619
  16.2 15.3 %collective-permute-start.2 = (f32[96,2048]{1,0:T(8,128)S(1)}, f32[96,2048]{1,0:T(8,128)S(1)}, u32[]{:S(2)}, u32[]{:S(2)}) collective-permute-start(f32[96,2048]{1,0:T(8,128)S(1)} %pad_maximum_fusion.own_ref), channel_id=1, source_target_pairs={{0,1},{1,0},{2,3},{3,2},{4,5},{5,4},{6,7},{7,6},{8,9},{9,8},{10,11... | collective-permute-start | bytes 2359304 | tf_op jit(solution)/shard_map/ppermute | solution.py:623
  16.3 15.2 %collective-permute-start.3 = (f32[96,2048]{1,0:T(8,128)S(1)}, f32[96,2048]{1,0:T(8,128)}, u32[]{:S(2)}, u32[]{:S(2)}) collective-permute-start(f32[96,2048]{1,0:T(8,128)S(1)} %pad_maximum_fusion.own_ref), channel_id=1, source_target_pairs={{1,2},{2,1},{3,4},{4,3},{5,6},{6,5},{9,10},{10,9},{11,12},{12,11},... | collective-permute-start | bytes 2359304 | tf_op jit(solution)/shard_map/ppermute | solution.py:623
  18.4 13.1 %copy-start = (s32[1,1,8]{2,1,0:T(1,128)S(1)}, s32[1,1,8]{2,1,0:T(1,128)}, u32[]{:S(2)}) copy-start(s32[1,1,8]{2,1,0:T(1,128)} %param.26) | copy-start | bytes 100
  18.4 13.1 %copy-start.1 = (bf16[768,256]{1,0:T(8,128)(2,1)S(1)}, bf16[768,256]{1,0:T(8,128)(2,1)}, u32[]{:S(2)}) copy-start(bf16[768,256]{1,0:T(8,128)(2,1)} %constant.50.clone.wxf_ref) | copy-start | bytes 1179652
  18.4 13.1 %copy-start.2 = (bf16[384,512]{1,0:T(8,128)(2,1)S(1)}, bf16[384,512]{1,0:T(8,128)(2,1)}, u32[]{:S(2)}) copy-start(bf16[384,512]{1,0:T(8,128)(2,1)} %constant.54.clone.wxe_ref) | copy-start | bytes 1179652
  18.4 13.1 %copy-start.3 = (bf16[192,768]{1,0:T(8,128)(2,1)S(1)}, bf16[192,768]{1,0:T(8,128)(2,1)}, u32[]{:S(2)}) copy-start(bf16[192,768]{1,0:T(8,128)(2,1)} %constant.57.clone.wxo_ref) | copy-start | bytes 884740
  18.4 13.1 %copy-start.4 = (bf16[192,576]{1,0:T(8,128)(2,1)S(1)}, bf16[192,576]{1,0:T(8,128)(2,1)}, u32[]{:S(2)}) copy-start(bf16[192,576]{1,0:T(8,128)(2,1)} %constant.51.clone.wyf_ref) | copy-start | bytes 663556
  18.4 13.1 %copy-start.5 = (bf16[192,576]{1,0:T(8,128)(2,1)S(1)}, bf16[192,576]{1,0:T(8,128)(2,1)}, u32[]{:S(2)}) copy-start(bf16[192,576]{1,0:T(8,128)(2,1)} %constant.56.clone.wyo_ref) | copy-start | bytes 663556
  18.4 13.1 %copy-start.6 = (bf16[768,128]{1,0:T(8,128)(2,1)S(1)}, bf16[768,128]{1,0:T(8,128)(2,1)}, u32[]{:S(2)}) copy-start(bf16[768,128]{1,0:T(8,128)(2,1)} %constant.49.clone.wzi_ref) | copy-start | bytes 589828
  18.5 13.1 %copy-start.7 = (bf16[384,256]{1,0:T(8,128)(2,1)S(1)}, bf16[384,256]{1,0:T(8,128)(2,1)}, u32[]{:S(2)}) copy-start(bf16[384,256]{1,0:T(8,128)(2,1)} %constant.48.clone.wz_ref) | copy-start | bytes 589828
  18.5 13.1 %copy-start.8 = (bf16[128,512]{1,0:T(8,128)(2,1)S(1)}, bf16[128,512]{1,0:T(8,128)(2,1)}, u32[]{:S(2)}) copy-start(bf16[128,512]{1,0:T(8,128)(2,1)} %constant.53.clone.wxi_ref) | copy-start | bytes 393220
  18.5 13.1 %copy-start.9 = (bf16[128,384]{1,0:T(8,128)(2,1)S(1)}, bf16[128,384]{1,0:T(8,128)(2,1)}, u32[]{:S(2)}) copy-start(bf16[128,384]{1,0:T(8,128)(2,1)} %constant.52.clone.wyi_ref) | copy-start | bytes 294916
  18.5 13.1 %copy-start.10 = (bf16[192,192]{1,0:T(8,128)(2,1)S(1)}, bf16[192,192]{1,0:T(8,128)(2,1)}, u32[]{:S(2)}) copy-start(bf16[192,192]{1,0:T(8,128)(2,1)} %constant.55.clone.wye_ref) | copy-start | bytes 221188
  31.6 63.7 %copy-start.14 = (f32[32,2048]{1,0:T(8,128)S(1)}, f32[32,2048]{1,0:T(8,128)}, u32[]{:S(2)}) copy-start(f32[32,2048]{1,0:T(8,128)} %param.23) | copy-start | bytes 786436
  70.9 9.7 %collective-permute-start.4 = (f32[96,2048]{1,0:T(8,128)S(1)}, f32[96,2048]{1,0:T(8,128)S(1)}, u32[]{:S(2)}, u32[]{:S(2)}) collective-permute-start(f32[96,2048]{1,0:T(8,128)S(1)} %get-tuple-element.12), channel_id=1, source_target_pairs={{0,1},{1,0},{2,3},{3,2},{4,5},{5,4},{6,7},{7,6},{8,9},{9,8},{10,11... | collective-permute-start | bytes 2359304 | tf_op jit(solution)/shard_map/ppermute | solution.py:630
  71.0 10.5 %collective-permute-start.6 = (f32[64,2048]{1,0:T(8,128)S(1)}, f32[64,2048]{1,0:T(8,128)S(1)}, u32[]{:S(2)}, u32[]{:S(2)}) collective-permute-start(f32[64,2048]{1,0:T(8,128)S(1)} %get-tuple-element.14), channel_id=1, source_target_pairs={{1,2},{2,1},{3,4},{4,3},{5,6},{6,5},{9,10},{10,9},{11,12},{12,11},... | collective-permute-start | bytes 1572872 | tf_op jit(solution)/shard_map/ppermute | solution.py:629
  72.9 12.1 %collective-permute-start.5 = (f32[32,2048]{1,0:T(8,128)S(1)}, f32[32,2048]{1,0:T(8,128)S(1)}, u32[]{:S(2)}, u32[]{:S(2)}) collective-permute-start(f32[32,2048]{1,0:T(8,128)S(1)} %get-tuple-element.13), channel_id=1, source_target_pairs={{1,2},{2,1},{3,4},{4,3},{5,6},{6,5},{9,10},{10,9},{11,12},{12,11},... | collective-permute-start | bytes 786440 | tf_op jit(solution)/shard_map/ppermute | solution.py:631
  76.5 1.2 %copy-start.11 = (f32[1728,128]{1,0:T(8,128)S(1)}, f32[1728,128]{1,0:T(8,128)}, u32[]{:S(2)}) copy-start(f32[1728,128]{1,0:T(8,128)} %get-tuple-element.10.real) | copy-start | bytes 2654212
  77.7 1.2 %copy-start.12 = (f32[1728,128]{1,0:T(8,128)S(1)}, f32[1728,128]{1,0:T(8,128)}, u32[]{:S(2)}) copy-start(f32[1728,128]{1,0:T(8,128)} %get-tuple-element.11.imag) | copy-start | bytes 2654212
  81.5 9.1 %collective-permute-start.7 = (f32[32,2048]{1,0:T(8,128)S(1)}, f32[32,2048]{1,0:T(8,128)S(1)}, u32[]{:S(2)}, u32[]{:S(2)}) collective-permute-start(f32[32,2048]{1,0:T(8,128)S(1)} %get-tuple-element.15), channel_id=1, source_target_pairs={{0,8},{8,0},{16,24},{24,16},{32,40},{40,32},{48,56},{56,48},{64,72... | collective-permute-start | bytes 786440 | tf_op jit(solution)/shard_map/ppermute | solution.py:636
  83.1 12.2 %collective-permute-start.8 = (f32[32,2048]{1,0:T(8,128)S(1)}, f32[32,2048]{1,0:T(8,128)S(1)}, u32[]{:S(2)}, u32[]{:S(2)}) collective-permute-start(f32[32,2048]{1,0:T(8,128)S(1)} %get-tuple-element.16), channel_id=1, source_target_pairs={{8,16},{16,8},{24,32},{32,24},{40,48},{48,40},{56,64},{64,56},{72,... | collective-permute-start | bytes 786440 | tf_op jit(solution)/shard_map/ppermute | solution.py:635

commit v8 on v7

--- a/solution.py
+++ b/solution.py
@@ -322,8 +322,8 @@
 MAIN_LIMIT = 48 * MIB
 TAIL_LIMIT = 16 * MIB
 UY = 12
-UP = 12
-UG = 12
+UP = 24
+UG = 24
 UF = 8
 UT = 12
 
@@ -628,8 +628,9 @@
     )
     other_outer = lax.ppermute(outer, "by", second_y)
     one = lax.ppermute(rim, "by", first_y)
+    center, inner = lax.optimization_barrier((tail_call(real, imag), inner))
     other_inner = lax.ppermute(inner, "by", second_y)
-    sums = tail_call(real, imag) + one
+    sums = center + one
     low = sums[:BX] + other_outer[:BX]
     high = sums[2 * BX:] + other_outer[BX:]
     other = lax.ppermute(jnp.where(odd_x == 1, high, low), "bx", second_x)

time: 97.6 us -> 96.4 us (0.988)
  the two profiles are of different devices: /device:TPU:66 before, /device:TPU:38 now
where the time goes in v8:
time: 96.4 us; the launch traced here: 96.5 us
  Pallas kernels  36.7 us (38%)
  starting transfers between devices  34.9 us (36%)
  waiting for transfers between devices  20.3 us (21%)
  local copies, waits for them, and re-layouts  2.41 us (2%)
  other arithmetic  1.08 us (1%)
  between operations  0.98 us (1%)
    pallas_call x1, Pallas kernels, main_call(): pl.pallas_call(main_kernel, out_shape=[jax.ShapeDtypeStruct(shape, F32) f...  23.3 us
    ppermute x1, starting transfers between devices, per_device(): one = lax.ppermute(rim, 'by', first_y)  19.2 us
    pallas_call x2, Pallas kernels, otf_call(): pl.pallas_call(functools.partial(otf_kernel, begin, end), out_shape=jax.S...  11.7 us
    ppermute x1, waiting for transfers between devices, per_device(): lax.ppermute(own, 'by', second_y)  9.17 us
    ppermute x1, waiting for transfers between devices, per_device(): one = lax.ppermute(jnp.where(odd_x == 1, low, high), 'bx', first_x)  5.32 us
    ppermute x1, starting transfers between devices, per_device(): other = lax.ppermute(estimate, 'bx', second_x)  4.34 us
    ppermute x1, waiting for transfers between devices, per_device(): other = lax.ppermute(jnp.where(odd_x == 1, high, low), 'bx', second_x)  4.02 us
    ppermute x1, starting transfers between devices, per_device(): other_inner = lax.ppermute(inner, 'by', second_y)  3.64 us
  transfers between devices with their start and end apart: 9, of which 5 were waited for; matrix products, arithmetic and copies ran while one was open for 0% of the time, Pallas kernels for 14%

profile of v8, /device:TPU:38, one launch (start us, length us, event | category | flops | bytes accessed | tf_op | source)
XLA Modules:
  0.0 96.5 jit_solution(11060834311235815954)
XLA Ops:
  0.0 1.6 %collective-permute-start = (f32[32,2048]{1,0:T(8,128)}, f32[32,2048]{1,0:T(8,128)S(1)}, u32[]{:S(2)}, u32[]{:S(2)}) collective-permute-start(f32[32,2048]{1,0:T(8,128)} %param.23), channel_id=1, source_target_pairs={{0,8},{8,0},{16,24},{24,16},{32,40},{40,32},{48,56},{56,48},{64,72... | collective-permute-start | bytes 786440 | tf_op jit(solution)/shard_map/ppermute | solution.py:618
  1.6 4.3 %collective-permute-start.1 = (f32[32,2048]{1,0:T(8,128)}, f32[32,2048]{1,0:T(8,128)S(1)}, u32[]{:S(2)}, u32[]{:S(2)}) collective-permute-start(f32[32,2048]{1,0:T(8,128)} %param.23), channel_id=1, source_target_pairs={{8,16},{16,8},{24,32},{32,24},{40,48},{48,40},{56,64},{64,56},{72,... | collective-permute-start | bytes 786440 | tf_op jit(solution)/shard_map/ppermute | solution.py:619
  6.6 9.7 %otf.2.rest_0_ = f32[5,48,2,96,128]{4,3,2,1,0:T(8,128)} custom-call(s32[1]{0:T(128)} %bitcast.4.count_ref, s32[8]{0:T(128)} %bitcast.8, f32[8,64,4096]{2,1,0:T(8,128)} %psf_hbm.3, bf16[384,256]{1,0:T(8,128)(2,1)} %constant.45.clone.wz_hbm, bf16[384,256]{1,0:T(8,128)(2,1)} %constant.46.clone.wx_hbm, bf16[192,384]{1,0:T(8,128)(2,1)} %constant.47.clone.wy_hbm), custom_call_target="tpu_custom_call" | custom-call | flops 8000000000 | bytes 12000000 | tf_op jit(solution)/shard_map/otf/pallas_call | solution.py:516
  16.3 0.0 collective-permute-done
  16.3 0.0 collective-permute-done.1
  16.4 0.0 copy-done.13
  16.4 0.1 pad_maximum_fusion.own_ref
  16.5 0.1 collective-permute-start.2
  16.6 2.1 %collective-permute-start.3 = (f32[96,2048]{1,0:T(8,128)S(1)}, f32[96,2048]{1,0:T(8,128)}, u32[]{:S(2)}, u32[]{:S(2)}) collective-permute-start(f32[96,2048]{1,0:T(8,128)S(1)} %pad_maximum_fusion.own_ref), channel_id=1, source_target_pairs={{1,2},{2,1},{3,4},{4,3},{5,6},{6,5},{9,10},{10,9},{11,12},{12,11},... | collective-permute-start | bytes 2359304 | tf_op jit(solution)/shard_map/ppermute | solution.py:623
  18.7 0.0 copy-start
  18.7 0.0 copy-start.1
  18.7 0.0 copy-start.2
  18.7 0.0 copy-start.3
  18.7 0.0 copy-start.4
  18.7 0.0 copy-start.5
  18.7 0.0 copy-start.6
  18.8 0.0 copy-start.7
  18.8 0.0 copy-start.8
  18.8 0.0 copy-start.9
  18.8 0.0 copy-start.10
  18.8 2.0 %otf.3.otf_hbm = f32[5,48,2,96,128]{4,3,2,1,0:T(8,128)} custom-call(s32[1]{0:T(128)} %bitcast.5.count_ref, s32[8]{0:T(128)} %bitcast.9, f32[8,64,4096]{2,1,0:T(8,128)} %psf_hbm.3, bf16[384,256]{1,0:T(8,128)(2,1)} %constant.45.clone.wz_hbm, bf16[384,256]{1,0:T(8,128)(2,1)} %constant.46.clone.wx_hbm, ...), custom_call_target="tpu_custom_call", output_to_operand_aliasing={{}: (6, {})} | custom-call | flops 12000000000 | bytes 18000000 | tf_op jit(solution)/shard_map/otf/pallas_call | solution.py:516
  20.8 0.0 collective-permute-done.2.first_ref
  20.8 9.2 %collective-permute-done.3.second_ref = f32[96,2048]{1,0:T(8,128)} collective-permute-done((f32[96,2048]{1,0:T(8,128)S(1)}, f32[96,2048]{1,0:T(8,128)}, u32[]{:S(2)}, u32[]{:S(2)}) %collective-permute-start.3) | collective-permute-done | bytes 786464 | tf_op jit(solution)/shard_map/ppermute | solution.py:623
  30.0 0.0 copy-done
  30.0 0.0 copy-done.1
  30.0 0.0 copy-done.2
  30.0 0.0 copy-done.3
  30.0 0.0 copy-done.4
  30.1 0.0 copy-start.14
  30.1 23.3 %views.1 = (f32[96,2048]{1,0:T(8,128)S(1)}, f32[64,2048]{1,0:T(8,128)S(1)}, f32[32,2048]{1,0:T(8,128)S(1)}, f32[1728,128]{1,0:T(8,128)}, f32[1728,128]{1,0:T(8,128)}) custom-call(s32[1]{0:T(128)} %bitcast.6.count_ref, s32[8]{0:T(128)S(1)} %bitcast.10, s32[1]{0:T(128)} %bitcast.2.odd_ref, f32[96,2048]{1,0:T(8,128)S(1)} %pad_maximum_fusion.own_ref, ...), custom_call_target="tpu_custom_call" | custom-call | flops 30000001024 | bytes 40000000 | tf_op jit(solution)/shard_map/views/pallas_call | solution.py:556
  53.4 19.2 %collective-permute-start.4 = (f32[96,2048]{1,0:T(8,128)S(1)}, f32[96,2048]{1,0:T(8,128)S(1)}, u32[]{:S(2)}, u32[]{:S(2)}) collective-permute-start(f32[96,2048]{1,0:T(8,128)S(1)} %get-tuple-element.16), channel_id=1, source_target_pairs={{0,1},{1,0},{2,3},{3,2},{4,5},{5,4},{6,7},{7,6},{8,9},{9,8},{10,11... | collective-permute-start | bytes 2359304 | tf_op jit(solution)/shard_map/ppermute | solution.py:630
  72.7 1.9 %collective-permute-start.6 = (f32[64,2048]{1,0:T(8,128)S(1)}, f32[64,2048]{1,0:T(8,128)S(1)}, u32[]{:S(2)}, u32[]{:S(2)}) collective-permute-start(f32[64,2048]{1,0:T(8,128)S(1)} %get-tuple-element.18), channel_id=1, source_target_pairs={{1,2},{2,1},{3,4},{4,3},{5,6},{6,5},{9,10},{10,9},{11,12},{12,11},... | collective-permute-start | bytes 1572872 | tf_op jit(solution)/shard_map/ppermute | solution.py:629
  74.6 0.0 copy-start.11
  74.6 1.2 %copy-done.11 = f32[1728,128]{1,0:T(8,128)S(1)} copy-done((f32[1728,128]{1,0:T(8,128)S(1)}, f32[1728,128]{1,0:T(8,128)}, u32[]{:S(2)}) %copy-start.11) | copy-done | bytes 884760
  75.7 1.2 %copy-done.12 = f32[1728,128]{1,0:T(8,128)S(1)} copy-done((f32[1728,128]{1,0:T(8,128)S(1)}, f32[1728,128]{1,0:T(8,128)}, u32[]{:S(2)}) %copy-start.12) | copy-done | bytes 884760
  76.9 1.7 %tail.1 = f32[96,2048]{1,0:T(8,128)S(1)} custom-call(f32[1728,128]{1,0:T(8,128)S(1)} %copy-done.11, f32[1728,128]{1,0:T(8,128)S(1)} %copy-done.12, bf16[768,128]{1,0:T(8,128)(2,1)S(1)} %copy-done.6, bf16[192,768]{1,0:T(8,128)(2,1)S(1)} %copy-done.3), custom_call_target="tpu_custom_call" | custom-call | flops 4000000000 | bytes 3000000 | tf_op jit(solution)/shard_map/tail/pallas_call | solution.py:593
  78.6 3.6 %collective-permute-start.5 = (f32[32,2048]{1,0:T(8,128)S(1)}, f32[32,2048]{1,0:T(8,128)S(1)}, u32[]{:S(2)}, u32[]{:S(2)}) collective-permute-start(f32[32,2048]{1,0:T(8,128)S(1)} %get-tuple-element.17), channel_id=1, source_target_pairs={{1,2},{2,1},{3,4},{4,3},{5,6},{6,5},{9,10},{10,9},{11,12},{12,11},... | collective-permute-start | bytes 786440 | tf_op jit(solution)/shard_map/ppermute | solution.py:632
  82.3 0.0 collective-permute-done.4
  82.3 0.1 add.24
  82.4 0.8 collective-permute-done.6
  83.1 0.1 broadcast_select_fusion.1
  83.2 0.1 collective-permute-start.7
  83.3 1.9 %collective-permute-start.8 = (f32[32,2048]{1,0:T(8,128)S(1)}, f32[32,2048]{1,0:T(8,128)S(1)}, u32[]{:S(2)}, u32[]{:S(2)}) collective-permute-start(f32[32,2048]{1,0:T(8,128)S(1)} %get-tuple-element.20), channel_id=1, source_target_pairs={{8,16},{16,8},{24,32},{32,24},{40,48},{48,40},{56,64},{64,56},{72,... | collective-permute-start | bytes 786440 | tf_op jit(solution)/shard_map/ppermute | solution.py:636
  85.2 1.1 %collective-permute-done.5 = f32[32,2048]{1,0:T(8,128)S(1)} collective-permute-done((f32[32,2048]{1,0:T(8,128)S(1)}, f32[32,2048]{1,0:T(8,128)S(1)}, u32[]{:S(2)}, u32[]{:S(2)}) %collective-permute-start.5) | collective-permute-done | bytes 262176 | tf_op jit(solution)/shard_map/ppermute | solution.py:632
  86.3 5.3 %collective-permute-done.7 = f32[32,2048]{1,0:T(8,128)S(1)} collective-permute-done((f32[32,2048]{1,0:T(8,128)S(1)}, f32[32,2048]{1,0:T(8,128)S(1)}, u32[]{:S(2)}, u32[]{:S(2)}) %collective-permute-start.7) | collective-permute-done | bytes 262176 | tf_op jit(solution)/shard_map/ppermute | solution.py:637
  91.6 4.0 %collective-permute-done.8 = f32[32,2048]{1,0:T(8,128)S(1)} collective-permute-done((f32[32,2048]{1,0:T(8,128)S(1)}, f32[32,2048]{1,0:T(8,128)S(1)}, u32[]{:S(2)}, u32[]{:S(2)}) %collective-permute-start.8) | collective-permute-done | bytes 262176 | tf_op jit(solution)/shard_map/ppermute | solution.py:636
  95.6 0.0 copy-done.14
  95.6 0.8 fusion.4
  (9 shorter events, 0.1 us)
Async XLA Ops:
  0.0 16.4 %copy-start.13 = (f32[32,2048]{1,0:T(8,128)S(1)}, f32[32,2048]{1,0:T(8,128)}, u32[]{:S(2)}) copy-start(f32[32,2048]{1,0:T(8,128)} %param.23) | copy-start | bytes 786436
  0.0 16.3 %collective-permute-start = (f32[32,2048]{1,0:T(8,128)}, f32[32,2048]{1,0:T(8,128)S(1)}, u32[]{:S(2)}, u32[]{:S(2)}) collective-permute-start(f32[32,2048]{1,0:T(8,128)} %param.23), channel_id=1, source_target_pairs={{0,8},{8,0},{16,24},{24,16},{32,40},{40,32},{48,56},{56,48},{64,72... | collective-permute-start | bytes 786440 | tf_op jit(solution)/shard_map/ppermute | solution.py:618
  1.6 14.8 %collective-permute-start.1 = (f32[32,2048]{1,0:T(8,128)}, f32[32,2048]{1,0:T(8,128)S(1)}, u32[]{:S(2)}, u32[]{:S(2)}) collective-permute-start(f32[32,2048]{1,0:T(8,128)} %param.23), channel_id=1, source_target_pairs={{8,16},{16,8},{24,32},{32,24},{40,48},{48,40},{56,64},{64,56},{72,... | collective-permute-start | bytes 786440 | tf_op jit(solution)/shard_map/ppermute | solution.py:619
  16.5 4.3 %collective-permute-start.2 = (f32[96,2048]{1,0:T(8,128)S(1)}, f32[96,2048]{1,0:T(8,128)S(1)}, u32[]{:S(2)}, u32[]{:S(2)}) collective-permute-start(f32[96,2048]{1,0:T(8,128)S(1)} %pad_maximum_fusion.own_ref), channel_id=1, source_target_pairs={{0,1},{1,0},{2,3},{3,2},{4,5},{5,4},{6,7},{7,6},{8,9},{9,8},{10,11... | collective-permute-start | bytes 2359304 | tf_op jit(solution)/shard_map/ppermute | solution.py:623
  16.6 13.4 %collective-permute-start.3 = (f32[96,2048]{1,0:T(8,128)S(1)}, f32[96,2048]{1,0:T(8,128)}, u32[]{:S(2)}, u32[]{:S(2)}) collective-permute-start(f32[96,2048]{1,0:T(8,128)S(1)} %pad_maximum_fusion.own_ref), channel_id=1, source_target_pairs={{1,2},{2,1},{3,4},{4,3},{5,6},{6,5},{9,10},{10,9},{11,12},{12,11},... | collective-permute-start | bytes 2359304 | tf_op jit(solution)/shard_map/ppermute | solution.py:623
  18.7 11.3 %copy-start = (s32[1,1,8]{2,1,0:T(1,128)S(1)}, s32[1,1,8]{2,1,0:T(1,128)}, u32[]{:S(2)}) copy-start(s32[1,1,8]{2,1,0:T(1,128)} %param.26) | copy-start | bytes 100
  18.7 11.3 %copy-start.1 = (bf16[768,256]{1,0:T(8,128)(2,1)S(1)}, bf16[768,256]{1,0:T(8,128)(2,1)}, u32[]{:S(2)}) copy-start(bf16[768,256]{1,0:T(8,128)(2,1)} %constant.50.clone.wxf_ref) | copy-start | bytes 1179652
  18.7 11.3 %copy-start.2 = (bf16[384,512]{1,0:T(8,128)(2,1)S(1)}, bf16[384,512]{1,0:T(8,128)(2,1)}, u32[]{:S(2)}) copy-start(bf16[384,512]{1,0:T(8,128)(2,1)} %constant.54.clone.wxe_ref) | copy-start | bytes 1179652
  18.7 11.3 %copy-start.3 = (bf16[192,768]{1,0:T(8,128)(2,1)S(1)}, bf16[192,768]{1,0:T(8,128)(2,1)}, u32[]{:S(2)}) copy-start(bf16[192,768]{1,0:T(8,128)(2,1)} %constant.57.clone.wxo_ref) | copy-start | bytes 884740
  18.7 11.3 %copy-start.4 = (bf16[192,576]{1,0:T(8,128)(2,1)S(1)}, bf16[192,576]{1,0:T(8,128)(2,1)}, u32[]{:S(2)}) copy-start(bf16[192,576]{1,0:T(8,128)(2,1)} %constant.51.clone.wyf_ref) | copy-start | bytes 663556
  18.7 11.3 %copy-start.5 = (bf16[192,576]{1,0:T(8,128)(2,1)S(1)}, bf16[192,576]{1,0:T(8,128)(2,1)}, u32[]{:S(2)}) copy-start(bf16[192,576]{1,0:T(8,128)(2,1)} %constant.56.clone.wyo_ref) | copy-start | bytes 663556
  18.7 11.3 %copy-start.6 = (bf16[768,128]{1,0:T(8,128)(2,1)S(1)}, bf16[768,128]{1,0:T(8,128)(2,1)}, u32[]{:S(2)}) copy-start(bf16[768,128]{1,0:T(8,128)(2,1)} %constant.49.clone.wzi_ref) | copy-start | bytes 589828
  18.8 11.3 %copy-start.7 = (bf16[384,256]{1,0:T(8,128)(2,1)S(1)}, bf16[384,256]{1,0:T(8,128)(2,1)}, u32[]{:S(2)}) copy-start(bf16[384,256]{1,0:T(8,128)(2,1)} %constant.48.clone.wz_ref) | copy-start | bytes 589828
  18.8 11.3 %copy-start.8 = (bf16[128,512]{1,0:T(8,128)(2,1)S(1)}, bf16[128,512]{1,0:T(8,128)(2,1)}, u32[]{:S(2)}) copy-start(bf16[128,512]{1,0:T(8,128)(2,1)} %constant.53.clone.wxi_ref) | copy-start | bytes 393220
  18.8 11.3 %copy-start.9 = (bf16[128,384]{1,0:T(8,128)(2,1)S(1)}, bf16[128,384]{1,0:T(8,128)(2,1)}, u32[]{:S(2)}) copy-start(bf16[128,384]{1,0:T(8,128)(2,1)} %constant.52.clone.wyi_ref) | copy-start | bytes 294916
  18.8 11.3 %copy-start.10 = (bf16[192,192]{1,0:T(8,128)(2,1)S(1)}, bf16[192,192]{1,0:T(8,128)(2,1)}, u32[]{:S(2)}) copy-start(bf16[192,192]{1,0:T(8,128)(2,1)} %constant.55.clone.wye_ref) | copy-start | bytes 221188
  30.1 65.6 %copy-start.14 = (f32[32,2048]{1,0:T(8,128)S(1)}, f32[32,2048]{1,0:T(8,128)}, u32[]{:S(2)}) copy-start(f32[32,2048]{1,0:T(8,128)} %param.23) | copy-start | bytes 786436
  53.4 28.8 %collective-permute-start.4 = (f32[96,2048]{1,0:T(8,128)S(1)}, f32[96,2048]{1,0:T(8,128)S(1)}, u32[]{:S(2)}, u32[]{:S(2)}) collective-permute-start(f32[96,2048]{1,0:T(8,128)S(1)} %get-tuple-element.16), channel_id=1, source_target_pairs={{0,1},{1,0},{2,3},{3,2},{4,5},{5,4},{6,7},{7,6},{8,9},{9,8},{10,11... | collective-permute-start | bytes 2359304 | tf_op jit(solution)/shard_map/ppermute | solution.py:630
  72.7 10.5 %collective-permute-start.6 = (f32[64,2048]{1,0:T(8,128)S(1)}, f32[64,2048]{1,0:T(8,128)S(1)}, u32[]{:S(2)}, u32[]{:S(2)}) collective-permute-start(f32[64,2048]{1,0:T(8,128)S(1)} %get-tuple-element.18), channel_id=1, source_target_pairs={{1,2},{2,1},{3,4},{4,3},{5,6},{6,5},{9,10},{10,9},{11,12},{12,11},... | collective-permute-start | bytes 1572872 | tf_op jit(solution)/shard_map/ppermute | solution.py:629
  74.6 1.2 %copy-start.11 = (f32[1728,128]{1,0:T(8,128)S(1)}, f32[1728,128]{1,0:T(8,128)}, u32[]{:S(2)}) copy-start(f32[1728,128]{1,0:T(8,128)} %get-tuple-element.12.real) | copy-start | bytes 2654212
  75.7 1.2 %copy-start.12 = (f32[1728,128]{1,0:T(8,128)S(1)}, f32[1728,128]{1,0:T(8,128)}, u32[]{:S(2)}) copy-start(f32[1728,128]{1,0:T(8,128)} %get-tuple-element.13.imag) | copy-start | bytes 2654212
  78.6 7.7 %collective-permute-start.5 = (f32[32,2048]{1,0:T(8,128)S(1)}, f32[32,2048]{1,0:T(8,128)S(1)}, u32[]{:S(2)}, u32[]{:S(2)}) collective-permute-start(f32[32,2048]{1,0:T(8,128)S(1)} %get-tuple-element.17), channel_id=1, source_target_pairs={{1,2},{2,1},{3,4},{4,3},{5,6},{6,5},{9,10},{10,9},{11,12},{12,11},... | collective-permute-start | bytes 786440 | tf_op jit(solution)/shard_map/ppermute | solution.py:632
  83.2 8.4 %collective-permute-start.7 = (f32[32,2048]{1,0:T(8,128)S(1)}, f32[32,2048]{1,0:T(8,128)S(1)}, u32[]{:S(2)}, u32[]{:S(2)}) collective-permute-start(f32[32,2048]{1,0:T(8,128)S(1)} %get-tuple-element.19), channel_id=1, source_target_pairs={{0,8},{8,0},{16,24},{24,16},{32,40},{40,32},{48,56},{56,48},{64,72... | collective-permute-start | bytes 786440 | tf_op jit(solution)/shard_map/ppermute | solution.py:637
  83.3 12.3 %collective-permute-start.8 = (f32[32,2048]{1,0:T(8,128)S(1)}, f32[32,2048]{1,0:T(8,128)S(1)}, u32[]{:S(2)}, u32[]{:S(2)}) collective-permute-start(f32[32,2048]{1,0:T(8,128)S(1)} %get-tuple-element.20), channel_id=1, source_target_pairs={{8,16},{16,8},{24,32},{32,24},{40,48},{48,40},{56,64},{64,56},{72,... | collective-permute-start | bytes 786440 | tf_op jit(solution)/shard_map/ppermute | solution.py:636

commit v9 on v8

--- a/solution.py
+++ b/solution.py
@@ -358,9 +358,9 @@
 def main_kernel(
     count_ref, ids_ref, odd_ref, own_ref, first_ref, second_ref, views_hbm, otf_hbm,
     wz_ref, wzi_ref, wxf_ref, wyf_ref, wyi_ref, wxi_ref, wxe_ref, wye_ref, wyo_ref, wxo_ref,
-    first_out, outer_out, inner_out, real_hbm, imag_hbm,
+    first_out, outer_out, inner_out, real_out, imag_out,
     field, total, big_real, big_imag, real, imag, lines, error, otf, image,
-    wide0, wide1, thin0, thin1, last0, last1, otf_sem, image_sem, own_sem,
+    wide0, wide1, thin0, thin1, last0, last1, otf_sem, image_sem,
 ):
     count = count_ref[0]
 
@@ -468,26 +468,18 @@
             imags = [total[kz + at, 1] for at in range(2)]
             for at, out in enumerate(along_y(wyo_ref[...], reals, imags)):
                 row = (kz + at) * YPITCH
-                for value, big, own in zip(out, (big_real, big_imag), (real, imag)):
+                for value, big, own in zip(out, (big_real, big_imag), (real_out, imag_out)):
                     big[pl.ds(row, BY), :] = value[:BY]
                     own[pl.ds(row, BY), :] = value[BY:2 * BY]
                     big[pl.ds(KZ * YPITCH + row, BY), :] = value[2 * BY:]
 
     loop(KZ // (2 * UT), inverse_y)
-    copies = (
-        pltpu.make_async_copy(real, real_hbm, own_sem.at[0]),
-        pltpu.make_async_copy(imag, imag_hbm, own_sem.at[1]),
-    )
-    for copy in copies:
-        copy.start()
     chunks = [
         (big_real, big_imag, side * KZ * YPITCH + y, out, y // 2)
         for side, out in ((odd, (outer_out, inner_out)), (1 - odd, (first_out,)))
         for y in range(0, BY, 8)
     ]
     final_sums(wxo_ref, wzi_ref, chunks, (last0, last1))
-    for copy in copies:
-        copy.wait()
 
 
 def tail_kernel(real, imag, wzi_ref, wxo_ref, out, last0, last1):
@@ -560,7 +552,7 @@
             for shape in (WIDE, (2 * BX, BY * SZ), (BX, BY * SZ), ROWS, ROWS)
         ],
         in_specs=[IN_SMEM] * 3 + [IN_VMEM] * 3 + [ANYWHERE] * 2 + [IN_VMEM] * len(tables),
-        out_specs=[IN_VMEM] * 3 + [ANYWHERE] * 2,
+        out_specs=[IN_VMEM] * 5,
         scratch_shapes=[
             pltpu.VMEM(SPECTRUM, F32),
             pltpu.VMEM(SPECTRUM, F32),
@@ -578,7 +570,6 @@
             pltpu.VMEM((ZPE * KZ, 3 * LANES), BF16),
             LAST,
             LAST,
-            pltpu.SemaphoreType.DMA((2,)),
             pltpu.SemaphoreType.DMA((2,)),
             pltpu.SemaphoreType.DMA((2,)),
         ],

time: 96.4 us -> 96.3 us (level)
  the two profiles are of different devices: /device:TPU:38 before, /device:TPU:66 now
where the time goes in v9:
time: 96.3 us; the launch traced here: 95 us
  Pallas kernels  63.2 us (66%)
  starting transfers between devices  17.3 us (18%)
  waiting for transfers between devices  10 us (10%)
  local copies, waits for them, and re-layouts  2.41 us (3%)
  other arithmetic  1.08 us (1%)
  between operations  1.02 us (1%)
    pallas_call x1, Pallas kernels, main_call(): pl.pallas_call(main_kernel, out_shape=[jax.ShapeDtypeStruct(shape, F32) f...  38.8 us
    pallas_call x2, Pallas kernels, otf_call(): pl.pallas_call(functools.partial(otf_kernel, begin, end), out_shape=jax.S...  22.7 us
    ppermute x1, waiting for transfers between devices, per_device(): one = lax.ppermute(jnp.where(odd_x == 1, low, high), 'bx', first_x)  5.25 us
    ppermute x1, starting transfers between devices, per_device(): other = lax.ppermute(estimate, 'bx', second_x)  4.05 us
    ppermute x1, waiting for transfers between devices, per_device(): other = lax.ppermute(jnp.where(odd_x == 1, high, low), 'bx', second_x)  4.02 us
    ppermute x1, starting transfers between devices, per_device(): other = lax.ppermute(jnp.where(odd_x == 1, high, low), 'bx', second_x)  3.7 us
    ppermute x1, starting transfers between devices, per_device(): other_inner = lax.ppermute(inner, 'by', second_y)  3.64 us
    unnamed x30, local copies, waits for them, and re-layouts  2.41 us
  transfers between devices with their start and end apart: 9, of which 3 were waited for; matrix products, arithmetic and copies ran while one was open for 0% of the time, Pallas kernels for 26%

profile of v9, /device:TPU:66, one launch (start us, length us, event | category | flops | bytes accessed | tf_op | source)
XLA Modules:
  0.0 95.0 jit_solution(16982114732075683976)
XLA Ops:
  0.0 1.6 %collective-permute-start = (f32[32,2048]{1,0:T(8,128)}, f32[32,2048]{1,0:T(8,128)S(1)}, u32[]{:S(2)}, u32[]{:S(2)}) collective-permute-start(f32[32,2048]{1,0:T(8,128)} %param.23), channel_id=1, source_target_pairs={{0,8},{8,0},{16,24},{24,16},{32,40},{40,32},{48,56},{56,48},{64,72... | collective-permute-start | bytes 786440 | tf_op jit(solution)/shard_map/ppermute | solution.py:609
  1.6 4.1 %collective-permute-start.1 = (f32[32,2048]{1,0:T(8,128)}, f32[32,2048]{1,0:T(8,128)S(1)}, u32[]{:S(2)}, u32[]{:S(2)}) collective-permute-start(f32[32,2048]{1,0:T(8,128)} %param.23), channel_id=1, source_target_pairs={{8,16},{16,8},{24,32},{32,24},{40,48},{48,40},{56,64},{64,56},{72,... | collective-permute-start | bytes 786440 | tf_op jit(solution)/shard_map/ppermute | solution.py:610
  6.3 9.7 %otf.2.rest_0_ = f32[5,48,2,96,128]{4,3,2,1,0:T(8,128)} custom-call(s32[1]{0:T(128)} %bitcast.4.count_ref, s32[8]{0:T(128)} %bitcast.8, f32[8,64,4096]{2,1,0:T(8,128)} %psf_hbm.3, bf16[384,256]{1,0:T(8,128)(2,1)} %constant.45.clone.wz_hbm, bf16[384,256]{1,0:T(8,128)(2,1)} %constant.46.clone.wx_hbm, bf16[192,384]{1,0:T(8,128)(2,1)} %constant.47.clone.wy_hbm), custom_call_target="tpu_custom_call" | custom-call | flops 8000000000 | bytes 12000000 | tf_op jit(solution)/shard_map/otf/pallas_call | solution.py:508
  16.0 0.0 collective-permute-done
  16.0 0.0 collective-permute-done.1
  16.1 0.0 copy-done.13
  16.1 0.1 pad_maximum_fusion.own_ref
  16.2 0.1 collective-permute-start.2
  16.3 2.1 %collective-permute-start.3 = (f32[96,2048]{1,0:T(8,128)S(1)}, f32[96,2048]{1,0:T(8,128)}, u32[]{:S(2)}, u32[]{:S(2)}) collective-permute-start(f32[96,2048]{1,0:T(8,128)S(1)} %pad_maximum_fusion.own_ref), channel_id=1, source_target_pairs={{1,2},{2,1},{3,4},{4,3},{5,6},{6,5},{9,10},{10,9},{11,12},{12,11},... | collective-permute-start | bytes 2359304 | tf_op jit(solution)/shard_map/ppermute | solution.py:614
  18.4 0.0 copy-start
  18.4 0.0 copy-start.1
  18.4 0.0 copy-start.2
  18.4 0.0 copy-start.3
  18.4 0.0 copy-start.4
  18.4 0.0 copy-start.5
  18.4 0.0 copy-start.6
  18.5 0.0 copy-start.7
  18.5 0.0 copy-start.8
  18.5 0.0 copy-start.9
  18.5 0.0 copy-start.10
  18.5 12.9 %otf.3.otf_hbm = f32[5,48,2,96,128]{4,3,2,1,0:T(8,128)} custom-call(s32[1]{0:T(128)} %bitcast.5.count_ref, s32[8]{0:T(128)} %bitcast.9, f32[8,64,4096]{2,1,0:T(8,128)} %psf_hbm.3, bf16[384,256]{1,0:T(8,128)(2,1)} %constant.45.clone.wz_hbm, bf16[384,256]{1,0:T(8,128)(2,1)} %constant.46.clone.wx_hbm, ...), custom_call_target="tpu_custom_call", output_to_operand_aliasing={{}: (6, {})} | custom-call | flops 12000000000 | bytes 18000000 | tf_op jit(solution)/shard_map/otf/pallas_call | solution.py:508
  31.5 0.0 collective-permute-done.2.first_ref
  31.5 0.0 collective-permute-done.3.second_ref
  31.5 0.0 copy-done
  31.5 0.0 copy-done.1
  31.5 0.0 copy-done.2
  31.5 0.0 copy-done.3
  31.5 0.0 copy-done.4
  31.5 0.0 copy-done.5
  31.6 0.0 copy-start.14
  31.6 38.8 %views.1 = (f32[96,2048]{1,0:T(8,128)S(1)}, f32[64,2048]{1,0:T(8,128)S(1)}, f32[32,2048]{1,0:T(8,128)S(1)}, f32[1728,128]{1,0:T(8,128)}, f32[1728,128]{1,0:T(8,128)}) custom-call(s32[1]{0:T(128)} %bitcast.6.count_ref, s32[8]{0:T(128)S(1)} %bitcast.10, s32[1]{0:T(128)} %bitcast.2.odd_ref, f32[96,2048]{1,0:T(8,128)S(1)} %pad_maximum_fusion.own_ref, ...), custom_call_target="tpu_custom_call" | custom-call | flops 30000001024 | bytes 40000000 | tf_op jit(solution)/shard_map/views/pallas_call | solution.py:548
  70.4 0.1 collective-permute-start.4
  70.5 1.9 %collective-permute-start.6 = (f32[64,2048]{1,0:T(8,128)S(1)}, f32[64,2048]{1,0:T(8,128)S(1)}, u32[]{:S(2)}, u32[]{:S(2)}) collective-permute-start(f32[64,2048]{1,0:T(8,128)S(1)} %get-tuple-element.18), channel_id=1, source_target_pairs={{1,2},{2,1},{3,4},{4,3},{5,6},{6,5},{9,10},{10,9},{11,12},{12,11},... | collective-permute-start | bytes 1572872 | tf_op jit(solution)/shard_map/ppermute | solution.py:620
  72.4 0.0 copy-start.11
  72.5 1.2 %copy-done.11 = f32[1728,128]{1,0:T(8,128)S(1)} copy-done((f32[1728,128]{1,0:T(8,128)S(1)}, f32[1728,128]{1,0:T(8,128)}, u32[]{:S(2)}) %copy-start.11) | copy-done | bytes 884760
  73.6 1.2 %copy-done.12 = f32[1728,128]{1,0:T(8,128)S(1)} copy-done((f32[1728,128]{1,0:T(8,128)S(1)}, f32[1728,128]{1,0:T(8,128)}, u32[]{:S(2)}) %copy-start.12) | copy-done | bytes 884760
  74.8 1.7 %tail.1 = f32[96,2048]{1,0:T(8,128)S(1)} custom-call(f32[1728,128]{1,0:T(8,128)S(1)} %copy-done.11, f32[1728,128]{1,0:T(8,128)S(1)} %copy-done.12, bf16[768,128]{1,0:T(8,128)(2,1)S(1)} %copy-done.6, bf16[192,768]{1,0:T(8,128)(2,1)S(1)} %copy-done.3), custom_call_target="tpu_custom_call" | custom-call | flops 4000000000 | bytes 3000000 | tf_op jit(solution)/shard_map/tail/pallas_call | solution.py:584
  76.5 3.6 %collective-permute-start.5 = (f32[32,2048]{1,0:T(8,128)S(1)}, f32[32,2048]{1,0:T(8,128)S(1)}, u32[]{:S(2)}, u32[]{:S(2)}) collective-permute-start(f32[32,2048]{1,0:T(8,128)S(1)} %get-tuple-element.17), channel_id=1, source_target_pairs={{1,2},{2,1},{3,4},{4,3},{5,6},{6,5},{9,10},{10,9},{11,12},{12,11},... | collective-permute-start | bytes 786440 | tf_op jit(solution)/shard_map/ppermute | solution.py:623
  80.1 0.0 collective-permute-done.4
  80.1 0.1 add.24
  80.3 0.8 collective-permute-done.6
  81.0 0.1 broadcast_select_fusion.1
  81.1 0.1 collective-permute-start.7
  81.2 3.7 %collective-permute-start.8 = (f32[32,2048]{1,0:T(8,128)S(1)}, f32[32,2048]{1,0:T(8,128)S(1)}, u32[]{:S(2)}, u32[]{:S(2)}) collective-permute-start(f32[32,2048]{1,0:T(8,128)S(1)} %get-tuple-element.20), channel_id=1, source_target_pairs={{8,16},{16,8},{24,32},{32,24},{40,48},{48,40},{56,64},{64,56},{72,... | collective-permute-start | bytes 786440 | tf_op jit(solution)/shard_map/ppermute | solution.py:627
  84.9 0.0 collective-permute-done.5
  84.9 5.3 %collective-permute-done.7 = f32[32,2048]{1,0:T(8,128)S(1)} collective-permute-done((f32[32,2048]{1,0:T(8,128)S(1)}, f32[32,2048]{1,0:T(8,128)S(1)}, u32[]{:S(2)}, u32[]{:S(2)}) %collective-permute-start.7) | collective-permute-done | bytes 262176 | tf_op jit(solution)/shard_map/ppermute | solution.py:628
  90.2 4.0 %collective-permute-done.8 = f32[32,2048]{1,0:T(8,128)S(1)} collective-permute-done((f32[32,2048]{1,0:T(8,128)S(1)}, f32[32,2048]{1,0:T(8,128)S(1)}, u32[]{:S(2)}, u32[]{:S(2)}) %collective-permute-start.8) | collective-permute-done | bytes 262176 | tf_op jit(solution)/shard_map/ppermute | solution.py:627
  94.2 0.8 fusion.4
  (9 shorter events, 0.1 us)
Async XLA Ops:
  0.0 16.1 %copy-start.13 = (f32[32,2048]{1,0:T(8,128)S(1)}, f32[32,2048]{1,0:T(8,128)}, u32[]{:S(2)}) copy-start(f32[32,2048]{1,0:T(8,128)} %param.23) | copy-start | bytes 786436
  0.0 16.0 %collective-permute-start = (f32[32,2048]{1,0:T(8,128)}, f32[32,2048]{1,0:T(8,128)S(1)}, u32[]{:S(2)}, u32[]{:S(2)}) collective-permute-start(f32[32,2048]{1,0:T(8,128)} %param.23), channel_id=1, source_target_pairs={{0,8},{8,0},{16,24},{24,16},{32,40},{40,32},{48,56},{56,48},{64,72... | collective-permute-start | bytes 786440 | tf_op jit(solution)/shard_map/ppermute | solution.py:609
  1.6 14.5 %collective-permute-start.1 = (f32[32,2048]{1,0:T(8,128)}, f32[32,2048]{1,0:T(8,128)S(1)}, u32[]{:S(2)}, u32[]{:S(2)}) collective-permute-start(f32[32,2048]{1,0:T(8,128)} %param.23), channel_id=1, source_target_pairs={{8,16},{16,8},{24,32},{32,24},{40,48},{48,40},{56,64},{64,56},{72,... | collective-permute-start | bytes 786440 | tf_op jit(solution)/shard_map/ppermute | solution.py:610
  16.2 15.3 %collective-permute-start.2 = (f32[96,2048]{1,0:T(8,128)S(1)}, f32[96,2048]{1,0:T(8,128)S(1)}, u32[]{:S(2)}, u32[]{:S(2)}) collective-permute-start(f32[96,2048]{1,0:T(8,128)S(1)} %pad_maximum_fusion.own_ref), channel_id=1, source_target_pairs={{0,1},{1,0},{2,3},{3,2},{4,5},{5,4},{6,7},{7,6},{8,9},{9,8},{10,11... | collective-permute-start | bytes 2359304 | tf_op jit(solution)/shard_map/ppermute | solution.py:614
  16.3 15.2 %collective-permute-start.3 = (f32[96,2048]{1,0:T(8,128)S(1)}, f32[96,2048]{1,0:T(8,128)}, u32[]{:S(2)}, u32[]{:S(2)}) collective-permute-start(f32[96,2048]{1,0:T(8,128)S(1)} %pad_maximum_fusion.own_ref), channel_id=1, source_target_pairs={{1,2},{2,1},{3,4},{4,3},{5,6},{6,5},{9,10},{10,9},{11,12},{12,11},... | collective-permute-start | bytes 2359304 | tf_op jit(solution)/shard_map/ppermute | solution.py:614
  18.4 13.1 %copy-start = (s32[1,1,8]{2,1,0:T(1,128)S(1)}, s32[1,1,8]{2,1,0:T(1,128)}, u32[]{:S(2)}) copy-start(s32[1,1,8]{2,1,0:T(1,128)} %param.26) | copy-start | bytes 100
  18.4 13.1 %copy-start.1 = (bf16[768,256]{1,0:T(8,128)(2,1)S(1)}, bf16[768,256]{1,0:T(8,128)(2,1)}, u32[]{:S(2)}) copy-start(bf16[768,256]{1,0:T(8,128)(2,1)} %constant.50.clone.wxf_ref) | copy-start | bytes 1179652
  18.4 13.1 %copy-start.2 = (bf16[384,512]{1,0:T(8,128)(2,1)S(1)}, bf16[384,512]{1,0:T(8,128)(2,1)}, u32[]{:S(2)}) copy-start(bf16[384,512]{1,0:T(8,128)(2,1)} %constant.54.clone.wxe_ref) | copy-start | bytes 1179652
  18.4 13.1 %copy-start.3 = (bf16[192,768]{1,0:T(8,128)(2,1)S(1)}, bf16[192,768]{1,0:T(8,128)(2,1)}, u32[]{:S(2)}) copy-start(bf16[192,768]{1,0:T(8,128)(2,1)} %constant.57.clone.wxo_ref) | copy-start | bytes 884740
  18.4 13.1 %copy-start.4 = (bf16[192,576]{1,0:T(8,128)(2,1)S(1)}, bf16[192,576]{1,0:T(8,128)(2,1)}, u32[]{:S(2)}) copy-start(bf16[192,576]{1,0:T(8,128)(2,1)} %constant.51.clone.wyf_ref) | copy-start | bytes 663556
  18.4 13.1 %copy-start.5 = (bf16[192,576]{1,0:T(8,128)(2,1)S(1)}, bf16[192,576]{1,0:T(8,128)(2,1)}, u32[]{:S(2)}) copy-start(bf16[192,576]{1,0:T(8,128)(2,1)} %constant.56.clone.wyo_ref) | copy-start | bytes 663556
  18.4 13.1 %copy-start.6 = (bf16[768,128]{1,0:T(8,128)(2,1)S(1)}, bf16[768,128]{1,0:T(8,128)(2,1)}, u32[]{:S(2)}) copy-start(bf16[768,128]{1,0:T(8,128)(2,1)} %constant.49.clone.wzi_ref) | copy-start | bytes 589828
  18.5 13.1 %copy-start.7 = (bf16[384,256]{1,0:T(8,128)(2,1)S(1)}, bf16[384,256]{1,0:T(8,128)(2,1)}, u32[]{:S(2)}) copy-start(bf16[384,256]{1,0:T(8,128)(2,1)} %constant.48.clone.wz_ref) | copy-start | bytes 589828
  18.5 13.1 %copy-start.8 = (bf16[128,512]{1,0:T(8,128)(2,1)S(1)}, bf16[128,512]{1,0:T(8,128)(2,1)}, u32[]{:S(2)}) copy-start(bf16[128,512]{1,0:T(8,128)(2,1)} %constant.53.clone.wxi_ref) | copy-start | bytes 393220
  18.5 13.1 %copy-start.9 = (bf16[128,384]{1,0:T(8,128)(2,1)S(1)}, bf16[128,384]{1,0:T(8,128)(2,1)}, u32[]{:S(2)}) copy-start(bf16[128,384]{1,0:T(8,128)(2,1)} %constant.52.clone.wyi_ref) | copy-start | bytes 294916
  18.5 13.1 %copy-start.10 = (bf16[192,192]{1,0:T(8,128)(2,1)S(1)}, bf16[192,192]{1,0:T(8,128)(2,1)}, u32[]{:S(2)}) copy-start(bf16[192,192]{1,0:T(8,128)(2,1)} %constant.55.clone.wye_ref) | copy-start | bytes 221188
  31.6 62.6 %copy-start.14 = (f32[32,2048]{1,0:T(8,128)S(1)}, f32[32,2048]{1,0:T(8,128)}, u32[]{:S(2)}) copy-start(f32[32,2048]{1,0:T(8,128)} %param.23) | copy-start | bytes 786436
  70.4 9.7 %collective-permute-start.4 = (f32[96,2048]{1,0:T(8,128)S(1)}, f32[96,2048]{1,0:T(8,128)S(1)}, u32[]{:S(2)}, u32[]{:S(2)}) collective-permute-start(f32[96,2048]{1,0:T(8,128)S(1)} %get-tuple-element.16), channel_id=1, source_target_pairs={{0,1},{1,0},{2,3},{3,2},{4,5},{5,4},{6,7},{7,6},{8,9},{9,8},{10,11... | collective-permute-start | bytes 2359304 | tf_op jit(solution)/shard_map/ppermute | solution.py:621
  70.5 10.5 %collective-permute-start.6 = (f32[64,2048]{1,0:T(8,128)S(1)}, f32[64,2048]{1,0:T(8,128)S(1)}, u32[]{:S(2)}, u32[]{:S(2)}) collective-permute-start(f32[64,2048]{1,0:T(8,128)S(1)} %get-tuple-element.18), channel_id=1, source_target_pairs={{1,2},{2,1},{3,4},{4,3},{5,6},{6,5},{9,10},{10,9},{11,12},{12,11},... | collective-permute-start | bytes 1572872 | tf_op jit(solution)/shard_map/ppermute | solution.py:620
  72.4 1.2 %copy-start.11 = (f32[1728,128]{1,0:T(8,128)S(1)}, f32[1728,128]{1,0:T(8,128)}, u32[]{:S(2)}) copy-start(f32[1728,128]{1,0:T(8,128)} %get-tuple-element.12.real) | copy-start | bytes 2654212
  73.6 1.2 %copy-start.12 = (f32[1728,128]{1,0:T(8,128)S(1)}, f32[1728,128]{1,0:T(8,128)}, u32[]{:S(2)}) copy-start(f32[1728,128]{1,0:T(8,128)} %get-tuple-element.13.imag) | copy-start | bytes 2654212
  76.5 8.4 %collective-permute-start.5 = (f32[32,2048]{1,0:T(8,128)S(1)}, f32[32,2048]{1,0:T(8,128)S(1)}, u32[]{:S(2)}, u32[]{:S(2)}) collective-permute-start(f32[32,2048]{1,0:T(8,128)S(1)} %get-tuple-element.17), channel_id=1, source_target_pairs={{1,2},{2,1},{3,4},{4,3},{5,6},{6,5},{9,10},{10,9},{11,12},{12,11},... | collective-permute-start | bytes 786440 | tf_op jit(solution)/shard_map/ppermute | solution.py:623
  81.1 9.1 %collective-permute-start.7 = (f32[32,2048]{1,0:T(8,128)S(1)}, f32[32,2048]{1,0:T(8,128)S(1)}, u32[]{:S(2)}, u32[]{:S(2)}) collective-permute-start(f32[32,2048]{1,0:T(8,128)S(1)} %get-tuple-element.19), channel_id=1, source_target_pairs={{0,8},{8,0},{16,24},{24,16},{32,40},{40,32},{48,56},{56,48},{64,72... | collective-permute-start | bytes 786440 | tf_op jit(solution)/shard_map/ppermute | solution.py:628
  81.2 13.0 %collective-permute-start.8 = (f32[32,2048]{1,0:T(8,128)S(1)}, f32[32,2048]{1,0:T(8,128)S(1)}, u32[]{:S(2)}, u32[]{:S(2)}) collective-permute-start(f32[32,2048]{1,0:T(8,128)S(1)} %get-tuple-element.20), channel_id=1, source_target_pairs={{8,16},{16,8},{24,32},{32,24},{40,48},{48,40},{56,64},{64,56},{72,... | collective-permute-start | bytes 786440 | tf_op jit(solution)/shard_map/ppermute | solution.py:627
